TPU v7x, 32 devices: a whole 2x2x4 slice. The times are simulated.
32 devices in a mesh: groups: 2 (over y), gx: 4 (over z), gy: 2 (over x), gz: 2 (over core).
Axes of the slice: x: 2, y: 2, z: 4, core: 2. Of those that a mesh axis runs over, the one named last changes fastest.
Arguments:
- concentration: float32 [32, 2, 8, 128, 128], P(('groups', 'gx', 'gy', 'gz')), parts along dimension 0, may hold values from -6 to 6
- diffusivity: float32 [32, 8, 128, 128], P(('groups', 'gx', 'gy', 'gz')), parts along dimension 0, may hold values from 0.05 to 1
- rates: float32 [32, 2], P(('groups', 'gx', 'gy', 'gz')), parts along dimension 0, may hold values from 0.2 to 1.5
- velocity: float32 [4, 3], P('groups'), parts along dimension 0, may hold values from -1 to 1
- neighbours: int32 [32, 2], P('groups'), parts along dimension 0, may hold values from -1 to 15, as said below
- migrate: int32 [3, 32], P(None, 'groups'), parts along dimension 1, may hold values 0 or 1
- bit_order: int32 [6], P('groups'), parts along dimension 0, may hold values from 0 to 3, as said below
Outputs:
- final_field: float32 [32, 2, 8, 128, 128], P(('groups', 'gx', 'gy', 'gz')), parts along dimension 0
There are 2 independent parts, one for each index of `groups`. A program takes and returns all parts, laid end to end along the dimension named above; each array names one. Nothing has to cross between parts.
Inputs may be any that keep to these rules, and one draw needn't show every extreme that they name: `neighbours`: column 0 names the patch beside a patch's first x cell, column 1 the one beside its last, -1 where the domain ends; if q is beside p on one side then p is beside q on the other. `bit_order`: distinct bit numbers of the device number within a run; the highest bit is among them.
All inputs are finite; a program needn't handle non-finite values.
Results may differ from a plain program's by a relative error of at most 0.00002.
Values sent between devices are 32-bit elements; how exact they have to be, the bound alone decides.
No kernel may reach another device: no remote copies, remote signals or barrier semaphores. Data moves between devices by JAX's collectives and lax.ppermute only.
A program may use at most 128 MiB of HBM per device.

v0:
```python
from functools import partial
from itertools import permutations

import jax
import jax.numpy as jnp
from jax import lax
from jax.experimental import pallas as pl
from jax.experimental.pallas import tpu as pltpu
from jax.sharding import PartitionSpec as P

time_step = 0.1
AXES = ("gx", "gy", "gz")
ROUNDS = 3
STEPS = ROUNDS + 1
LANES = 128
ROWS = 8
SMEM = pl.BlockSpec(memory_space=pltpu.SMEM)
VMEM = pl.BlockSpec(memory_space=pltpu.VMEM)
PARAMS = pltpu.CompilerParams(vmem_limit_bytes=32 * 2**20)


def lane_index():
    return lax.broadcasted_iota(jnp.int32, (ROWS, LANES), 1)


def row_index():
    return lax.broadcasted_iota(jnp.int32, (ROWS, LANES), 0)


def speeds(velocity_ref, species, direction):
    v = velocity_ref[species, direction] * time_step
    return jnp.maximum(v, 0.0), jnp.minimum(v, 0.0)


def prepare_kernel(bits, here_ref, neighbours_ref, migrate_ref, order_ref, rates_ref, u_ref, k_ref, plan_ref, own_ref, sent_ref):
    here = here_ref[0]
    for side in range(2):
        beside = neighbours_ref[here, side]
        plan_ref[side] = jnp.maximum(beside, 0)
        plan_ref[2 + side] = (beside >= 0).astype(jnp.int32)
    top = bits - 1
    order = [order_ref[r] for r in range(ROUNDS)]
    place = jnp.where(order[0] == top, 0, jnp.where(order[1] == top, 1, 2))
    first = jnp.where(place == 0, order[1], order[0])
    second = jnp.where(place == 2, order[1], order[2])
    second = jnp.where(second > first, second - 1, second)
    plan_ref[4] = (place * top + first) * (top - 1) + second
    for r in range(ROUNDS):
        partner = jnp.bitwise_xor(here, jnp.left_shift(jnp.int32(1), order[r]))
        plan_ref[5 + r] = ((migrate_ref[r, here] + migrate_ref[r, partner]) > 0).astype(jnp.int32)
    depth = k_ref.shape[0]
    wide = lax.broadcasted_iota(jnp.int32, (LANES, LANES), 1)
    for a in range(3):
        packed = jnp.zeros((LANES, LANES), jnp.float32)
        for z in range(depth):
            plane = k_ref[z] if a == 2 else u_ref[a, z]
            moved = pltpu.roll(plane, (16 * z + 8) % LANES, 1)
            packed = jnp.where((wide >= 16 * z) & (wide < 16 * z + 16), moved, packed)
        turned = packed.T
        own_ref[a] = turned.reshape(depth, 16, LANES)
        for z in range(depth):
            high = turned[16 * z : 16 * z + 8]
            low = turned[16 * z + 8 : 16 * z + 16]
            sent_ref[a * depth + z] = pltpu.roll(jnp.where(row_index() < 4, low, high), 4, 0)
    for r in range(2):
        sent_ref[3 * depth + r] = jnp.full((ROWS, LANES), rates_ref[0, r], jnp.float32)


def interior_kernel(velocity_ref, rates_ref, u_ref, k_ref, out_ref, ub, kp, kxr, kxl, ky, kz, c0):
    depth, height, _ = k_ref.shape
    blocks = height // ROWS
    half = 0.5 * time_step
    zero = jnp.zeros((ROWS, LANES), jnp.float32)
    for z in range(depth):
        for edge in (0, height + ROWS):
            kp[z, edge : edge + ROWS] = zero
            ky[z, edge : edge + ROWS] = zero
            for s in range(2):
                for i in range(2):
                    ub[s, i, z, edge : edge + ROWS] = zero
        kp[z, ROWS : ROWS + height] = k_ref[z]
        for i in range(2):
            ub[0, i, z, ROWS : ROWS + height] = u_ref[i, z]
    pos = [[speeds(velocity_ref, i, d) for d in range(3)] for i in range(2)]
    decay = time_step * rates_ref[0, 1]
    growth = time_step * rates_ref[0, 0]

    def coefficients(b, _):
        y = pl.multiple_of(b * ROWS, ROWS)
        at = y + ROWS
        row = row_index() + y
        has_next = (row < height - 1).astype(jnp.float32)
        has_prior = (row > 0).astype(jnp.float32)
        below = zero
        for z in range(depth):
            k = kp[z, pl.ds(at, ROWS)]
            xr = half * (k + pltpu.roll(k, LANES - 1, 1))
            xl = pltpu.roll(xr, 1, 1)
            yr = half * (k + kp[z, pl.ds(at + 1, ROWS)]) * has_next
            yl = half * (k + kp[z, pl.ds(at - 1, ROWS)]) * has_prior
            above = half * (k + kp[z + 1, pl.ds(at, ROWS)]) if z < depth - 1 else zero
            kxr[z, pl.ds(y, ROWS)] = xr
            kxl[z, pl.ds(y, ROWS)] = xl
            ky[z, pl.ds(at, ROWS)] = yr
            kz[z, pl.ds(y, ROWS)] = above
            total = 1.0 - ((xr + xl) + (yr + yl) + (above + below))
            for i in range(2):
                (px, mx), (py, my), (pz, mz) = pos[i]
                level = px - mx
                if z < depth - 1:
                    level = level + pz
                if z > 0:
                    level = level - mz
                if i == 1:
                    level = level + decay
                c0[i, z, pl.ds(y, ROWS)] = total - (level + py * has_next - my * has_prior)
            below = above
        return 0

    lax.fori_loop(0, blocks, coefficients, 0)

    for step in range(STEPS):
        src = step % 2

        def advance(b, _):
            y = pl.multiple_of(b * ROWS, ROWS)
            at = y + ROWS
            prior = [zero, zero]
            here = [ub[src, i, 0, pl.ds(at, ROWS)] for i in range(2)]
            zl = zero
            for z in range(depth):
                last = z == depth - 1
                after = [zero, zero] if last else [ub[src, i, z + 1, pl.ds(at, ROWS)] for i in range(2)]
                xr = kxr[z, pl.ds(y, ROWS)]
                xl = kxl[z, pl.ds(y, ROWS)]
                yr = ky[z, pl.ds(at, ROWS)]
                yl = ky[z, pl.ds(at - 1, ROWS)]
                zr = kz[z, pl.ds(y, ROWS)]
                q = (growth * here[0]) * here[1]
                for i in range(2):
                    (px, mx), (py, my), (pz, mz) = pos[i]
                    u = here[i]
                    new = c0[i, z, pl.ds(y, ROWS)] * u
                    new = new + (xr - mx) * pltpu.roll(u, LANES - 1, 1) + (xl + px) * pltpu.roll(u, 1, 1)
                    new = new + (
                        (yr - my) * ub[src, i, z, pl.ds(at + 1, ROWS)] + (yl + py) * ub[src, i, z, pl.ds(at - 1, ROWS)]
                    )
                    if not last:
                        new = new + (zr - mz) * after[i]
                    if z > 0:
                        new = new + (zl + pz) * prior[i]
                    new = new - q if i == 0 else new + q
                    if step == STEPS - 1:
                        out_ref[i, z, pl.ds(y, ROWS)] = new
                    else:
                        ub[1 - src, i, z, pl.ds(at, ROWS)] = new
                prior, here, zl = here, after, zr
            return 0

        lax.fori_loop(0, blocks, advance, 0)


def edge_kernel(plan_ref, velocity_ref, rates_ref, left_ref, right_ref, own_ref, out_ref, ub, kp, kxr, kxl, ky, kz, c0):
    depth = own_ref.shape[1]
    half = 0.5 * time_step
    zero = jnp.zeros((ROWS, LANES), jnp.float32)
    row = row_index()
    lane = lane_index()
    kept = jnp.where(row < 4, plan_ref[3], plan_ref[2]).astype(jnp.float32)

    def beside(tile):
        both = jnp.where(row < 4, left_ref[0, tile], right_ref[0, tile])
        return pltpu.roll(both, 4, 0) * kept

    decay = [jnp.full((ROWS, LANES), time_step * rates_ref[0, 1])] * 3
    growth = [jnp.full((ROWS, LANES), time_step * rates_ref[0, 0])] * 3
    growth[1] = time_step * beside(3 * depth)
    decay[1] = time_step * beside(3 * depth + 1)
    pos = [[speeds(velocity_ref, i, d) for d in range(3)] for i in range(2)]
    has_next = (lane < LANES - 1).astype(jnp.float32)
    has_prior = (lane > 0).astype(jnp.float32)
    ends = [(pos[i][1][0] * has_prior, pos[i][1][1] * has_next) for i in range(2)]
    for z in range(depth + 2):
        inside = 0 < z < depth + 1
        for block in range(5):
            at = slice(block * ROWS, block * ROWS + ROWS)
            for s in range(2):
                for i in range(2):
                    if not inside or block in (0, 4):
                        ub[s, i, z, at] = zero
            if not inside or block in (0, 4):
                kp[z, at] = zero
        if inside:
            for a in range(3):
                parts = [own_ref[a, z - 1, 0:8], beside(a * depth + z - 1), own_ref[a, z - 1, 8:16]]
                for block in range(3):
                    at = slice(block * ROWS + ROWS, block * ROWS + 2 * ROWS)
                    if a == 2:
                        kp[z, at] = parts[block]
                    else:
                        ub[0, a, z, at] = parts[block]
    for block in range(3):
        kz[0, block * ROWS : block * ROWS + ROWS] = zero

    def coefficients(z, _):
        upper = (z < depth).astype(jnp.float32)
        lower = (z > 1).astype(jnp.float32)
        for block in range(3):
            at = ROWS * (block + 1)
            here = slice(at, at + ROWS)
            put = slice(block * ROWS, block * ROWS + ROWS)
            k = kp[z, here]
            xr = half * (k + kp[z, at + 1 : at + 1 + ROWS])
            xl = half * (k + kp[z, at - 1 : at - 1 + ROWS])
            yr = half * (k + pltpu.roll(k, LANES - 1, 1)) * has_next
            yl = pltpu.roll(yr, 1, 1)
            zr = half * upper * (k + kp[z + 1, here])
            zl = half * lower * (k + kp[z - 1, here])
            kxr[z, put] = xr
            kxl[z, put] = xl
            ky[z, put] = yr
            kz[z, put] = zr
            total = 1.0 - ((xr + xl) + (yr + yl) + (zr + zl))
            for i in range(2):
                (px, mx), (py, my), (pz, mz) = pos[i]
                level = px - mx + pz * upper - mz * lower + (py * has_next - my * has_prior)
                if i == 1:
                    level = level + decay[block]
                c0[i, z, put] = total - level
        return 0

    lax.fori_loop(1, depth + 1, coefficients, 0)

    for step in range(STEPS):
        src = step % 2

        def advance(z, _):
            for block in range(3):
                at = ROWS * (block + 1)
                here = slice(at, at + ROWS)
                put = slice(block * ROWS, block * ROWS + ROWS)
                xr, xl, yr, zr, zl = kxr[z, put], kxl[z, put], ky[z, put], kz[z, put], kz[z - 1, put]
                yl = pltpu.roll(yr, 1, 1)
                pair = [ub[src, i, z, here] for i in range(2)]
                q = (growth[block] * pair[0]) * pair[1]
                for i in range(2):
                    (px, mx), _, (pz, mz) = pos[i]
                    py, my = ends[i]
                    u = pair[i]
                    new = c0[i, z, put] * u
                    new = new + (xr - mx) * ub[src, i, z, at + 1 : at + 1 + ROWS]
                    new = new + (xl + px) * ub[src, i, z, at - 1 : at - 1 + ROWS]
                    new = new + ((yr - my) * pltpu.roll(u, LANES - 1, 1) + (yl + py) * pltpu.roll(u, 1, 1))
                    new = new + ((zr - mz) * ub[src, i, z + 1, here] + (zl + pz) * ub[src, i, z - 1, here])
                    new = new - q if i == 0 else new + q
                    if block == 1:
                        new = new * kept
                    ub[1 - src, i, z, here] = new
            return 0

        lax.fori_loop(1, depth + 1, advance, 0)
    for i in range(2):
        for z in range(depth):
            high = ub[STEPS % 2, i, z + 1, ROWS : 2 * ROWS]
            low = ub[STEPS % 2, i, z + 1, 3 * ROWS : 4 * ROWS]
            out_ref[i, z] = pltpu.roll(jnp.where(row < 4, low, high), 4, 0)


def merge_kernel(u_ref, edge_ref, out_ref):
    depth = u_ref.shape[1]
    turned = edge_ref[...].reshape(2 * depth * ROWS, LANES).T
    wide = lax.broadcasted_iota(jnp.int32, (LANES, LANES), 1)
    rim = (wide < 4) | (wide >= LANES - 4)
    for i in range(2):
        for z in range(depth):
            shift = (LANES - 4 - ROWS * (i * depth + z)) % LANES
            out_ref[i, z] = jnp.where(rim, pltpu.roll(turned, shift, 1), u_ref[i, z])


def swap(block, bit):
    count = lax.axis_size(AXES)
    return lax.ppermute(block, AXES, [(low, low ^ 1 << bit) for low in range(count)])


def route(field, moved, bits, sizes):
    out = []
    start = 0
    for size in sizes:
        part = field[start : start + size]
        for r, bit in enumerate(bits):
            part = jnp.where(moved[r] > 0, swap(part, bit), part)
        out.append(part)
        start += size
    return jnp.concatenate(out, axis=0)


def per_device(concentration, diffusivity, rates, velocity, neighbours, migrate, bit_order):
    devices = lax.axis_size(AXES)
    bits = devices.bit_length() - 1
    _, species, depth, height, width = concentration.shape
    field = concentration[0]
    kappa = diffusivity[0]
    here = lax.axis_index(AXES).astype(jnp.int32).reshape(1)
    f32 = jnp.float32
    tiles = 3 * depth + 2
    plan, own, sent = pl.pallas_call(
        partial(prepare_kernel, bits),
        out_shape=(
            jax.ShapeDtypeStruct((8,), jnp.int32),
            jax.ShapeDtypeStruct((3, depth, 16, LANES), f32),
            jax.ShapeDtypeStruct((tiles, ROWS, LANES), f32),
        ),
        in_specs=[SMEM] * 5 + [VMEM] * 2,
        out_specs=(SMEM, VMEM, VMEM),
        compiler_params=PARAMS,
        name="prepare",
    )(here, neighbours, migrate, bit_order, rates, field, kappa)
    gathered = lax.all_gather(sent, AXES, axis=0, tiled=False)
    padded = height + 2 * ROWS
    inner = pl.pallas_call(
        interior_kernel,
        out_shape=jax.ShapeDtypeStruct(field.shape, f32),
        in_specs=[SMEM] * 2 + [VMEM] * 2,
        out_specs=VMEM,
        scratch_shapes=[
            pltpu.VMEM((2, species, depth, padded, width), f32),
            pltpu.VMEM((depth, padded, width), f32),
            pltpu.VMEM((depth, height, width), f32),
            pltpu.VMEM((depth, height, width), f32),
            pltpu.VMEM((depth, padded, width), f32),
            pltpu.VMEM((depth, height, width), f32),
            pltpu.VMEM((species, depth, height, width), f32),
        ],
        compiler_params=PARAMS,
        cost_estimate=pl.CostEstimate(flops=40_000_000, bytes_accessed=10_000_000, transcendentals=0),
        name="interior",
    )(velocity, rates, field, kappa)
    edges = pl.pallas_call(
        edge_kernel,
        out_shape=jax.ShapeDtypeStruct((species, depth, ROWS, LANES), f32),
        grid_spec=pltpu.PrefetchScalarGridSpec(
            num_scalar_prefetch=1,
            grid=(1,),
            in_specs=[
                SMEM,
                SMEM,
                pl.BlockSpec((1, tiles, ROWS, LANES), lambda i, plan: (plan[0], 0, 0, 0)),
                pl.BlockSpec((1, tiles, ROWS, LANES), lambda i, plan: (plan[1], 0, 0, 0)),
                VMEM,
            ],
            out_specs=pl.BlockSpec((species, depth, ROWS, LANES), lambda i, plan: (0, 0, 0, 0)),
            scratch_shapes=[
                pltpu.VMEM((2, species, depth + 2, 40, LANES), f32),
                pltpu.VMEM((depth + 2, 40, LANES), f32),
                pltpu.VMEM((depth + 2, 24, LANES), f32),
                pltpu.VMEM((depth + 2, 24, LANES), f32),
                pltpu.VMEM((depth + 2, 24, LANES), f32),
                pltpu.VMEM((depth + 2, 24, LANES), f32),
                pltpu.VMEM((species, depth + 2, 24, LANES), f32),
            ],
        ),
        compiler_params=PARAMS,
        name="edges",
    )(plan, velocity, rates, gathered, gathered, own)
    whole = pl.pallas_call(
        merge_kernel,
        out_shape=jax.ShapeDtypeStruct(field.shape, f32),
        in_specs=[VMEM] * 2,
        out_specs=VMEM,
        compiler_params=PARAMS,
        name="merge",
    )(inner, edges)
    planes = whole.reshape(species * depth, height, width)
    top = bits - 1
    branches = []
    for place in range(ROUNDS):
        for others in permutations(range(top), 2):
            order = list(others)
            order.insert(place, top)
            sizes = [(4, 4, 4, 4), (2, 4, 4, 4, 2), (2, 4, 5, 5)][place] if devices <= 16 else (species * depth,)
            if place == 0 and devices <= 16:
                sizes = (5, 5, 4, 2)
            branches.append(partial(route, bits=order, sizes=sizes))
    final = lax.switch(plan[4], branches, planes, plan[5:8])
    return final.reshape(concentration.shape)


def solution(mesh):
    spread = ("groups",) + AXES
    in_specs = (
        P(spread, None, None, None, None),
        P(spread, None, None, None),
        P(spread, None),
        P("groups", None),
        P("groups", None),
        P(None, "groups"),
        P("groups"),
    )
    out_specs = P(spread, None, None, None, None)
    return jax.shard_map(per_device, mesh=mesh, in_specs=in_specs, out_specs=out_specs, check_vma=False)
```

profile of v0, /device:TPU:4, one launch (start us, length us, event | category | flops | bytes accessed | tf_op | source)
XLA Modules:
  0.0 146.8 jit_solution(3197330030236102326)
XLA Ops:
  6.5 0.8 copy.27.neighbours_ref
  7.3 1.2 copy-done.1
  8.5 1.0 copy-done.3
  10.2 0.7 copy-done.8
  11.6 2.0 %prepare.1 = (s32[8]{0:T(128)S(1)}, f32[3,8,16,128]{3,2,1,0:T(8,128)S(1)}, f32[26,8,128]{2,1,0:T(8,128)}) custom-call(s32[1]{0:T(128)} %bitcast.90.here_ref, s32[16,2]{1,0:T(8,128)S(1)} %copy.27.neighbours_ref, s32[3,16]{1,0:T(4,128)S(1)} %copy-done.8, s32[3]{0:T(128)S(1)} %copy-done.9, f32[1,2]{1,0:T(1,128)S(1)} %copy-done.5, ...), custom_call_target="tpu_custom_call" | custom-call | tf_op jit(solution)/shard_map/prepare/pallas_call | solution.py:306
  14.8 10.2 %interior.1.u_ref = f32[2,8,128,128]{3,2,1,0:T(8,128)S(1)} custom-call(f32[2,3]{1,0:T(2,128)S(1)} %copy-done.7, f32[1,2]{1,0:T(1,128)S(1)} %copy-done.6, f32[2,8,128,128]{3,2,1,0:T(8,128)S(1)} %bitcast.98, f32[8,128,128]{2,1,0:T(8,128)S(1)} %bitcast.100), custom_call_target="tpu_custom_call" | custom-call | flops 40000000 | bytes 10000000 | tf_op jit(solution)/shard_map/interior/pallas_call | solution.py:320
  25.0 30.1 %all-gather.3.cloned.1.call-done = f32[416,8,128]{2,1,0:T(8,128)} async-done(((f32[26,8,128]{2,1,0:T(8,128)}), f32[416,8,128]{2,1,0:T(8,128)}) %all-gather.3.cloned.1.call-update) | async-done | bytes 1703952 | tf_op jit(solution)/shard_map/all_gather | solution.py:318
  55.1 1.5 copy-done
  56.6 5.9 %edges.1.edge_ref = f32[2,8,8,128]{3,2,1,0:T(8,128)S(1)} custom-call(s32[8]{0:T(128)S(1)} %get-tuple-element.172.plan_ref, f32[2,3]{1,0:T(2,128)S(1)} %copy-done.7, f32[1,2]{1,0:T(1,128)S(1)} %copy-done.6, f32[16,26,8,128]{3,2,1,0:T(8,128)S(1)} %bitcast.95, f32[16,26,8,128]{3,2,1,0:T(8,128)S(1)} %bitcast.96, f32[3,8,16,128]{3,2,1,0:T(8,128)S(1)} %get-tuple-element.174.own_ref), custom_call_target="tpu_custom_call" | custom-call | tf_op jit(solution)/shard_map/edges/pallas_call | solution.py:338
  62.9 77.1 %conditional.1 = (f32[1,2,8,128,128]{4,3,2,1,0:T(8,128)}) conditional(s32[]{:T(128)} %bitcast.93, (s32[8]{0:T(128)S(1)}, f32[2,8,128,128]{3,2,1,0:T(8,128)S(1)}) %tuple.77, (s32[8]{0:T(128)S(1)}, f32[2,8,128,128]{3,2,1,0:T(8,128)S(1)}) %tuple.77, (s32[8]{0:T(128)S(1)}, f32[2,8,128,128]{3,2,1,0:T(8,128)S(1)}) %tuple.77, ...), branch_computations={%region_0.1_spmd, %region_1.2_spmd, %region_2.3_spmd, %region_3.4_... | conditional | flops 1572867 | bytes 26214948 | solution.py:384
  64.7 7.5 %collective-permute-done.45 = f32[2,128,128]{2,1,0:T(8,128)S(1)} collective-permute-done((f32[2,128,128]{2,1,0:T(8,128)S(1)}, f32[2,128,128]{2,1,0:T(8,128)S(1)}, u32[]{:S(2)}, u32[]{:S(2)}) %collective-permute-start.45) | collective-permute-done | bytes 131104 | tf_op jit(solution)/shard_map/cond/branch_3_fun/ppermute | solution.py:282
  72.9 3.0 %collective-permute-start.42 = (f32[4,128,128]{2,1,0:T(8,128)S(1)}, f32[4,128,128]{2,1,0:T(8,128)S(1)}, u32[]{:S(2)}, u32[]{:S(2)}) collective-permute-start(f32[4,128,128]{2,1,0:T(8,128)S(1)} %slice.667), channel_id=1, source_target_pairs={{0,8},{1,9},{2,10},{3,11},{4,12},{5,13},{6,14},{7,15},{8,0},{9,1},... | collective-permute-start | bytes 786440 | tf_op jit(solution)/shard_map/cond/branch_3_fun/ppermute | solution.py:282
  77.8 17.3 %collective-permute-done.36 = f32[5,128,128]{2,1,0:T(8,128)S(1)} collective-permute-done((f32[5,128,128]{2,1,0:T(8,128)S(1)}, f32[5,128,128]{2,1,0:T(8,128)S(1)}, u32[]{:S(2)}, u32[]{:S(2)}) %collective-permute-start.36) | collective-permute-done | bytes 327712 | tf_op jit(solution)/shard_map/cond/branch_3_fun/ppermute | solution.py:282
  95.3 12.5 %collective-permute-done.42 = f32[4,128,128]{2,1,0:T(8,128)S(1)} collective-permute-done((f32[4,128,128]{2,1,0:T(8,128)S(1)}, f32[4,128,128]{2,1,0:T(8,128)S(1)}, u32[]{:S(2)}, u32[]{:S(2)}) %collective-permute-start.42) | collective-permute-done | bytes 262176 | tf_op jit(solution)/shard_map/cond/branch_3_fun/ppermute | solution.py:282
  107.8 1.3 collective-permute-start.43
  109.1 0.8 collective-permute-start.37
  110.0 4.8 %collective-permute-done.39 = f32[5,128,128]{2,1,0:T(8,128)S(1)} collective-permute-done((f32[5,128,128]{2,1,0:T(8,128)S(1)}, f32[5,128,128]{2,1,0:T(8,128)S(1)}, u32[]{:S(2)}, u32[]{:S(2)}) %collective-permute-start.39) | collective-permute-done | bytes 327712 | tf_op jit(solution)/shard_map/cond/branch_3_fun/ppermute | solution.py:282
  114.8 1.3 collective-permute-start.40
  116.1 1.0 collective-permute-done.43
  117.2 6.9 %collective-permute-done.37 = f32[5,128,128]{2,1,0:T(8,128)S(1)} collective-permute-done((f32[5,128,128]{2,1,0:T(8,128)S(1)}, f32[5,128,128]{2,1,0:T(8,128)S(1)}, u32[]{:S(2)}, u32[]{:S(2)}) %collective-permute-start.37) | collective-permute-done | bytes 327712 | tf_op jit(solution)/shard_map/cond/branch_3_fun/ppermute | solution.py:282
  124.2 5.8 %collective-permute-done.40 = f32[5,128,128]{2,1,0:T(8,128)S(1)} collective-permute-done((f32[5,128,128]{2,1,0:T(8,128)S(1)}, f32[5,128,128]{2,1,0:T(8,128)S(1)}, u32[]{:S(2)}, u32[]{:S(2)}) %collective-permute-start.40) | collective-permute-done | bytes 327712 | tf_op jit(solution)/shard_map/cond/branch_3_fun/ppermute | solution.py:282
  130.3 1.6 %collective-permute-done.38 = f32[5,128,128]{2,1,0:T(8,128)S(1)} collective-permute-done((f32[5,128,128]{2,1,0:T(8,128)S(1)}, f32[5,128,128]{2,1,0:T(8,128)S(1)}, u32[]{:S(2)}, u32[]{:S(2)}) %collective-permute-start.38) | collective-permute-done | bytes 327712 | tf_op jit(solution)/shard_map/cond/branch_3_fun/ppermute | solution.py:282
  131.9 7.0 %collective-permute-done.41 = f32[5,128,128]{2,1,0:T(8,128)S(1)} collective-permute-done((f32[5,128,128]{2,1,0:T(8,128)S(1)}, f32[5,128,128]{2,1,0:T(8,128)S(1)}, u32[]{:S(2)}, u32[]{:S(2)}) %collective-permute-start.41) | collective-permute-done | bytes 327712 | tf_op jit(solution)/shard_map/cond/branch_3_fun/ppermute | solution.py:282
  138.9 1.0 pad_maximum_fusion.3
  (47 shorter events, 5.6 us)
Async XLA Ops:
  6.5 8.2 %copy-start.6 = (f32[1,2]{1,0:T(1,128)S(1)}, f32[1,2]{1,0:T(1,128)}, u32[]{:S(2)}) copy-start(f32[1,2]{1,0:T(1,128)} %rates_ref.5) | copy-start | bytes 28
  6.5 8.2 %copy-start.7 = (f32[2,3]{1,0:T(2,128)S(1)}, f32[2,3]{1,0:T(2,128)}, u32[]{:S(2)}) copy-start(f32[2,3]{1,0:T(2,128)} %velocity_ref.3) | copy-start | bytes 76
  6.5 48.6 %all-gather.3.cloned.1.call-start = ((), (), s32[]{:S(2)}) async-start(), calls=%async_computation | async-start | bytes 1810432 | tf_op jit(solution)/shard_map/all_gather | solution.py:318
  7.3 1.2 copy-start.1
  8.5 1.0 copy-start.3
  9.6 0.7 copy-start.5
  10.2 0.7 copy-start.8
  10.9 0.7 copy-start.9
  11.6 3.2 %copy-start.2 = (f32[1,2,8,128,128]{4,3,2,1,0:T(8,128)S(1)}, f32[1,2,8,128,128]{4,3,2,1,0:T(8,128)}, u32[]{:S(2)}) copy-start(f32[1,2,8,128,128]{4,3,2,1,0:T(8,128)} %param.25) | copy-start | bytes 3145732
  11.6 3.2 %copy-start.4 = (f32[1,8,128,128]{3,2,1,0:T(8,128)S(1)}, f32[1,8,128,128]{3,2,1,0:T(8,128)}, u32[]{:S(2)}) copy-start(f32[1,8,128,128]{3,2,1,0:T(8,128)} %param.26) | copy-start | bytes 1572868
  55.1 1.5 copy-start
  62.9 9.3 %collective-permute-start.45 = (f32[2,128,128]{2,1,0:T(8,128)S(1)}, f32[2,128,128]{2,1,0:T(8,128)S(1)}, u32[]{:S(2)}, u32[]{:S(2)}) collective-permute-start(f32[2,128,128]{2,1,0:T(8,128)S(1)} %slice.668), channel_id=1, source_target_pairs={{0,8},{1,9},{2,10},{3,11},{4,12},{5,13},{6,14},{7,15},{8,0},{9,1},... | collective-permute-start | bytes 393224 | tf_op jit(solution)/shard_map/cond/branch_3_fun/ppermute | solution.py:282
  72.2 5.5 %collective-permute-start.46 = (f32[2,128,128]{2,1,0:T(8,128)S(1)}, f32[2,128,128]{2,1,0:T(8,128)S(1)}, u32[]{:S(2)}, u32[]{:S(2)}) collective-permute-start(f32[2,128,128]{2,1,0:T(8,128)S(1)} %broadcast_select_fusion.45), channel_id=1, source_target_pairs={{0,2},{1,3},{2,0},{3,1},{4,6},{5,7},{6,4},{7,5},{8,10},{9,11},{10,... | collective-permute-start | bytes 393224 | tf_op jit(solution)/shard_map/cond/branch_3_fun/ppermute | solution.py:282
  72.8 22.3 %collective-permute-start.36 = (f32[5,128,128]{2,1,0:T(8,128)S(1)}, f32[5,128,128]{2,1,0:T(8,128)S(1)}, u32[]{:S(2)}, u32[]{:S(2)}) collective-permute-start(f32[5,128,128]{2,1,0:T(8,128)S(1)} %slice.665), channel_id=1, source_target_pairs={{0,8},{1,9},{2,10},{3,11},{4,12},{5,13},{6,14},{7,15},{8,0},{9,1},... | collective-permute-start | bytes 983048 | tf_op jit(solution)/shard_map/cond/branch_3_fun/ppermute | solution.py:282
  72.9 34.9 %collective-permute-start.42 = (f32[4,128,128]{2,1,0:T(8,128)S(1)}, f32[4,128,128]{2,1,0:T(8,128)S(1)}, u32[]{:S(2)}, u32[]{:S(2)}) collective-permute-start(f32[4,128,128]{2,1,0:T(8,128)S(1)} %slice.667), channel_id=1, source_target_pairs={{0,8},{1,9},{2,10},{3,11},{4,12},{5,13},{6,14},{7,15},{8,0},{9,1},... | collective-permute-start | bytes 786440 | tf_op jit(solution)/shard_map/cond/branch_3_fun/ppermute | solution.py:282
  77.8 32.2 %collective-permute-start.47 = (f32[2,128,128]{2,1,0:T(8,128)S(1)}, f32[2,128,128]{2,1,0:T(8,128)S(1)}, u32[]{:S(2)}, u32[]{:S(2)}) collective-permute-start(f32[2,128,128]{2,1,0:T(8,128)S(1)} %broadcast_select_fusion.46), channel_id=1, source_target_pairs={{0,4},{1,5},{2,6},{3,7},{4,0},{5,1},{6,2},{7,3},{8,12},{9,13},{10,... | collective-permute-start | bytes 393224 | tf_op jit(solution)/shard_map/cond/branch_3_fun/ppermute | solution.py:282
  95.2 19.5 %collective-permute-start.39 = (f32[5,128,128]{2,1,0:T(8,128)S(1)}, f32[5,128,128]{2,1,0:T(8,128)S(1)}, u32[]{:S(2)}, u32[]{:S(2)}) collective-permute-start(f32[5,128,128]{2,1,0:T(8,128)S(1)} %get-tuple-element.192), channel_id=1, source_target_pairs={{0,8},{1,9},{2,10},{3,11},{4,12},{5,13},{6,14},{7,15},{8,0},{9,1},... | collective-permute-start | bytes 983048 | tf_op jit(solution)/shard_map/cond/branch_3_fun/ppermute | solution.py:282
  107.8 9.2 %collective-permute-start.43 = (f32[4,128,128]{2,1,0:T(8,128)S(1)}, f32[4,128,128]{2,1,0:T(8,128)S(1)}, u32[]{:S(2)}, u32[]{:S(2)}) collective-permute-start(f32[4,128,128]{2,1,0:T(8,128)S(1)} %broadcast_select_fusion.42), channel_id=1, source_target_pairs={{0,2},{1,3},{2,0},{3,1},{4,6},{5,7},{6,4},{7,5},{8,10},{9,11},{10,... | collective-permute-start | bytes 786440 | tf_op jit(solution)/shard_map/cond/branch_3_fun/ppermute | solution.py:282
  109.1 15.0 %collective-permute-start.37 = (f32[5,128,128]{2,1,0:T(8,128)S(1)}, f32[5,128,128]{2,1,0:T(8,128)S(1)}, u32[]{:S(2)}, u32[]{:S(2)}) collective-permute-start(f32[5,128,128]{2,1,0:T(8,128)S(1)} %get-tuple-element.191), channel_id=1, source_target_pairs={{0,2},{1,3},{2,0},{3,1},{4,6},{5,7},{6,4},{7,5},{8,10},{9,11},{10,... | collective-permute-start | bytes 983048 | tf_op jit(solution)/shard_map/cond/branch_3_fun/ppermute | solution.py:282
  114.8 15.3 %collective-permute-start.40 = (f32[5,128,128]{2,1,0:T(8,128)S(1)}, f32[5,128,128]{2,1,0:T(8,128)S(1)}, u32[]{:S(2)}, u32[]{:S(2)}) collective-permute-start(f32[5,128,128]{2,1,0:T(8,128)S(1)} %broadcast_select_fusion.36), channel_id=1, source_target_pairs={{0,2},{1,3},{2,0},{3,1},{4,6},{5,7},{6,4},{7,5},{8,10},{9,11},{10,... | collective-permute-start | bytes 983048 | tf_op jit(solution)/shard_map/cond/branch_3_fun/ppermute | solution.py:282
  117.1 13.1 %collective-permute-start.44 = (f32[4,128,128]{2,1,0:T(8,128)S(1)}, f32[4,128,128]{2,1,0:T(8,128)S(1)}, u32[]{:S(2)}, u32[]{:S(2)}) collective-permute-start(f32[4,128,128]{2,1,0:T(8,128)S(1)} %broadcast_select_fusion.43), channel_id=1, source_target_pairs={{0,4},{1,5},{2,6},{3,7},{4,0},{5,1},{6,2},{7,3},{8,12},{9,13},{10,... | collective-permute-start | bytes 786440 | tf_op jit(solution)/shard_map/cond/branch_3_fun/ppermute | solution.py:282
  124.2 7.7 %collective-permute-start.38 = (f32[5,128,128]{2,1,0:T(8,128)S(1)}, f32[5,128,128]{2,1,0:T(8,128)S(1)}, u32[]{:S(2)}, u32[]{:S(2)}) collective-permute-start(f32[5,128,128]{2,1,0:T(8,128)S(1)} %broadcast_select_fusion.39), channel_id=1, source_target_pairs={{0,4},{1,5},{2,6},{3,7},{4,0},{5,1},{6,2},{7,3},{8,12},{9,13},{10,... | collective-permute-start | bytes 983048 | tf_op jit(solution)/shard_map/cond/branch_3_fun/ppermute | solution.py:282
  130.1 8.7 %collective-permute-start.41 = (f32[5,128,128]{2,1,0:T(8,128)S(1)}, f32[5,128,128]{2,1,0:T(8,128)S(1)}, u32[]{:S(2)}, u32[]{:S(2)}) collective-permute-start(f32[5,128,128]{2,1,0:T(8,128)S(1)} %broadcast_select_fusion.38), channel_id=1, source_target_pairs={{0,4},{1,5},{2,6},{3,7},{4,0},{5,1},{6,2},{7,3},{8,12},{9,13},{10,... | collective-permute-start | bytes 983048 | tf_op jit(solution)/shard_map/cond/branch_3_fun/ppermute | solution.py:282
Sparse Core Ops, SparseCore 0:
  13.7 41.3 all-gather.2
where the time goes:
time: 147 us
  waiting for transfers between devices  95.1 us (65%)
  Pallas kernels  18.5 us (13%)
  between operations  14 us (10%)
  starting transfers between devices  7.92 us (5%)
  local copies, waits for them, and re-layouts  7.79 us (5%)
  loops' own time  2.04 us (1%)
  other arithmetic  1.47 us (1%)
    ppermute x12, waiting for transfers between devices, swap(): lax.ppermute(block, AXES, [(low, low ^ 1 << bit) for low in range(count)])  65 us
    all_gather x1, waiting for transfers between devices, per_device(): gathered = lax.all_gather(sent, AXES, axis=0, tiled=False)  30.1 us
    pallas_call x1, Pallas kernels, per_device(): pl.pallas_call(interior_kernel, out_shape=jax.ShapeDtypeStruct(field.shap...  10.2 us
    ppermute x12, starting transfers between devices, swap(): lax.ppermute(block, AXES, [(low, low ^ 1 << bit) for low in range(count)])  7.91 us
    unnamed x21, local copies, waits for them, and re-layouts  6.5 us
    pallas_call x1, Pallas kernels, per_device(): pl.pallas_call(edge_kernel, out_shape=jax.ShapeDtypeStruct((species, dept...  5.87 us
  transfers between devices with their start and end apart: 13, of which 11 were waited for; matrix products, arithmetic and copies ran while one was open for 1% of the time, Pallas kernels for 7%

commit v1 on v0

--- a/solution.py
+++ b/solution.py
@@ -283,15 +283,20 @@
 
 
 def route(field, moved, bits, sizes):
-    out = []
+    top = max(bits)
+    done = [[] for _ in bits]
     start = 0
     for size in sizes:
         part = field[start : start + size]
         for r, bit in enumerate(bits):
-            part = jnp.where(moved[r] > 0, swap(part, bit), part)
-        out.append(part)
+            ahead = 2 if bit == top else 1
+            if len(done[r]) >= ahead:
+                part, done[r][-ahead] = lax.optimization_barrier((part, done[r][-ahead]))
+            other = swap(part, bit)
+            part = jnp.where(moved[r] > 0, other, part)
+            done[r].append(part)
         start += size
-    return jnp.concatenate(out, axis=0)
+    return jnp.concatenate(done[-1], axis=0)
 
 
 def per_device(concentration, diffusivity, rates, velocity, neighbours, migrate, bit_order):
@@ -377,9 +382,7 @@
         for others in permutations(range(top), 2):
             order = list(others)
             order.insert(place, top)
-            sizes = [(4, 4, 4, 4), (2, 4, 4, 4, 2), (2, 4, 5, 5)][place] if devices <= 16 else (species * depth,)
-            if place == 0 and devices <= 16:
-                sizes = (5, 5, 4, 2)
+            sizes = (2,) * depth if devices <= 16 else (species * depth,)
             branches.append(partial(route, bits=order, sizes=sizes))
     final = lax.switch(plan[4], branches, planes, plan[5:8])
     return final.reshape(concentration.shape)

time: 147 us -> 175 us (1.19); the launches traced: 147 us -> 172 us
  loops' own time: 2.04 us -> 25.3 us
  waiting for transfers between devices: 95.1 us -> 77.6 us
  starting transfers between devices: 7.92 us -> 22.6 us
  local copies, waits for them, and re-layouts: 7.79 us -> 12.4 us
    another operation x1, loops' own time: 2.04 us -> 25.3 us  [per_device(): final = lax.switch(plan[4], branches, planes, plan[5:8])]
    ppermute x12 -> x24, waiting for transfers between devices: 65 us -> 47.4 us  [swap(): lax.ppermute(block, AXES, [(low, low ^ 1 << bit) for low in range(count)])]
    ppermute x12 -> x24, starting transfers between devices: 7.91 us -> 22.6 us  [swap(): lax.ppermute(block, AXES, [(low, low ^ 1 << bit) for low in range(count)])]
    cond x0 -> x7, local copies, waits for them, and re-layouts: none -> 4.65 us
  transfers between devices with their start and end apart: 13 -> 25, of which waited for: 11 -> 13; matrix products, arithmetic and copies ran while one was open for 1% -> 4% of each run, Pallas kernels for 7% -> 6%
where the time goes in v1:
time: 175 us; the launch traced here: 172 us
  waiting for transfers between devices  77.6 us (44%)
  loops' own time  25.3 us (14%)
  starting transfers between devices  22.6 us (13%)
  Pallas kernels  18.5 us (11%)
  between operations  14.6 us (8%)
  local copies, waits for them, and re-layouts  12.4 us (7%)
    ppermute x24, waiting for transfers between devices, swap(): lax.ppermute(block, AXES, [(low, low ^ 1 << bit) for low in range(count)])  47.4 us
    all_gather x1, waiting for transfers between devices, per_device(): gathered = lax.all_gather(sent, AXES, axis=0, tiled=False)  30.1 us
    another operation x1, loops' own time, per_device(): final = lax.switch(plan[4], branches, planes, plan[5:8])  25.3 us
    ppermute x24, starting transfers between devices, swap(): lax.ppermute(block, AXES, [(low, low ^ 1 << bit) for low in range(count)])  22.6 us
    pallas_call x1, Pallas kernels, per_device(): pl.pallas_call(interior_kernel, out_shape=jax.ShapeDtypeStruct(field.shap...  10.2 us
    unnamed x21, local copies, waits for them, and re-layouts  6.5 us
    pallas_call x1, Pallas kernels, per_device(): pl.pallas_call(edge_kernel, out_shape=jax.ShapeDtypeStruct((species, dept...  5.87 us
    cond x7, local copies, waits for them, and re-layouts  4.65 us
  transfers between devices with their start and end apart: 25, of which 13 were waited for; matrix products, arithmetic and copies ran while one was open for 4% of the time, Pallas kernels for 6%

profile of v1, /device:TPU:4, one launch (start us, length us, event | category | flops | bytes accessed | tf_op | source)
XLA Modules:
  0.0 172.1 jit_solution(13809039603706037135)
XLA Ops:
  6.5 0.8 copy.27.neighbours_ref
  7.3 1.2 copy-done.1
  8.5 1.0 copy-done.3
  11.6 2.0 %prepare.1 = (s32[8]{0:T(128)S(1)}, f32[3,8,16,128]{3,2,1,0:T(8,128)S(1)}, f32[26,8,128]{2,1,0:T(8,128)}) custom-call(s32[1]{0:T(128)} %bitcast.90.here_ref, s32[16,2]{1,0:T(8,128)S(1)} %copy.27.neighbours_ref, s32[3,16]{1,0:T(4,128)S(1)} %copy-done.8, s32[3]{0:T(128)S(1)} %copy-done.9, f32[1,2]{1,0:T(1,128)S(1)} %copy-done.5, ...), custom_call_target="tpu_custom_call" | custom-call | tf_op jit(solution)/shard_map/prepare/pallas_call | solution.py:311
  14.7 10.2 %interior.1.u_ref = f32[2,8,128,128]{3,2,1,0:T(8,128)S(1)} custom-call(f32[2,3]{1,0:T(2,128)S(1)} %copy-done.7, f32[1,2]{1,0:T(1,128)S(1)} %copy-done.6, f32[2,8,128,128]{3,2,1,0:T(8,128)S(1)} %bitcast.98, f32[8,128,128]{2,1,0:T(8,128)S(1)} %bitcast.100), custom_call_target="tpu_custom_call" | custom-call | flops 40000000 | bytes 10000000 | tf_op jit(solution)/shard_map/interior/pallas_call | solution.py:325
  25.0 30.1 %all-gather.3.cloned.1.call-done = f32[416,8,128]{2,1,0:T(8,128)} async-done(((f32[26,8,128]{2,1,0:T(8,128)}), f32[416,8,128]{2,1,0:T(8,128)}) %all-gather.3.cloned.1.call-update) | async-done | bytes 1703952 | tf_op jit(solution)/shard_map/all_gather | solution.py:323
  55.1 1.5 copy-done
  56.5 5.9 %edges.1.edge_ref = f32[2,8,8,128]{3,2,1,0:T(8,128)S(1)} custom-call(s32[8]{0:T(128)S(1)} %get-tuple-element.652.plan_ref, f32[2,3]{1,0:T(2,128)S(1)} %copy-done.7, f32[1,2]{1,0:T(1,128)S(1)} %copy-done.6, f32[16,26,8,128]{3,2,1,0:T(8,128)S(1)} %bitcast.95, f32[16,26,8,128]{3,2,1,0:T(8,128)S(1)} %bitcast.96, f32[3,8,16,128]{3,2,1,0:T(8,128)S(1)} %get-tuple-element.654.own_ref), custom_call_target="tpu_custom_call" | custom-call | tf_op jit(solution)/shard_map/edges/pallas_call | solution.py:343
  62.9 101.8 %conditional.1 = (f32[1,2,8,128,128]{4,3,2,1,0:T(8,128)}) conditional(s32[]{:T(128)} %bitcast.93, (s32[8]{0:T(128)S(1)}, f32[2,8,128,128]{3,2,1,0:T(8,128)S(1)}) %tuple.437, (s32[8]{0:T(128)S(1)}, f32[2,8,128,128]{3,2,1,0:T(8,128)S(1)}) %tuple.437, (s32[8]{0:T(128)S(1)}, f32[2,8,128,128]{3,2,1,0:T(8,128)S(1)}) %tuple.437, ...), branch_computations={%region_0.1_spmd, %region_1.2_spmd, %region_2.3_spmd, %region_3.4_... | conditional | flops 786435 | bytes 25953804 | solution.py:387
  63.5 2.4 %collective-permute-start.25 = (f32[2,128,128]{2,1,0:T(8,128)S(1)}, f32[2,128,128]{2,1,0:T(8,128)S(1)}, u32[]{:S(2)}, u32[]{:S(2)}) collective-permute-start(f32[2,128,128]{2,1,0:T(8,128)S(1)} %get-tuple-element.677), channel_id=1, source_target_pairs={{0,8},{1,9},{2,10},{3,11},{4,12},{5,13},{6,14},{7,15},{8,0},{9,1},... | collective-permute-start | bytes 393224 | tf_op jit(solution)/shard_map/cond/branch_1_fun/ppermute | solution.py:282
  67.2 7.8 %collective-permute-done.24 = f32[2,128,128]{2,1,0:T(8,128)S(1)} collective-permute-done((f32[2,128,128]{2,1,0:T(8,128)S(1)}, f32[2,128,128]{2,1,0:T(8,128)S(1)}, u32[]{:S(2)}, u32[]{:S(2)}) %collective-permute-start.24) | collective-permute-done | bytes 131104 | tf_op jit(solution)/shard_map/cond/branch_1_fun/ppermute | solution.py:282
  75.1 2.7 %collective-permute-done.25 = f32[2,128,128]{2,1,0:T(8,128)S(1)} collective-permute-done((f32[2,128,128]{2,1,0:T(8,128)S(1)}, f32[2,128,128]{2,1,0:T(8,128)S(1)}, u32[]{:S(2)}, u32[]{:S(2)}) %collective-permute-start.25) | collective-permute-done | bytes 131104 | tf_op jit(solution)/shard_map/cond/branch_1_fun/ppermute | solution.py:282
  79.4 2.9 %collective-permute-start.32 = (f32[2,128,128]{2,1,0:T(8,128)S(1)}, f32[2,128,128]{2,1,0:T(8,128)S(1)}, u32[]{:S(2)}, u32[]{:S(2)}) collective-permute-start(f32[2,128,128]{2,1,0:T(8,128)S(1)} %get-tuple-element.170), channel_id=1, source_target_pairs={{0,8},{1,9},{2,10},{3,11},{4,12},{5,13},{6,14},{7,15},{8,0},{9,1},... | collective-permute-start | bytes 393224 | tf_op jit(solution)/shard_map/cond/branch_1_fun/ppermute | solution.py:282
  82.5 8.3 %collective-permute-done.29 = f32[2,128,128]{2,1,0:T(8,128)S(1)} collective-permute-done((f32[2,128,128]{2,1,0:T(8,128)S(1)}, f32[2,128,128]{2,1,0:T(8,128)S(1)}, u32[]{:S(2)}, u32[]{:S(2)}) %collective-permute-start.29) | collective-permute-done | bytes 131104 | tf_op jit(solution)/shard_map/cond/branch_1_fun/ppermute | solution.py:282
  90.8 2.7 %collective-permute-done.32 = f32[2,128,128]{2,1,0:T(8,128)S(1)} collective-permute-done((f32[2,128,128]{2,1,0:T(8,128)S(1)}, f32[2,128,128]{2,1,0:T(8,128)S(1)}, u32[]{:S(2)}, u32[]{:S(2)}) %collective-permute-start.32) | collective-permute-done | bytes 131104 | tf_op jit(solution)/shard_map/cond/branch_1_fun/ppermute | solution.py:282
  93.9 8.3 %collective-permute-start.31 = (f32[2,128,128]{2,1,0:T(8,128)S(1)}, f32[2,128,128]{2,1,0:T(8,128)S(1)}, u32[]{:S(2)}, u32[]{:S(2)}) collective-permute-start(f32[2,128,128]{2,1,0:T(8,128)S(1)} %broadcast_select_fusion.44), channel_id=1, source_target_pairs={{0,4},{1,5},{2,6},{3,7},{4,0},{5,1},{6,2},{7,3},{8,12},{9,13},{10,... | collective-permute-start | bytes 393224 | tf_op jit(solution)/shard_map/cond/branch_1_fun/ppermute | solution.py:282
  102.3 3.8 %collective-permute-done.31 = f32[2,128,128]{2,1,0:T(8,128)S(1)} collective-permute-done((f32[2,128,128]{2,1,0:T(8,128)S(1)}, f32[2,128,128]{2,1,0:T(8,128)S(1)}, u32[]{:S(2)}, u32[]{:S(2)}) %collective-permute-start.31) | collective-permute-done | bytes 131104 | tf_op jit(solution)/shard_map/cond/branch_1_fun/ppermute | solution.py:282
  106.1 2.5 %collective-permute-start.34 = (f32[2,128,128]{2,1,0:T(8,128)S(1)}, f32[2,128,128]{2,1,0:T(8,128)S(1)}, u32[]{:S(2)}, u32[]{:S(2)}) collective-permute-start(f32[2,128,128]{2,1,0:T(8,128)S(1)} %broadcast_select_fusion.43), channel_id=1, source_target_pairs={{0,4},{1,5},{2,6},{3,7},{4,0},{5,1},{6,2},{7,3},{8,12},{9,13},{10,... | collective-permute-start | bytes 393224 | tf_op jit(solution)/shard_map/cond/branch_1_fun/ppermute | solution.py:282
  108.7 3.6 %collective-permute-start.44 = (f32[2,128,128]{2,1,0:T(8,128)S(1)}, f32[2,128,128]{2,1,0:T(8,128)S(1)}, u32[]{:S(2)}, u32[]{:S(2)}) collective-permute-start(f32[2,128,128]{2,1,0:T(8,128)S(1)} %get-tuple-element.186), channel_id=1, source_target_pairs={{0,8},{1,9},{2,10},{3,11},{4,12},{5,13},{6,14},{7,15},{8,0},{9,1},... | collective-permute-start | bytes 393224 | tf_op jit(solution)/shard_map/cond/branch_1_fun/ppermute | solution.py:282
  114.6 5.7 %collective-permute-done.37 = f32[2,128,128]{2,1,0:T(8,128)S(1)} collective-permute-done((f32[2,128,128]{2,1,0:T(8,128)S(1)}, f32[2,128,128]{2,1,0:T(8,128)S(1)}, u32[]{:S(2)}, u32[]{:S(2)}) %collective-permute-start.37) | collective-permute-done | bytes 131104 | tf_op jit(solution)/shard_map/cond/branch_1_fun/ppermute | solution.py:282
  120.6 5.0 %collective-permute-done.40 = f32[2,128,128]{2,1,0:T(8,128)S(1)} collective-permute-done((f32[2,128,128]{2,1,0:T(8,128)S(1)}, f32[2,128,128]{2,1,0:T(8,128)S(1)}, u32[]{:S(2)}, u32[]{:S(2)}) %collective-permute-start.40) | collective-permute-done | bytes 131104 | tf_op jit(solution)/shard_map/cond/branch_1_fun/ppermute | solution.py:282
  127.3 3.4 %collective-permute-done.43 = f32[2,128,128]{2,1,0:T(8,128)S(1)} collective-permute-done((f32[2,128,128]{2,1,0:T(8,128)S(1)}, f32[2,128,128]{2,1,0:T(8,128)S(1)}, u32[]{:S(2)}, u32[]{:S(2)}) %collective-permute-start.43) | collective-permute-done | bytes 131104 | tf_op jit(solution)/shard_map/cond/branch_1_fun/ppermute | solution.py:282
  132.4 3.4 %collective-permute-done.46 = f32[2,128,128]{2,1,0:T(8,128)S(1)} collective-permute-done((f32[2,128,128]{2,1,0:T(8,128)S(1)}, f32[2,128,128]{2,1,0:T(8,128)S(1)}, u32[]{:S(2)}, u32[]{:S(2)}) %collective-permute-start.46) | collective-permute-done | bytes 131104 | tf_op jit(solution)/shard_map/cond/branch_1_fun/ppermute | solution.py:282
  137.5 3.4 %collective-permute-done.47 = f32[2,128,128]{2,1,0:T(8,128)S(1)} collective-permute-done((f32[2,128,128]{2,1,0:T(8,128)S(1)}, f32[2,128,128]{2,1,0:T(8,128)S(1)}, u32[]{:S(2)}, u32[]{:S(2)}) %collective-permute-start.47) | collective-permute-done | bytes 131104 | tf_op jit(solution)/shard_map/cond/branch_1_fun/ppermute | solution.py:282
  (86 shorter events, 13.7 us)
Async XLA Ops:
  6.5 48.5 %all-gather.3.cloned.1.call-start = ((), (), s32[]{:S(2)}) async-start(), calls=%async_computation | async-start | bytes 1810432 | tf_op jit(solution)/shard_map/all_gather | solution.py:323
  62.9 12.1 %collective-permute-start.24 = (f32[2,128,128]{2,1,0:T(8,128)S(1)}, f32[2,128,128]{2,1,0:T(8,128)S(1)}, u32[]{:S(2)}, u32[]{:S(2)}) collective-permute-start(f32[2,128,128]{2,1,0:T(8,128)S(1)} %get-tuple-element.678), channel_id=1, source_target_pairs={{0,8},{1,9},{2,10},{3,11},{4,12},{5,13},{6,14},{7,15},{8,0},{9,1},... | collective-permute-start | bytes 393224 | tf_op jit(solution)/shard_map/cond/branch_1_fun/ppermute | solution.py:282
  63.5 14.3 %collective-permute-start.25 = (f32[2,128,128]{2,1,0:T(8,128)S(1)}, f32[2,128,128]{2,1,0:T(8,128)S(1)}, u32[]{:S(2)}, u32[]{:S(2)}) collective-permute-start(f32[2,128,128]{2,1,0:T(8,128)S(1)} %get-tuple-element.677), channel_id=1, source_target_pairs={{0,8},{1,9},{2,10},{3,11},{4,12},{5,13},{6,14},{7,15},{8,0},{9,1},... | collective-permute-start | bytes 393224 | tf_op jit(solution)/shard_map/cond/branch_1_fun/ppermute | solution.py:282
  77.9 4.4 %collective-permute-start.26 = (f32[2,128,128]{2,1,0:T(8,128)S(1)}, f32[2,128,128]{2,1,0:T(8,128)S(1)}, u32[]{:S(2)}, u32[]{:S(2)}) collective-permute-start(f32[2,128,128]{2,1,0:T(8,128)S(1)} %get-tuple-element.671), channel_id=1, source_target_pairs={{0,1},{1,0},{2,3},{3,2},{4,5},{5,4},{6,7},{7,6},{8,9},{9,8},{10,11... | collective-permute-start | bytes 393224 | tf_op jit(solution)/shard_map/cond/branch_1_fun/ppermute | solution.py:282
  79.3 11.4 %collective-permute-start.29 = (f32[2,128,128]{2,1,0:T(8,128)S(1)}, f32[2,128,128]{2,1,0:T(8,128)S(1)}, u32[]{:S(2)}, u32[]{:S(2)}) collective-permute-start(f32[2,128,128]{2,1,0:T(8,128)S(1)} %get-tuple-element.166), channel_id=1, source_target_pairs={{0,8},{1,9},{2,10},{3,11},{4,12},{5,13},{6,14},{7,15},{8,0},{9,1},... | collective-permute-start | bytes 393224 | tf_op jit(solution)/shard_map/cond/branch_1_fun/ppermute | solution.py:282
  79.4 14.1 %collective-permute-start.32 = (f32[2,128,128]{2,1,0:T(8,128)S(1)}, f32[2,128,128]{2,1,0:T(8,128)S(1)}, u32[]{:S(2)}, u32[]{:S(2)}) collective-permute-start(f32[2,128,128]{2,1,0:T(8,128)S(1)} %get-tuple-element.170), channel_id=1, source_target_pairs={{0,8},{1,9},{2,10},{3,11},{4,12},{5,13},{6,14},{7,15},{8,0},{9,1},... | collective-permute-start | bytes 393224 | tf_op jit(solution)/shard_map/cond/branch_1_fun/ppermute | solution.py:282
  82.3 11.5 %collective-permute-start.28 = (f32[2,128,128]{2,1,0:T(8,128)S(1)}, f32[2,128,128]{2,1,0:T(8,128)S(1)}, u32[]{:S(2)}, u32[]{:S(2)}) collective-permute-start(f32[2,128,128]{2,1,0:T(8,128)S(1)} %broadcast_select_fusion.45), channel_id=1, source_target_pairs={{0,4},{1,5},{2,6},{3,7},{4,0},{5,1},{6,2},{7,3},{8,12},{9,13},{10,... | collective-permute-start | bytes 393224 | tf_op jit(solution)/shard_map/cond/branch_1_fun/ppermute | solution.py:282
  82.4 11.4 %collective-permute-start.27 = (f32[2,128,128]{2,1,0:T(8,128)S(1)}, f32[2,128,128]{2,1,0:T(8,128)S(1)}, u32[]{:S(2)}, u32[]{:S(2)}) collective-permute-start(f32[2,128,128]{2,1,0:T(8,128)S(1)} %get-tuple-element.164), channel_id=1, source_target_pairs={{0,1},{1,0},{2,3},{3,2},{4,5},{5,4},{6,7},{7,6},{8,9},{9,8},{10,11... | collective-permute-start | bytes 393224 | tf_op jit(solution)/shard_map/cond/branch_1_fun/ppermute | solution.py:282
  90.7 11.4 %collective-permute-start.35 = (f32[2,128,128]{2,1,0:T(8,128)S(1)}, f32[2,128,128]{2,1,0:T(8,128)S(1)}, u32[]{:S(2)}, u32[]{:S(2)}) collective-permute-start(f32[2,128,128]{2,1,0:T(8,128)S(1)} %get-tuple-element.174), channel_id=1, source_target_pairs={{0,8},{1,9},{2,10},{3,11},{4,12},{5,13},{6,14},{7,15},{8,0},{9,1},... | collective-permute-start | bytes 393224 | tf_op jit(solution)/shard_map/cond/branch_1_fun/ppermute | solution.py:282
  93.5 15.2 %collective-permute-start.38 = (f32[2,128,128]{2,1,0:T(8,128)S(1)}, f32[2,128,128]{2,1,0:T(8,128)S(1)}, u32[]{:S(2)}, u32[]{:S(2)}) collective-permute-start(f32[2,128,128]{2,1,0:T(8,128)S(1)} %get-tuple-element.178), channel_id=1, source_target_pairs={{0,8},{1,9},{2,10},{3,11},{4,12},{5,13},{6,14},{7,15},{8,0},{9,1},... | collective-permute-start | bytes 393224 | tf_op jit(solution)/shard_map/cond/branch_1_fun/ppermute | solution.py:282
  93.9 12.2 %collective-permute-start.31 = (f32[2,128,128]{2,1,0:T(8,128)S(1)}, f32[2,128,128]{2,1,0:T(8,128)S(1)}, u32[]{:S(2)}, u32[]{:S(2)}) collective-permute-start(f32[2,128,128]{2,1,0:T(8,128)S(1)} %broadcast_select_fusion.44), channel_id=1, source_target_pairs={{0,4},{1,5},{2,6},{3,7},{4,0},{5,1},{6,2},{7,3},{8,12},{9,13},{10,... | collective-permute-start | bytes 393224 | tf_op jit(solution)/shard_map/cond/branch_1_fun/ppermute | solution.py:282
  102.2 3.9 %collective-permute-start.30 = (f32[2,128,128]{2,1,0:T(8,128)S(1)}, f32[2,128,128]{2,1,0:T(8,128)S(1)}, u32[]{:S(2)}, u32[]{:S(2)}) collective-permute-start(f32[2,128,128]{2,1,0:T(8,128)S(1)} %broadcast_select_fusion.35), channel_id=1, source_target_pairs={{0,1},{1,0},{2,3},{3,2},{4,5},{5,4},{6,7},{7,6},{8,9},{9,8},{10,11... | collective-permute-start | bytes 393224 | tf_op jit(solution)/shard_map/cond/branch_1_fun/ppermute | solution.py:282
  102.2 12.2 %collective-permute-start.41 = (f32[2,128,128]{2,1,0:T(8,128)S(1)}, f32[2,128,128]{2,1,0:T(8,128)S(1)}, u32[]{:S(2)}, u32[]{:S(2)}) collective-permute-start(f32[2,128,128]{2,1,0:T(8,128)S(1)} %get-tuple-element.182), channel_id=1, source_target_pairs={{0,8},{1,9},{2,10},{3,11},{4,12},{5,13},{6,14},{7,15},{8,0},{9,1},... | collective-permute-start | bytes 393224 | tf_op jit(solution)/shard_map/cond/branch_1_fun/ppermute | solution.py:282
  106.1 7.4 %collective-permute-start.34 = (f32[2,128,128]{2,1,0:T(8,128)S(1)}, f32[2,128,128]{2,1,0:T(8,128)S(1)}, u32[]{:S(2)}, u32[]{:S(2)}) collective-permute-start(f32[2,128,128]{2,1,0:T(8,128)S(1)} %broadcast_select_fusion.43), channel_id=1, source_target_pairs={{0,4},{1,5},{2,6},{3,7},{4,0},{5,1},{6,2},{7,3},{8,12},{9,13},{10,... | collective-permute-start | bytes 393224 | tf_op jit(solution)/shard_map/cond/branch_1_fun/ppermute | solution.py:282
  108.7 11.8 %collective-permute-start.44 = (f32[2,128,128]{2,1,0:T(8,128)S(1)}, f32[2,128,128]{2,1,0:T(8,128)S(1)}, u32[]{:S(2)}, u32[]{:S(2)}) collective-permute-start(f32[2,128,128]{2,1,0:T(8,128)S(1)} %get-tuple-element.186), channel_id=1, source_target_pairs={{0,8},{1,9},{2,10},{3,11},{4,12},{5,13},{6,14},{7,15},{8,0},{9,1},... | collective-permute-start | bytes 393224 | tf_op jit(solution)/shard_map/cond/branch_1_fun/ppermute | solution.py:282
  114.3 6.0 %collective-permute-start.37 = (f32[2,128,128]{2,1,0:T(8,128)S(1)}, f32[2,128,128]{2,1,0:T(8,128)S(1)}, u32[]{:S(2)}, u32[]{:S(2)}) collective-permute-start(f32[2,128,128]{2,1,0:T(8,128)S(1)} %broadcast_select_fusion.42), channel_id=1, source_target_pairs={{0,4},{1,5},{2,6},{3,7},{4,0},{5,1},{6,2},{7,3},{8,12},{9,13},{10,... | collective-permute-start | bytes 393224 | tf_op jit(solution)/shard_map/cond/branch_1_fun/ppermute | solution.py:282
  114.4 6.0 %collective-permute-start.36 = (f32[2,128,128]{2,1,0:T(8,128)S(1)}, f32[2,128,128]{2,1,0:T(8,128)S(1)}, u32[]{:S(2)}, u32[]{:S(2)}) collective-permute-start(f32[2,128,128]{2,1,0:T(8,128)S(1)} %broadcast_select_fusion.33), channel_id=1, source_target_pairs={{0,1},{1,0},{2,3},{3,2},{4,5},{5,4},{6,7},{7,6},{8,9},{9,8},{10,11... | collective-permute-start | bytes 393224 | tf_op jit(solution)/shard_map/cond/branch_1_fun/ppermute | solution.py:282
  120.4 5.2 %collective-permute-start.40 = (f32[2,128,128]{2,1,0:T(8,128)S(1)}, f32[2,128,128]{2,1,0:T(8,128)S(1)}, u32[]{:S(2)}, u32[]{:S(2)}) collective-permute-start(f32[2,128,128]{2,1,0:T(8,128)S(1)} %broadcast_select_fusion.41), channel_id=1, source_target_pairs={{0,4},{1,5},{2,6},{3,7},{4,0},{5,1},{6,2},{7,3},{8,12},{9,13},{10,... | collective-permute-start | bytes 393224 | tf_op jit(solution)/shard_map/cond/branch_1_fun/ppermute | solution.py:282
  120.5 5.1 %collective-permute-start.39 = (f32[2,128,128]{2,1,0:T(8,128)S(1)}, f32[2,128,128]{2,1,0:T(8,128)S(1)}, u32[]{:S(2)}, u32[]{:S(2)}) collective-permute-start(f32[2,128,128]{2,1,0:T(8,128)S(1)} %broadcast_select_fusion.32), channel_id=1, source_target_pairs={{0,1},{1,0},{2,3},{3,2},{4,5},{5,4},{6,7},{7,6},{8,9},{9,8},{10,11... | collective-permute-start | bytes 393224 | tf_op jit(solution)/shard_map/cond/branch_1_fun/ppermute | solution.py:282
  125.7 5.0 %collective-permute-start.43 = (f32[2,128,128]{2,1,0:T(8,128)S(1)}, f32[2,128,128]{2,1,0:T(8,128)S(1)}, u32[]{:S(2)}, u32[]{:S(2)}) collective-permute-start(f32[2,128,128]{2,1,0:T(8,128)S(1)} %broadcast_select_fusion.40), channel_id=1, source_target_pairs={{0,4},{1,5},{2,6},{3,7},{4,0},{5,1},{6,2},{7,3},{8,12},{9,13},{10,... | collective-permute-start | bytes 393224 | tf_op jit(solution)/shard_map/cond/branch_1_fun/ppermute | solution.py:282
  127.3 3.4 %collective-permute-start.42 = (f32[2,128,128]{2,1,0:T(8,128)S(1)}, f32[2,128,128]{2,1,0:T(8,128)S(1)}, u32[]{:S(2)}, u32[]{:S(2)}) collective-permute-start(f32[2,128,128]{2,1,0:T(8,128)S(1)} %broadcast_select_fusion.31), channel_id=1, source_target_pairs={{0,1},{1,0},{2,3},{3,2},{4,5},{5,4},{6,7},{7,6},{8,9},{9,8},{10,11... | collective-permute-start | bytes 393224 | tf_op jit(solution)/shard_map/cond/branch_1_fun/ppermute | solution.py:282
  130.7 5.0 %collective-permute-start.46 = (f32[2,128,128]{2,1,0:T(8,128)S(1)}, f32[2,128,128]{2,1,0:T(8,128)S(1)}, u32[]{:S(2)}, u32[]{:S(2)}) collective-permute-start(f32[2,128,128]{2,1,0:T(8,128)S(1)} %broadcast_select_fusion.39), channel_id=1, source_target_pairs={{0,4},{1,5},{2,6},{3,7},{4,0},{5,1},{6,2},{7,3},{8,12},{9,13},{10,... | collective-permute-start | bytes 393224 | tf_op jit(solution)/shard_map/cond/branch_1_fun/ppermute | solution.py:282
  132.4 3.4 %collective-permute-start.45 = (f32[2,128,128]{2,1,0:T(8,128)S(1)}, f32[2,128,128]{2,1,0:T(8,128)S(1)}, u32[]{:S(2)}, u32[]{:S(2)}) collective-permute-start(f32[2,128,128]{2,1,0:T(8,128)S(1)} %broadcast_select_fusion.30), channel_id=1, source_target_pairs={{0,1},{1,0},{2,3},{3,2},{4,5},{5,4},{6,7},{7,6},{8,9},{9,8},{10,11... | collective-permute-start | bytes 393224 | tf_op jit(solution)/shard_map/cond/branch_1_fun/ppermute | solution.py:282
  135.8 5.0 %collective-permute-start.47 = (f32[2,128,128]{2,1,0:T(8,128)S(1)}, f32[2,128,128]{2,1,0:T(8,128)S(1)}, u32[]{:S(2)}, u32[]{:S(2)}) collective-permute-start(f32[2,128,128]{2,1,0:T(8,128)S(1)} %broadcast_select_fusion.38), channel_id=1, source_target_pairs={{0,4},{1,5},{2,6},{3,7},{4,0},{5,1},{6,2},{7,3},{8,12},{9,13},{10,... | collective-permute-start | bytes 393224 | tf_op jit(solution)/shard_map/cond/branch_1_fun/ppermute | solution.py:282
  (11 other events, 29.7 us)
Sparse Core Ops, SparseCore 0:
  13.7 41.3 all-gather.2

commit v2 on v0

--- a/solution.py
+++ b/solution.py
@@ -1,5 +1,5 @@
 from functools import partial
-from itertools import permutations
+from itertools import combinations
 
 import jax
 import jax.numpy as jnp
@@ -32,22 +32,29 @@
     return jnp.maximum(v, 0.0), jnp.minimum(v, 0.0)
 
 
-def prepare_kernel(bits, here_ref, neighbours_ref, migrate_ref, order_ref, rates_ref, u_ref, k_ref, plan_ref, own_ref, sent_ref):
+def prepare_kernel(top, here_ref, neighbours_ref, migrate_ref, order_ref, rates_ref, u_ref, k_ref, plan_ref, own_ref, sent_ref):
     here = here_ref[0]
     for side in range(2):
         beside = neighbours_ref[here, side]
         plan_ref[side] = jnp.maximum(beside, 0)
         plan_ref[2 + side] = (beside >= 0).astype(jnp.int32)
-    top = bits - 1
     order = [order_ref[r] for r in range(ROUNDS)]
-    place = jnp.where(order[0] == top, 0, jnp.where(order[1] == top, 1, 2))
-    first = jnp.where(place == 0, order[1], order[0])
-    second = jnp.where(place == 2, order[1], order[2])
-    second = jnp.where(second > first, second - 1, second)
-    plan_ref[4] = (place * top + first) * (top - 1) + second
-    for r in range(ROUNDS):
-        partner = jnp.bitwise_xor(here, jnp.left_shift(jnp.int32(1), order[r]))
-        plan_ref[5 + r] = ((migrate_ref[r, here] + migrate_ref[r, partner]) > 0).astype(jnp.int32)
+    low = jnp.minimum(jnp.minimum(order[0], order[1]), order[2])
+    high = order[0] + order[1] + order[2] - top - low
+    plan_ref[4] = ((low * (2 * top - 1 - low)) >> 1) + high - low - 1
+
+    def source(slot):
+        for r in reversed(range(ROUNDS)):
+            partner = jnp.bitwise_xor(slot, jnp.left_shift(jnp.int32(1), order[r]))
+            slot = jnp.where(migrate_ref[r, slot] + migrate_ref[r, partner] > 0, partner, slot)
+        return slot
+
+    def candidate(slot):
+        apart = jnp.bitwise_xor(source(slot), here)
+        return ((apart >> top) & 1) + 2 * ((apart >> low) & 1), (apart >> high) & 1
+
+    plan_ref[5], _ = candidate(jnp.bitwise_xor(here, jnp.left_shift(jnp.int32(1), high)))
+    plan_ref[6], plan_ref[7] = candidate(here)
     depth = k_ref.shape[0]
     wide = lax.broadcasted_iota(jnp.int32, (LANES, LANES), 1)
     for a in range(3):
@@ -282,60 +289,22 @@
     return lax.ppermute(block, AXES, [(low, low ^ 1 << bit) for low in range(count)])
 
 
-def route(field, moved, bits, sizes):
-    out = []
-    start = 0
-    for size in sizes:
-        part = field[start : start + size]
-        for r, bit in enumerate(bits):
-            part = jnp.where(moved[r] > 0, swap(part, bit), part)
-        out.append(part)
-        start += size
-    return jnp.concatenate(out, axis=0)
-
-
-def per_device(concentration, diffusivity, rates, velocity, neighbours, migrate, bit_order):
-    devices = lax.axis_size(AXES)
-    bits = devices.bit_length() - 1
-    _, species, depth, height, width = concentration.shape
-    field = concentration[0]
-    kappa = diffusivity[0]
-    here = lax.axis_index(AXES).astype(jnp.int32).reshape(1)
+def pick(index, options):
+    picked = options[0]
+    for number in range(1, 4):
+        picked = jnp.where(index == number, options[number], picked)
+    return picked
+
+
+def after(value, earlier):
+    return lax.optimization_barrier((value, earlier))
+
+
+def edge_call(plan, velocity, rates, gathered, own, tiles):
     f32 = jnp.float32
-    tiles = 3 * depth + 2
-    plan, own, sent = pl.pallas_call(
-        partial(prepare_kernel, bits),
-        out_shape=(
-            jax.ShapeDtypeStruct((8,), jnp.int32),
-            jax.ShapeDtypeStruct((3, depth, 16, LANES), f32),
-            jax.ShapeDtypeStruct((tiles, ROWS, LANES), f32),
-        ),
-        in_specs=[SMEM] * 5 + [VMEM] * 2,
-        out_specs=(SMEM, VMEM, VMEM),
-        compiler_params=PARAMS,
-        name="prepare",
-    )(here, neighbours, migrate, bit_order, rates, field, kappa)
-    gathered = lax.all_gather(sent, AXES, axis=0, tiled=False)
-    padded = height + 2 * ROWS
-    inner = pl.pallas_call(
-        interior_kernel,
-        out_shape=jax.ShapeDtypeStruct(field.shape, f32),
-        in_specs=[SMEM] * 2 + [VMEM] * 2,
-        out_specs=VMEM,
-        scratch_shapes=[
-            pltpu.VMEM((2, species, depth, padded, width), f32),
-            pltpu.VMEM((depth, padded, width), f32),
-            pltpu.VMEM((depth, height, width), f32),
-            pltpu.VMEM((depth, height, width), f32),
-            pltpu.VMEM((depth, padded, width), f32),
-            pltpu.VMEM((depth, height, width), f32),
-            pltpu.VMEM((species, depth, height, width), f32),
-        ],
-        compiler_params=PARAMS,
-        cost_estimate=pl.CostEstimate(flops=40_000_000, bytes_accessed=10_000_000, transcendentals=0),
-        name="interior",
-    )(velocity, rates, field, kappa)
-    edges = pl.pallas_call(
+    species = 2
+    depth = own.shape[1]
+    return pl.pallas_call(
         edge_kernel,
         out_shape=jax.ShapeDtypeStruct((species, depth, ROWS, LANES), f32),
         grid_spec=pltpu.PrefetchScalarGridSpec(
@@ -362,26 +331,107 @@
         compiler_params=PARAMS,
         name="edges",
     )(plan, velocity, rates, gathered, gathered, own)
-    whole = pl.pallas_call(
+
+
+def spans(total):
+    sizes = (5, 5, 4, 2) if total == 16 else (total,)
+    return [(sum(sizes[:n]), sum(sizes[: n + 1])) for n in range(len(sizes))]
+
+
+def run(low, high, top, field, kappa, rates, velocity, plan, own, sent):
+    species, depth, height, width = field.shape
+    f32 = jnp.float32
+    tiles = sent.shape[0]
+    gathered = lax.all_gather(sent, AXES, axis=0, tiled=False)
+    padded = height + 2 * ROWS
+    inner = pl.pallas_call(
+        interior_kernel,
+        out_shape=jax.ShapeDtypeStruct(field.shape, f32),
+        in_specs=[SMEM] * 2 + [VMEM] * 2,
+        out_specs=VMEM,
+        scratch_shapes=[
+            pltpu.VMEM((2, species, depth, padded, width), f32),
+            pltpu.VMEM((depth, padded, width), f32),
+            pltpu.VMEM((depth, height, width), f32),
+            pltpu.VMEM((depth, height, width), f32),
+            pltpu.VMEM((depth, padded, width), f32),
+            pltpu.VMEM((depth, height, width), f32),
+            pltpu.VMEM((species, depth, height, width), f32),
+        ],
+        compiler_params=PARAMS,
+        cost_estimate=pl.CostEstimate(flops=40_000_000, bytes_accessed=10_000_000, transcendentals=0),
+        name="interior",
+    )(velocity, rates, field, kappa)
+    planes = inner.reshape(species * depth, height, width)
+    cuts = spans(species * depth)
+    last = len(cuts) - 1
+    across = swap(planes, low)
+    near = []
+    far = []
+    sent_on = []
+    out = []
+
+    def start_near(n):
+        part = planes[cuts[n][0] : cuts[n][1]]
+        if n >= 2:
+            part, near[n - 2] = after(part, near[n - 2])
+        if n >= 3:
+            part, far[n - 3] = after(part, far[n - 3])
+        near.append(swap(part, top))
+
+    for n in range(min(2, last + 1)):
+        start_near(n)
+    for n, (start, stop) in enumerate(cuts):
+        part = near[n]
+        if n == last:
+            own, part = after(own, part) if n == 0 else (own, part)
+            if n > 0:
+                own, near[n - 1] = after(own, near[n - 1])
+            edges = edge_call(plan, velocity, rates, gathered, own, tiles)
+            part, edges = after(part, edges)
+        if n >= 2:
+            part, sent_on[n - 2] = after(part, sent_on[n - 2])
+        far.append(swap(part, low))
+        if n + 2 <= last:
+            start_near(n + 2)
+        options = (planes[start:stop], near[n], across[start:stop], far[n])
+        sent_on.append(swap(pick(plan[5], options), high))
+        out.append(jnp.where(plan[7] > 0, sent_on[n], pick(plan[6], options)))
+    rim_near = swap(edges, top)
+    options = (edges, rim_near, swap(edges, low), swap(rim_near, low))
+    other = swap(pick(plan[5], options), high)
+    rim = jnp.where(plan[7] > 0, other, pick(plan[6], options))
+    final = jnp.concatenate(out, axis=0).reshape(field.shape)
+    return pl.pallas_call(
         merge_kernel,
         out_shape=jax.ShapeDtypeStruct(field.shape, f32),
         in_specs=[VMEM] * 2,
         out_specs=VMEM,
         compiler_params=PARAMS,
         name="merge",
-    )(inner, edges)
-    planes = whole.reshape(species * depth, height, width)
-    top = bits - 1
-    branches = []
-    for place in range(ROUNDS):
-        for others in permutations(range(top), 2):
-            order = list(others)
-            order.insert(place, top)
-            sizes = [(4, 4, 4, 4), (2, 4, 4, 4, 2), (2, 4, 5, 5)][place] if devices <= 16 else (species * depth,)
-            if place == 0 and devices <= 16:
-                sizes = (5, 5, 4, 2)
-            branches.append(partial(route, bits=order, sizes=sizes))
-    final = lax.switch(plan[4], branches, planes, plan[5:8])
+    )(final, rim)
+
+
+def per_device(concentration, diffusivity, rates, velocity, neighbours, migrate, bit_order):
+    top = lax.axis_size(AXES).bit_length() - 2
+    field = concentration[0]
+    kappa = diffusivity[0]
+    depth = kappa.shape[0]
+    here = lax.axis_index(AXES).astype(jnp.int32).reshape(1)
+    plan, own, sent = pl.pallas_call(
+        partial(prepare_kernel, top),
+        out_shape=(
+            jax.ShapeDtypeStruct((8,), jnp.int32),
+            jax.ShapeDtypeStruct((3, depth, 16, LANES), jnp.float32),
+            jax.ShapeDtypeStruct((3 * depth + 2, ROWS, LANES), jnp.float32),
+        ),
+        in_specs=[SMEM] * 5 + [VMEM] * 2,
+        out_specs=(SMEM, VMEM, VMEM),
+        compiler_params=PARAMS,
+        name="prepare",
+    )(here, neighbours, migrate, bit_order, rates, field, kappa)
+    branches = [partial(run, low, high, top) for low, high in combinations(range(top), 2)]
+    final = lax.switch(plan[4], branches, field, kappa, rates, velocity, plan, own, sent)
     return final.reshape(concentration.shape)
 
 

time: 147 us -> 135 us (0.918)
  the two profiles are of different devices: /device:TPU:4 before, /device:TPU:0 now
where the time goes in v2:
time: 135 us
  waiting for transfers between devices  61.6 us (46%)
  starting transfers between devices  24.1 us (18%)
  Pallas kernels  20 us (15%)
  between operations  14.1 us (10%)
  local copies, waits for them, and re-layouts  7.19 us (5%)
  loops' own time  4.82 us (4%)
  other arithmetic  3.04 us (2%)
    ppermute x17, waiting for transfers between devices, swap(): lax.ppermute(block, AXES, [(low, low ^ 1 << bit) for low in range(count)])  61 us
    ppermute x17, starting transfers between devices, swap(): lax.ppermute(block, AXES, [(low, low ^ 1 << bit) for low in range(count)])  24 us
    pallas_call x1, Pallas kernels, run(): pl.pallas_call(interior_kernel, out_shape=jax.ShapeDtypeStruct(field.shap...  11 us
    pallas_call x1, Pallas kernels, edge_call(): pl.pallas_call(edge_kernel, out_shape=jax.ShapeDtypeStruct((species, dept...  5.87 us
    another operation x1, loops' own time, per_device(): lax.switch(plan[4], branches, field, kappa, rates, velocity, plan, own, s...  4.82 us
    unnamed x7, local copies, waits for them, and re-layouts  3.06 us
  transfers between devices with their start and end apart: 18, of which 11 were waited for; matrix products, arithmetic and copies ran while one was open for 3% of the time, Pallas kernels for 13%

profile of v2, /device:TPU:0, one launch (start us, length us, event | category | flops | bytes accessed | tf_op | source)
XLA Modules:
  0.0 134.8 jit_solution(15529341115254435390)
XLA Ops:
  8.6 2.6 %prepare.1 = (s32[8]{0:T(128)S(1)}, f32[3,8,16,128]{3,2,1,0:T(8,128)S(1)}, f32[26,8,128]{2,1,0:T(8,128)}) custom-call(s32[1]{0:T(128)} %bitcast.33.here_ref, s32[16,2]{1,0:T(8,128)S(1)} %copy.12.neighbours_ref, s32[3,16]{1,0:T(4,128)S(1)} %copy-done.3, s32[3]{0:T(128)S(1)} %copy-done.4, f32[1,2]{1,0:T(1,128)} %rates_ref.1, f32[2,8,128,128]{3,2,1,0:T(8,128)} %bitcast.76, ...), custom_call_target="tpu_custom_call" | custom-call | tf_op jit(solution)/shard_map/prepare/pallas_call | solution.py:421
  12.5 114.4 %conditional.1 = (f32[1,2,8,128,128]{4,3,2,1,0:T(8,128)S(1)}) conditional(s32[]{:T(128)} %bitcast.36, (s32[8]{0:T(128)S(1)}, f32[2,3]{1,0:T(2,128)}, f32[1,2]{1,0:T(1,128)}, f32[2,8,128,128]{3,2,1,0:T(8,128)}, f32[8,128,128]{2,1,0:T(8,128)}, /*index=5*/f32[26,8,128]{2,1,0:T(8,128)}, f32[3,8,16,128]{3,2,1,0:T(8,128)S(1)}) %tuple.69, ...), branch_computations={%region_0.1_spmd, %region_1.2_spmd, %region_2.3_spmd} | conditional | flops 42736128 | bytes 61242128 | solution.py:434
  13.3 11.0 %interior.5 = f32[2,8,128,128]{3,2,1,0:T(8,128)S(1)} custom-call(f32[2,3]{1,0:T(2,128)} %get-tuple-element.87.velocity_ref, f32[1,2]{1,0:T(1,128)} %get-tuple-element.88.rates_ref, f32[2,8,128,128]{3,2,1,0:T(8,128)} %get-tuple-element.89.u_ref, f32[8,128,128]{2,1,0:T(8,128)} %get-tuple-element.90.k_ref), custom_call_target="tpu_custom_call" | custom-call | flops 40000000 | bytes 10000000 | tf_op jit(solution)/shard_map/cond/branch_2_fun/interior/pallas_call | solution.py:347
  24.3 3.0 %collective-permute-start.36 = (f32[16,128,128]{2,1,0:T(8,128)S(1)}, f32[16,128,128]{2,1,0:T(8,128)S(1)}, u32[]{:S(2)}, u32[]{:S(2)}) collective-permute-start(f32[16,128,128]{2,1,0:T(8,128)S(1)} %bitcast.57), channel_id=1, source_target_pairs={{0,2},{1,3},{2,0},{3,1},{4,6},{5,7},{6,4},{7,5},{8,10},{9,11},{10,... | collective-permute-start | bytes 3145736 | tf_op jit(solution)/shard_map/cond/branch_2_fun/ppermute | solution.py:289
  27.4 2.7 %collective-permute-start.34 = (f32[5,128,128]{2,1,0:T(8,128)S(1)}, f32[5,128,128]{2,1,0:T(8,128)S(1)}, u32[]{:S(2)}, u32[]{:S(2)}) collective-permute-start(f32[5,128,128]{2,1,0:T(8,128)S(1)} %get-tuple-element.132), channel_id=1, source_target_pairs={{0,8},{1,9},{2,10},{3,11},{4,12},{5,13},{6,14},{7,15},{8,0},{9,1},... | collective-permute-start | bytes 983048 | tf_op jit(solution)/shard_map/cond/branch_2_fun/ppermute | solution.py:289
  30.4 24.8 %collective-permute-done.34 = f32[5,128,128]{2,1,0:T(8,128)S(1)} collective-permute-done((f32[5,128,128]{2,1,0:T(8,128)S(1)}, f32[5,128,128]{2,1,0:T(8,128)S(1)}, u32[]{:S(2)}, u32[]{:S(2)}) %collective-permute-start.34) | collective-permute-done | bytes 327712 | tf_op jit(solution)/shard_map/cond/branch_2_fun/ppermute | solution.py:289
  56.1 8.8 %collective-permute-done.38 = f32[5,128,128]{2,1,0:T(8,128)S(1)} collective-permute-done((f32[5,128,128]{2,1,0:T(8,128)S(1)}, f32[5,128,128]{2,1,0:T(8,128)S(1)}, u32[]{:S(2)}, u32[]{:S(2)}) %collective-permute-start.38) | collective-permute-done | bytes 327712 | tf_op jit(solution)/shard_map/cond/branch_2_fun/ppermute | solution.py:289
  69.5 5.8 %collective-permute-done.39 = f32[5,128,128]{2,1,0:T(8,128)S(1)} collective-permute-done((f32[5,128,128]{2,1,0:T(8,128)S(1)}, f32[5,128,128]{2,1,0:T(8,128)S(1)}, u32[]{:S(2)}, u32[]{:S(2)}) %collective-permute-start.39) | collective-permute-done | bytes 327712 | tf_op jit(solution)/shard_map/cond/branch_2_fun/ppermute | solution.py:289
  76.6 3.4 %collective-permute-start.41 = (f32[4,128,128]{2,1,0:T(8,128)S(1)}, f32[4,128,128]{2,1,0:T(8,128)S(1)}, u32[]{:S(2)}, u32[]{:S(2)}) collective-permute-start(f32[4,128,128]{2,1,0:T(8,128)S(1)} %slice.169), channel_id=1, source_target_pairs={{0,8},{1,9},{2,10},{3,11},{4,12},{5,13},{6,14},{7,15},{8,0},{9,1},... | collective-permute-start | bytes 786440 | tf_op jit(solution)/shard_map/cond/branch_2_fun/ppermute | solution.py:289
  80.0 8.7 %collective-permute-done.41 = f32[4,128,128]{2,1,0:T(8,128)S(1)} collective-permute-done((f32[4,128,128]{2,1,0:T(8,128)S(1)}, f32[4,128,128]{2,1,0:T(8,128)S(1)}, u32[]{:S(2)}, u32[]{:S(2)}) %collective-permute-start.41) | collective-permute-done | bytes 262176 | tf_op jit(solution)/shard_map/cond/branch_2_fun/ppermute | solution.py:289
  88.7 1.9 %collective-permute-done.37 = f32[5,128,128]{2,1,0:T(8,128)} collective-permute-done((f32[5,128,128]{2,1,0:T(8,128)S(1)}, f32[5,128,128]{2,1,0:T(8,128)}, u32[]{:S(2)}, u32[]{:S(2)}) %collective-permute-start.37) | collective-permute-done | bytes 327712 | tf_op jit(solution)/shard_map/cond/branch_2_fun/ppermute | solution.py:289
  91.5 1.9 %collective-permute-start.40 = (f32[5,128,128]{2,1,0:T(8,128)}, f32[5,128,128]{2,1,0:T(8,128)}, u32[]{:S(2)}, u32[]{:S(2)}) collective-permute-start(f32[5,128,128]{2,1,0:T(8,128)} %get-tuple-element.131), channel_id=1, source_target_pairs={{0,4},{1,5},{2,6},{3,7},{4,0},{5,1},{6,2},{7,3},{8,12},{9,13},{10,... | collective-permute-start | bytes 983048 | tf_op jit(solution)/shard_map/cond/branch_2_fun/ppermute | solution.py:289
  96.1 1.9 %collective-permute-start.44 = (f32[2,128,128]{2,1,0:T(8,128)}, f32[2,128,128]{2,1,0:T(8,128)}, u32[]{:S(2)}, u32[]{:S(2)}) collective-permute-start(f32[2,128,128]{2,1,0:T(8,128)} %slice.172), channel_id=1, source_target_pairs={{0,8},{1,9},{2,10},{3,11},{4,12},{5,13},{6,14},{7,15},{8,0},{9,1},... | collective-permute-start | bytes 393224 | tf_op jit(solution)/shard_map/cond/branch_2_fun/ppermute | solution.py:289
  99.5 1.5 %collective-permute-start.43 = (f32[4,128,128]{2,1,0:T(8,128)}, f32[4,128,128]{2,1,0:T(8,128)}, u32[]{:S(2)}, u32[]{:S(2)}) collective-permute-start(f32[4,128,128]{2,1,0:T(8,128)} %select_select_fusion.25), channel_id=1, source_target_pairs={{0,4},{1,5},{2,6},{3,7},{4,0},{5,1},{6,2},{7,3},{8,12},{9,13},{10,... | collective-permute-start | bytes 786440 | tf_op jit(solution)/shard_map/cond/branch_2_fun/ppermute | solution.py:289
  101.0 1.4 %copy-done.2 = f32[416,8,128]{2,1,0:T(8,128)S(1)} copy-done((f32[416,8,128]{2,1,0:T(8,128)S(1)}, f32[416,8,128]{2,1,0:T(8,128)}, u32[]{:S(2)}) %copy-start.2) | copy-done | bytes 1703960 | tf_op jit(solution)/shard_map/cond
  102.5 5.9 %edges.5 = f32[2,8,8,128]{3,2,1,0:T(8,128)S(1)} custom-call(s32[8]{0:T(128)S(1)} %get-tuple-element.86.plan_ref, f32[2,3]{1,0:T(2,128)S(1)} %copy-done.20, f32[1,2]{1,0:T(1,128)S(1)} %copy-done.23, f32[16,26,8,128]{3,2,1,0:T(8,128)S(1)} %bitcast.71, f32[16,26,8,128]{3,2,1,0:T(8,128)S(1)} %bitcast.72, f32[3,8,16,128]{3,2,1,0:T(8,128)S(1)} %get-tuple-element.99.own_ref), custom_call_target="tpu_custom_call" | custom-call | tf_op jit(solution)/shard_map/cond/branch_2_fun/edges/pallas_call | solution.py:307
  108.4 2.0 %collective-permute-start.47 = (f32[2,8,8,128]{3,2,1,0:T(8,128)S(1)}, f32[2,8,8,128]{3,2,1,0:T(8,128)S(1)}, u32[]{:S(2)}, u32[]{:S(2)}) collective-permute-start(f32[2,8,8,128]{3,2,1,0:T(8,128)S(1)} %edges.5), channel_id=1, source_target_pairs={{0,8},{1,9},{2,10},{3,11},{4,12},{5,13},{6,14},{7,15},{8,0},{9,1},... | collective-permute-start | bytes 196616 | tf_op jit(solution)/shard_map/cond/branch_2_fun/ppermute | solution.py:289
  111.2 3.1 %collective-permute-done.47 = f32[2,8,8,128]{3,2,1,0:T(8,128)S(1)} collective-permute-done((f32[2,8,8,128]{3,2,1,0:T(8,128)S(1)}, f32[2,8,8,128]{3,2,1,0:T(8,128)S(1)}, u32[]{:S(2)}, u32[]{:S(2)}) %collective-permute-start.47) | collective-permute-done | bytes 65568 | tf_op jit(solution)/shard_map/cond/branch_2_fun/ppermute | solution.py:289
  115.2 1.2 collective-permute-start.45
  116.4 2.1 %collective-permute-done.48 = f32[2,8,8,128]{3,2,1,0:T(8,128)S(1)} collective-permute-done((f32[2,8,8,128]{3,2,1,0:T(8,128)S(1)}, f32[2,8,8,128]{3,2,1,0:T(8,128)S(1)}, u32[]{:S(2)}, u32[]{:S(2)}) %collective-permute-start.48) | collective-permute-done | bytes 65568 | tf_op jit(solution)/shard_map/cond/branch_2_fun/ppermute | solution.py:289
  118.6 1.8 %collective-permute-done.45 = f32[2,128,128]{2,1,0:T(8,128)S(1)} collective-permute-done((f32[2,128,128]{2,1,0:T(8,128)}, f32[2,128,128]{2,1,0:T(8,128)S(1)}, u32[]{:S(2)}, u32[]{:S(2)}) %collective-permute-start.45) | collective-permute-done | bytes 131104 | tf_op jit(solution)/shard_map/cond/branch_2_fun/ppermute | solution.py:289
  120.5 1.4 %collective-permute-start.46 = (f32[2,128,128]{2,1,0:T(8,128)S(1)}, f32[2,128,128]{2,1,0:T(8,128)S(1)}, u32[]{:S(2)}, u32[]{:S(2)}) collective-permute-start(f32[2,128,128]{2,1,0:T(8,128)S(1)} %select_select_fusion.27), channel_id=1, source_target_pairs={{0,4},{1,5},{2,6},{3,7},{4,0},{5,1},{6,2},{7,3},{8,12},{9,13},{10,... | collective-permute-start | bytes 393224 | tf_op jit(solution)/shard_map/cond/branch_2_fun/ppermute | solution.py:289
  121.9 1.0 collective-permute-done.50
  122.9 2.6 %collective-permute-done.46 = f32[2,128,128]{2,1,0:T(8,128)S(1)} collective-permute-done((f32[2,128,128]{2,1,0:T(8,128)S(1)}, f32[2,128,128]{2,1,0:T(8,128)S(1)}, u32[]{:S(2)}, u32[]{:S(2)}) %collective-permute-start.46) | collective-permute-done | bytes 131104 | tf_op jit(solution)/shard_map/cond/branch_2_fun/ppermute | solution.py:289
  (53 shorter events, 15.4 us)
Async XLA Ops:
  12.5 88.5 %all-gather.11.cloned.1.call-start = ((), (), s32[]{:S(2)}) async-start(), calls=%async_computation.2 | async-start | bytes 1810432 | tf_op jit(solution)/shard_map/cond/branch_2_fun/all_gather | solution.py:345
  24.3 51.1 %collective-permute-start.36 = (f32[16,128,128]{2,1,0:T(8,128)S(1)}, f32[16,128,128]{2,1,0:T(8,128)S(1)}, u32[]{:S(2)}, u32[]{:S(2)}) collective-permute-start(f32[16,128,128]{2,1,0:T(8,128)S(1)} %bitcast.57), channel_id=1, source_target_pairs={{0,2},{1,3},{2,0},{3,1},{4,6},{5,7},{6,4},{7,5},{8,10},{9,11},{10,... | collective-permute-start | bytes 3145736 | tf_op jit(solution)/shard_map/cond/branch_2_fun/ppermute | solution.py:289
  27.4 27.8 %collective-permute-start.34 = (f32[5,128,128]{2,1,0:T(8,128)S(1)}, f32[5,128,128]{2,1,0:T(8,128)S(1)}, u32[]{:S(2)}, u32[]{:S(2)}) collective-permute-start(f32[5,128,128]{2,1,0:T(8,128)S(1)} %get-tuple-element.132), channel_id=1, source_target_pairs={{0,8},{1,9},{2,10},{3,11},{4,12},{5,13},{6,14},{7,15},{8,0},{9,1},... | collective-permute-start | bytes 983048 | tf_op jit(solution)/shard_map/cond/branch_2_fun/ppermute | solution.py:289
  30.0 34.9 %collective-permute-start.38 = (f32[5,128,128]{2,1,0:T(8,128)S(1)}, f32[5,128,128]{2,1,0:T(8,128)S(1)}, u32[]{:S(2)}, u32[]{:S(2)}) collective-permute-start(f32[5,128,128]{2,1,0:T(8,128)S(1)} %get-tuple-element.133), channel_id=1, source_target_pairs={{0,8},{1,9},{2,10},{3,11},{4,12},{5,13},{6,14},{7,15},{8,0},{9,1},... | collective-permute-start | bytes 983048 | tf_op jit(solution)/shard_map/cond/branch_2_fun/ppermute | solution.py:289
  55.2 14.4 %collective-permute-start.35 = (f32[5,128,128]{2,1,0:T(8,128)S(1)}, f32[5,128,128]{2,1,0:T(8,128)S(1)}, u32[]{:S(2)}, u32[]{:S(2)}) collective-permute-start(f32[5,128,128]{2,1,0:T(8,128)S(1)} %collective-permute-done.34), channel_id=1, source_target_pairs={{0,2},{1,3},{2,0},{3,1},{4,6},{5,7},{6,4},{7,5},{8,10},{9,11},{10,... | collective-permute-start | bytes 983048 | tf_op jit(solution)/shard_map/cond/branch_2_fun/ppermute | solution.py:289
  64.9 10.5 %collective-permute-start.39 = (f32[5,128,128]{2,1,0:T(8,128)S(1)}, f32[5,128,128]{2,1,0:T(8,128)S(1)}, u32[]{:S(2)}, u32[]{:S(2)}) collective-permute-start(f32[5,128,128]{2,1,0:T(8,128)S(1)} %collective-permute-done.38), channel_id=1, source_target_pairs={{0,2},{1,3},{2,0},{3,1},{4,6},{5,7},{6,4},{7,5},{8,10},{9,11},{10,... | collective-permute-start | bytes 983048 | tf_op jit(solution)/shard_map/cond/branch_2_fun/ppermute | solution.py:289
  75.4 24.1 %copy-start.9 = (f32[5,128,128]{2,1,0:T(8,128)}, f32[5,128,128]{2,1,0:T(8,128)S(1)}, u32[]{:S(2)}) copy-start(f32[5,128,128]{2,1,0:T(8,128)S(1)} %collective-permute-done.39) | copy-start | bytes 983044 | tf_op jit(solution)/shard_map/cond
  75.4 25.6 %copy-start.20 = (f32[2,3]{1,0:T(2,128)S(1)}, f32[2,3]{1,0:T(2,128)}, u32[]{:S(2)}) copy-start(f32[2,3]{1,0:T(2,128)} %get-tuple-element.87.velocity_ref) | copy-start | bytes 76 | tf_op jit(solution)/shard_map/cond
  75.4 25.6 %copy-start.23 = (f32[1,2]{1,0:T(1,128)S(1)}, f32[1,2]{1,0:T(1,128)}, u32[]{:S(2)}) copy-start(f32[1,2]{1,0:T(1,128)} %get-tuple-element.88.rates_ref) | copy-start | bytes 28 | tf_op jit(solution)/shard_map/cond
  76.3 14.3 %collective-permute-start.37 = (f32[5,128,128]{2,1,0:T(8,128)S(1)}, f32[5,128,128]{2,1,0:T(8,128)}, u32[]{:S(2)}, u32[]{:S(2)}) collective-permute-start(f32[5,128,128]{2,1,0:T(8,128)S(1)} %get-tuple-element.130), channel_id=1, source_target_pairs={{0,4},{1,5},{2,6},{3,7},{4,0},{5,1},{6,2},{7,3},{8,12},{9,13},{10,... | collective-permute-start | bytes 983048 | tf_op jit(solution)/shard_map/cond/branch_2_fun/ppermute | solution.py:289
  76.6 12.1 %collective-permute-start.41 = (f32[4,128,128]{2,1,0:T(8,128)S(1)}, f32[4,128,128]{2,1,0:T(8,128)S(1)}, u32[]{:S(2)}, u32[]{:S(2)}) collective-permute-start(f32[4,128,128]{2,1,0:T(8,128)S(1)} %slice.169), channel_id=1, source_target_pairs={{0,8},{1,9},{2,10},{3,11},{4,12},{5,13},{6,14},{7,15},{8,0},{9,1},... | collective-permute-start | bytes 786440 | tf_op jit(solution)/shard_map/cond/branch_2_fun/ppermute | solution.py:289
  90.5 7.5 %collective-permute-start.42 = (f32[4,128,128]{2,1,0:T(8,128)S(1)}, f32[4,128,128]{2,1,0:T(8,128)S(1)}, u32[]{:S(2)}, u32[]{:S(2)}) collective-permute-start(f32[4,128,128]{2,1,0:T(8,128)S(1)} %collective-permute-done.41), channel_id=1, source_target_pairs={{0,2},{1,3},{2,0},{3,1},{4,6},{5,7},{6,4},{7,5},{8,10},{9,11},{10,... | collective-permute-start | bytes 786440 | tf_op jit(solution)/shard_map/cond/branch_2_fun/ppermute | solution.py:289
  91.5 18.8 %collective-permute-start.40 = (f32[5,128,128]{2,1,0:T(8,128)}, f32[5,128,128]{2,1,0:T(8,128)}, u32[]{:S(2)}, u32[]{:S(2)}) collective-permute-start(f32[5,128,128]{2,1,0:T(8,128)} %get-tuple-element.131), channel_id=1, source_target_pairs={{0,4},{1,5},{2,6},{3,7},{4,0},{5,1},{6,2},{7,3},{8,12},{9,13},{10,... | collective-permute-start | bytes 983048 | tf_op jit(solution)/shard_map/cond/branch_2_fun/ppermute | solution.py:289
  96.1 12.3 %collective-permute-start.44 = (f32[2,128,128]{2,1,0:T(8,128)}, f32[2,128,128]{2,1,0:T(8,128)}, u32[]{:S(2)}, u32[]{:S(2)}) collective-permute-start(f32[2,128,128]{2,1,0:T(8,128)} %slice.172), channel_id=1, source_target_pairs={{0,8},{1,9},{2,10},{3,11},{4,12},{5,13},{6,14},{7,15},{8,0},{9,1},... | collective-permute-start | bytes 393224 | tf_op jit(solution)/shard_map/cond/branch_2_fun/ppermute | solution.py:289
  99.5 15.6 %collective-permute-start.43 = (f32[4,128,128]{2,1,0:T(8,128)}, f32[4,128,128]{2,1,0:T(8,128)}, u32[]{:S(2)}, u32[]{:S(2)}) collective-permute-start(f32[4,128,128]{2,1,0:T(8,128)} %select_select_fusion.25), channel_id=1, source_target_pairs={{0,4},{1,5},{2,6},{3,7},{4,0},{5,1},{6,2},{7,3},{8,12},{9,13},{10,... | collective-permute-start | bytes 786440 | tf_op jit(solution)/shard_map/cond/branch_2_fun/ppermute | solution.py:289
  101.0 1.5 %copy-start.2 = (f32[416,8,128]{2,1,0:T(8,128)S(1)}, f32[416,8,128]{2,1,0:T(8,128)}, u32[]{:S(2)}) copy-start(f32[416,8,128]{2,1,0:T(8,128)} %all-gather.11.cloned.1.call-done) | copy-start | bytes 5111812 | tf_op jit(solution)/shard_map/cond
  102.5 7.9 %copy-start.10 = (f32[5,128,128]{2,1,0:T(8,128)S(1)}, f32[5,128,128]{2,1,0:T(8,128)}, u32[]{:S(2)}) copy-start(f32[5,128,128]{2,1,0:T(8,128)} %copy-done.9) | copy-start | bytes 983044 | tf_op jit(solution)/shard_map/cond
  108.4 5.9 %collective-permute-start.47 = (f32[2,8,8,128]{3,2,1,0:T(8,128)S(1)}, f32[2,8,8,128]{3,2,1,0:T(8,128)S(1)}, u32[]{:S(2)}, u32[]{:S(2)}) collective-permute-start(f32[2,8,8,128]{3,2,1,0:T(8,128)S(1)} %edges.5), channel_id=1, source_target_pairs={{0,8},{1,9},{2,10},{3,11},{4,12},{5,13},{6,14},{7,15},{8,0},{9,1},... | collective-permute-start | bytes 196616 | tf_op jit(solution)/shard_map/cond/branch_2_fun/ppermute | solution.py:289
  110.3 4.8 %copy-start.17 = (f32[4,128,128]{2,1,0:T(8,128)S(1)}, f32[4,128,128]{2,1,0:T(8,128)}, u32[]{:S(2)}) copy-start(f32[4,128,128]{2,1,0:T(8,128)} %copy-done.16) | copy-start | bytes 786436 | tf_op jit(solution)/shard_map/cond
  110.5 5.9 %collective-permute-start.49 = (f32[2,8,8,128]{3,2,1,0:T(8,128)S(1)}, f32[2,8,8,128]{3,2,1,0:T(8,128)S(1)}, u32[]{:S(2)}, u32[]{:S(2)}) collective-permute-start(f32[2,8,8,128]{3,2,1,0:T(8,128)S(1)} %edges.5), channel_id=1, source_target_pairs={{0,2},{1,3},{2,0},{3,1},{4,6},{5,7},{6,4},{7,5},{8,10},{9,11},{10,... | collective-permute-start | bytes 196616 | tf_op jit(solution)/shard_map/cond/branch_2_fun/ppermute | solution.py:289
  114.3 4.3 %collective-permute-start.48 = (f32[2,8,8,128]{3,2,1,0:T(8,128)S(1)}, f32[2,8,8,128]{3,2,1,0:T(8,128)S(1)}, u32[]{:S(2)}, u32[]{:S(2)}) collective-permute-start(f32[2,8,8,128]{3,2,1,0:T(8,128)S(1)} %collective-permute-done.47), channel_id=1, source_target_pairs={{0,2},{1,3},{2,0},{3,1},{4,6},{5,7},{6,4},{7,5},{8,10},{9,11},{10,... | collective-permute-start | bytes 196616 | tf_op jit(solution)/shard_map/cond/branch_2_fun/ppermute | solution.py:289
  115.2 5.2 %collective-permute-start.45 = (f32[2,128,128]{2,1,0:T(8,128)}, f32[2,128,128]{2,1,0:T(8,128)S(1)}, u32[]{:S(2)}, u32[]{:S(2)}) collective-permute-start(f32[2,128,128]{2,1,0:T(8,128)} %collective-permute-done.44), channel_id=1, source_target_pairs={{0,2},{1,3},{2,0},{3,1},{4,6},{5,7},{6,4},{7,5},{8,10},{9,11},{10,... | collective-permute-start | bytes 393224 | tf_op jit(solution)/shard_map/cond/branch_2_fun/ppermute | solution.py:289
  118.5 4.3 %collective-permute-start.50 = (f32[2,8,8,128]{3,2,1,0:T(8,128)S(1)}, f32[2,8,8,128]{3,2,1,0:T(8,128)S(1)}, u32[]{:S(2)}, u32[]{:S(2)}) collective-permute-start(f32[2,8,8,128]{3,2,1,0:T(8,128)S(1)} %select_select_fusion.29), channel_id=1, source_target_pairs={{0,4},{1,5},{2,6},{3,7},{4,0},{5,1},{6,2},{7,3},{8,12},{9,13},{10,... | collective-permute-start | bytes 196616 | tf_op jit(solution)/shard_map/cond/branch_2_fun/ppermute | solution.py:289
  120.5 5.0 %collective-permute-start.46 = (f32[2,128,128]{2,1,0:T(8,128)S(1)}, f32[2,128,128]{2,1,0:T(8,128)S(1)}, u32[]{:S(2)}, u32[]{:S(2)}) collective-permute-start(f32[2,128,128]{2,1,0:T(8,128)S(1)} %select_select_fusion.27), channel_id=1, source_target_pairs={{0,4},{1,5},{2,6},{3,7},{4,0},{5,1},{6,2},{7,3},{8,12},{9,13},{10,... | collective-permute-start | bytes 393224 | tf_op jit(solution)/shard_map/cond/branch_2_fun/ppermute | solution.py:289
  (4 other events, 3.0 us)
Sparse Core Ops, SparseCore 0:
  15.7 58.8 all-gather.10

commit v3 on v2

--- a/solution.py
+++ b/solution.py
@@ -36,7 +36,11 @@
     here = here_ref[0]
     for side in range(2):
         beside = neighbours_ref[here, side]
-        plan_ref[side] = jnp.maximum(beside, 0)
+        apart = jnp.bitwise_xor(jnp.maximum(beside, 0), here)
+        spot = jnp.int32(0)
+        for bit in range(top + 1):
+            spot = spot | (((apart >> bit) & 1) << (top - bit))
+        plan_ref[side] = spot
         plan_ref[2 + side] = (beside >= 0).astype(jnp.int32)
     order = [order_ref[r] for r in range(ROUNDS)]
     low = jnp.minimum(jnp.minimum(order[0], order[1]), order[2])
@@ -73,11 +77,15 @@
         sent_ref[3 * depth + r] = jnp.full((ROWS, LANES), rates_ref[0, r], jnp.float32)
 
 
-def interior_kernel(velocity_ref, rates_ref, u_ref, k_ref, out_ref, ub, kp, kxr, kxl, ky, kz, c0):
+def interior_kernel(first, cuts, velocity_ref, rates_ref, u_ref, k_ref, *refs):
+    out_refs, (ub, kp, kxr, kxl, ky, kz, c0) = refs[: len(cuts)], refs[len(cuts) :]
     depth, height, _ = k_ref.shape
     blocks = height // ROWS
+    last = first + sum(cuts)
+    start, stop = max(first - 1, 0), min(last + 1, blocks)
     half = 0.5 * time_step
     zero = jnp.zeros((ROWS, LANES), jnp.float32)
+    low, high = max(start - 1, 0) * ROWS, min(stop + 1, blocks) * ROWS
     for z in range(depth):
         for edge in (0, height + ROWS):
             kp[z, edge : edge + ROWS] = zero
@@ -85,9 +93,9 @@
             for s in range(2):
                 for i in range(2):
                     ub[s, i, z, edge : edge + ROWS] = zero
-        kp[z, ROWS : ROWS + height] = k_ref[z]
+        kp[z, ROWS + low : ROWS + high] = k_ref[z, low:high]
         for i in range(2):
-            ub[0, i, z, ROWS : ROWS + height] = u_ref[i, z]
+            ub[0, i, z, ROWS + low : ROWS + high] = u_ref[i, z, low:high]
     pos = [[speeds(velocity_ref, i, d) for d in range(3)] for i in range(2)]
     decay = time_step * rates_ref[0, 1]
     growth = time_step * rates_ref[0, 0]
@@ -124,47 +132,53 @@
             below = above
         return 0
 
-    lax.fori_loop(0, blocks, coefficients, 0)
-
-    for step in range(STEPS):
-        src = step % 2
-
-        def advance(b, _):
-            y = pl.multiple_of(b * ROWS, ROWS)
-            at = y + ROWS
-            prior = [zero, zero]
-            here = [ub[src, i, 0, pl.ds(at, ROWS)] for i in range(2)]
-            zl = zero
-            for z in range(depth):
-                last = z == depth - 1
-                after = [zero, zero] if last else [ub[src, i, z + 1, pl.ds(at, ROWS)] for i in range(2)]
-                xr = kxr[z, pl.ds(y, ROWS)]
-                xl = kxl[z, pl.ds(y, ROWS)]
-                yr = ky[z, pl.ds(at, ROWS)]
-                yl = ky[z, pl.ds(at - 1, ROWS)]
-                zr = kz[z, pl.ds(y, ROWS)]
-                q = (growth * here[0]) * here[1]
-                for i in range(2):
-                    (px, mx), (py, my), (pz, mz) = pos[i]
-                    u = here[i]
-                    new = c0[i, z, pl.ds(y, ROWS)] * u
-                    new = new + (xr - mx) * pltpu.roll(u, LANES - 1, 1) + (xl + px) * pltpu.roll(u, 1, 1)
-                    new = new + (
-                        (yr - my) * ub[src, i, z, pl.ds(at + 1, ROWS)] + (yl + py) * ub[src, i, z, pl.ds(at - 1, ROWS)]
-                    )
-                    if not last:
-                        new = new + (zr - mz) * after[i]
-                    if z > 0:
-                        new = new + (zl + pz) * prior[i]
-                    new = new - q if i == 0 else new + q
-                    if step == STEPS - 1:
-                        out_ref[i, z, pl.ds(y, ROWS)] = new
-                    else:
-                        ub[1 - src, i, z, pl.ds(at, ROWS)] = new
-                prior, here, zl = here, after, zr
-            return 0
-
-        lax.fori_loop(0, blocks, advance, 0)
+    lax.fori_loop(start, stop, coefficients, 0)
+
+    def advance(src, put, b, _):
+        y = pl.multiple_of(b * ROWS, ROWS)
+        at = y + ROWS
+        prior = [zero, zero]
+        here = [ub[src, i, 0, pl.ds(at, ROWS)] for i in range(2)]
+        zl = zero
+        for z in range(depth):
+            end = z == depth - 1
+            after = [zero, zero] if end else [ub[src, i, z + 1, pl.ds(at, ROWS)] for i in range(2)]
+            xr = kxr[z, pl.ds(y, ROWS)]
+            xl = kxl[z, pl.ds(y, ROWS)]
+            yr = ky[z, pl.ds(at, ROWS)]
+            yl = ky[z, pl.ds(at - 1, ROWS)]
+            zr = kz[z, pl.ds(y, ROWS)]
+            q = (growth * here[0]) * here[1]
+            for i in range(2):
+                (px, mx), (py, my), (pz, mz) = pos[i]
+                u = here[i]
+                new = c0[i, z, pl.ds(y, ROWS)] * u
+                new = new + (xr - mx) * pltpu.roll(u, LANES - 1, 1) + (xl + px) * pltpu.roll(u, 1, 1)
+                new = new + (
+                    (yr - my) * ub[src, i, z, pl.ds(at + 1, ROWS)] + (yl + py) * ub[src, i, z, pl.ds(at - 1, ROWS)]
+                )
+                if not end:
+                    new = new + (zr - mz) * after[i]
+                if z > 0:
+                    new = new + (zl + pz) * prior[i]
+                put(b, i, z, new - q if i == 0 else new + q)
+            prior, here, zl = here, after, zr
+        return 0
+
+    for step in range(STEPS - 1):
+
+        def keep(b, i, z, new, step=step):
+            ub[1 - step % 2, i, z, pl.ds(pl.multiple_of(b * ROWS + ROWS, ROWS), ROWS)] = new
+
+        lax.fori_loop(start, stop, partial(advance, step % 2, keep), 0)
+    begin = first
+    for cut, out_ref in zip(cuts, out_refs):
+
+        def give(b, i, z, new, out_ref=out_ref, begin=begin):
+            out_ref[i, z, pl.ds(pl.multiple_of((b - begin) * ROWS, ROWS), ROWS)] = new
+
+        lax.fori_loop(begin, begin + cut, partial(advance, (STEPS - 1) % 2, give), 0)
+        begin += cut
 
 
 def edge_kernel(plan_ref, velocity_ref, rates_ref, left_ref, right_ref, own_ref, out_ref, ub, kp, kxr, kxl, ky, kz, c0):
@@ -273,15 +287,21 @@
             out_ref[i, z] = pltpu.roll(jnp.where(row < 4, low, high), 4, 0)
 
 
-def merge_kernel(u_ref, edge_ref, out_ref):
-    depth = u_ref.shape[1]
+def merge_kernel(*refs):
+    *part_refs, edge_ref, out_ref = refs
+    depth = out_ref.shape[1]
     turned = edge_ref[...].reshape(2 * depth * ROWS, LANES).T
-    wide = lax.broadcasted_iota(jnp.int32, (LANES, LANES), 1)
-    rim = (wide < 4) | (wide >= LANES - 4)
-    for i in range(2):
-        for z in range(depth):
-            shift = (LANES - 4 - ROWS * (i * depth + z)) % LANES
-            out_ref[i, z] = jnp.where(rim, pltpu.roll(turned, shift, 1), u_ref[i, z])
+    begin = 0
+    for part_ref in part_refs:
+        rows = part_ref.shape[2]
+        wide = lax.broadcasted_iota(jnp.int32, (rows, LANES), 1)
+        rim = (wide < 4) | (wide >= LANES - 4)
+        for i in range(2):
+            for z in range(depth):
+                shift = (LANES - 4 - ROWS * (i * depth + z)) % LANES
+                turn = pltpu.roll(turned[begin : begin + rows], shift, 1)
+                out_ref[i, z, begin : begin + rows] = jnp.where(rim, turn, part_ref[i, z])
+        begin += rows
 
 
 def swap(block, bit):
@@ -296,14 +316,39 @@
     return picked
 
 
-def after(value, earlier):
-    return lax.optimization_barrier((value, earlier))
-
-
-def edge_call(plan, velocity, rates, gathered, own, tiles):
+def order(*values):
+    return lax.optimization_barrier(values)
+
+
+def interior_call(first, cuts, velocity, rates, field, kappa):
+    species, depth, height, width = field.shape
+    f32 = jnp.float32
+    padded = height + 2 * ROWS
+    return pl.pallas_call(
+        partial(interior_kernel, first, cuts),
+        out_shape=[jax.ShapeDtypeStruct((species, depth, cut * ROWS, width), f32) for cut in cuts],
+        in_specs=[SMEM] * 2 + [VMEM] * 2,
+        out_specs=[VMEM] * len(cuts),
+        scratch_shapes=[
+            pltpu.VMEM((2, species, depth, padded, width), f32),
+            pltpu.VMEM((depth, padded, width), f32),
+            pltpu.VMEM((depth, height, width), f32),
+            pltpu.VMEM((depth, height, width), f32),
+            pltpu.VMEM((depth, padded, width), f32),
+            pltpu.VMEM((depth, height, width), f32),
+            pltpu.VMEM((species, depth, height, width), f32),
+        ],
+        compiler_params=PARAMS,
+        cost_estimate=pl.CostEstimate(flops=40_000_000, bytes_accessed=10_000_000, transcendentals=0),
+        name="interior",
+    )(velocity, rates, field, kappa)
+
+
+def edge_call(plan, velocity, rates, gathered, own):
     f32 = jnp.float32
     species = 2
     depth = own.shape[1]
+    tiles = gathered.shape[1]
     return pl.pallas_call(
         edge_kernel,
         out_shape=jax.ShapeDtypeStruct((species, depth, ROWS, LANES), f32),
@@ -333,83 +378,54 @@
     )(plan, velocity, rates, gathered, gathered, own)
 
 
-def spans(total):
-    sizes = (5, 5, 4, 2) if total == 16 else (total,)
-    return [(sum(sizes[:n]), sum(sizes[: n + 1])) for n in range(len(sizes))]
+def double(strips, bit):
+    return jnp.concatenate([strips, swap(strips, bit)], axis=0)
 
 
 def run(low, high, top, field, kappa, rates, velocity, plan, own, sent):
-    species, depth, height, width = field.shape
-    f32 = jnp.float32
-    tiles = sent.shape[0]
-    gathered = lax.all_gather(sent, AXES, axis=0, tiled=False)
-    padded = height + 2 * ROWS
-    inner = pl.pallas_call(
-        interior_kernel,
-        out_shape=jax.ShapeDtypeStruct(field.shape, f32),
-        in_specs=[SMEM] * 2 + [VMEM] * 2,
-        out_specs=VMEM,
-        scratch_shapes=[
-            pltpu.VMEM((2, species, depth, padded, width), f32),
-            pltpu.VMEM((depth, padded, width), f32),
-            pltpu.VMEM((depth, height, width), f32),
-            pltpu.VMEM((depth, height, width), f32),
-            pltpu.VMEM((depth, padded, width), f32),
-            pltpu.VMEM((depth, height, width), f32),
-            pltpu.VMEM((species, depth, height, width), f32),
-        ],
-        compiler_params=PARAMS,
-        cost_estimate=pl.CostEstimate(flops=40_000_000, bytes_accessed=10_000_000, transcendentals=0),
-        name="interior",
-    )(velocity, rates, field, kappa)
-    planes = inner.reshape(species * depth, height, width)
-    cuts = spans(species * depth)
-    last = len(cuts) - 1
-    across = swap(planes, low)
-    near = []
-    far = []
-    sent_on = []
-    out = []
-
-    def start_near(n):
-        part = planes[cuts[n][0] : cuts[n][1]]
-        if n >= 2:
-            part, near[n - 2] = after(part, near[n - 2])
-        if n >= 3:
-            part, far[n - 3] = after(part, far[n - 3])
-        near.append(swap(part, top))
-
-    for n in range(min(2, last + 1)):
-        start_near(n)
-    for n, (start, stop) in enumerate(cuts):
-        part = near[n]
-        if n == last:
-            own, part = after(own, part) if n == 0 else (own, part)
-            if n > 0:
-                own, near[n - 1] = after(own, near[n - 1])
-            edges = edge_call(plan, velocity, rates, gathered, own, tiles)
-            part, edges = after(part, edges)
-        if n >= 2:
-            part, sent_on[n - 2] = after(part, sent_on[n - 2])
-        far.append(swap(part, low))
-        if n + 2 <= last:
-            start_near(n + 2)
-        options = (planes[start:stop], near[n], across[start:stop], far[n])
-        sent_on.append(swap(pick(plan[5], options), high))
-        out.append(jnp.where(plan[7] > 0, sent_on[n], pick(plan[6], options)))
-    rim_near = swap(edges, top)
-    options = (edges, rim_near, swap(edges, low), swap(rim_near, low))
-    other = swap(pick(plan[5], options), high)
-    rim = jnp.where(plan[7] > 0, other, pick(plan[6], options))
-    final = jnp.concatenate(out, axis=0).reshape(field.shape)
+    blocks = field.shape[2] // ROWS
+    cuts = (blocks * 7 // 16, blocks // 4, blocks * 3 // 16, blocks // 8)
+    give = partial(pick, plan[5])
+    keep = partial(pick, plan[6])
+
+    def result(options, other):
+        return jnp.where(plan[7] > 0, other, keep(options))
+
+    strips = double(sent[None], top)
+    (p0,) = interior_call(0, cuts[:1], velocity, rates, field, kappa)
+    p0, strips, field = order(p0, strips, field)
+    n0, a0 = swap(p0, top), swap(p0, low)
+    p1, p2, p3 = interior_call(cuts[0], cuts[1:], velocity, rates, field, kappa)
+    for bit in reversed(range(1, top)):
+        strips = double(strips, bit)
+        p1, strips = order(p1, strips)
+    p1, p2, p3, n0, a0, strips = order(p1, p2, p3, n0, a0, strips)
+    n1, a1, f0 = swap(p1, top), swap(p1, low), swap(n0, low)
+    strips = double(strips, 0)
+    p2, n1, a1, f0, strips = order(p2, n1, a1, f0, strips)
+    o0 = (p0, n0, a0, f0)
+    n2, a2, f1, h0 = swap(p2, top), swap(p2, low), swap(n1, low), swap(give(o0), high)
+    edges = edge_call(plan, velocity, rates, strips, own)
+    p3, n2, a2, f1, h0, edges = order(p3, n2, a2, f1, h0, edges)
+    o1 = (p1, n1, a1, f1)
+    n3, a3, f2, h1 = swap(p3, top), swap(p3, low), swap(n2, low), swap(give(o1), high)
+    en, ea = swap(edges, top), swap(edges, low)
+    n3, a3, f2, h1, en, ea = order(n3, a3, f2, h1, en, ea)
+    o2 = (p2, n2, a2, f2)
+    f3, h2, ef = swap(n3, low), swap(give(o2), high), swap(en, low)
+    f3, h2, ef = order(f3, h2, ef)
+    o3 = (p3, n3, a3, f3)
+    oe = (edges, en, ea, ef)
+    h3, eh = swap(give(o3), high), swap(give(oe), high)
+    parts = [result(*pair) for pair in ((o0, h0), (o1, h1), (o2, h2), (o3, h3), (oe, eh))]
     return pl.pallas_call(
         merge_kernel,
-        out_shape=jax.ShapeDtypeStruct(field.shape, f32),
-        in_specs=[VMEM] * 2,
+        out_shape=jax.ShapeDtypeStruct(field.shape, jnp.float32),
+        in_specs=[VMEM] * 5,
         out_specs=VMEM,
         compiler_params=PARAMS,
         name="merge",
-    )(final, rim)
+    )(*parts)
 
 
 def per_device(concentration, diffusivity, rates, velocity, neighbours, migrate, bit_order):

time: 135 us -> 114 us (0.84)
  between operations: 14.1 us -> 0.68 us
  waiting for transfers between devices: 61.6 us -> 55.6 us
  local copies, waits for them, and re-layouts: 7.19 us -> 4.31 us
  starting transfers between devices: 24.1 us -> 26.9 us
  other arithmetic: 3.04 us -> 0.79 us
  Pallas kernels: 20 us -> 21.4 us
    ppermute x17 -> x24, waiting for transfers between devices: 61 us -> 55.6 us  [swap(): lax.ppermute(block, AXES, [(low, low ^ 1 << bit) for low in range(count)])]
    ppermute x17 -> x24, starting transfers between devices: 24 us -> 26.9 us  [swap(): lax.ppermute(block, AXES, [(low, low ^ 1 << bit) for low in range(count)])]
    cond x14 -> x8, local copies, waits for them, and re-layouts: 2.17 us -> 0.03 us
    pallas_call x1 -> x2, Pallas kernels: 11 us -> 12.6 us  [interior_call(): pl.pallas_call(partial(interior_kernel, first, cuts), out_shape=[jax.Shap...]
    select_n x4 -> x5, other arithmetic: 1.73 us -> 0.25 us  [pick(): picked = jnp.where(index == number, options[number], picked)]
  transfers between devices with their start and end apart: 18 -> 24, of which waited for: 11 -> 11; matrix products, arithmetic and copies ran while one was open for 3% -> 1% of each run, Pallas kernels for 13% -> 16%
where the time goes in v3:
time: 114 us; the launch traced here: 115 us
  waiting for transfers between devices  55.6 us (49%)
  starting transfers between devices  26.9 us (24%)
  Pallas kernels  21.4 us (19%)
  loops' own time  5.05 us (4%)
  local copies, waits for them, and re-layouts  4.31 us (4%)
    ppermute x24, waiting for transfers between devices, swap(): lax.ppermute(block, AXES, [(low, low ^ 1 << bit) for low in range(count)])  55.6 us
    ppermute x24, starting transfers between devices, swap(): lax.ppermute(block, AXES, [(low, low ^ 1 << bit) for low in range(count)])  26.9 us
    pallas_call x2, Pallas kernels, interior_call(): pl.pallas_call(partial(interior_kernel, first, cuts), out_shape=[jax.Shap...  12.6 us
    pallas_call x1, Pallas kernels, edge_call(): pl.pallas_call(edge_kernel, out_shape=jax.ShapeDtypeStruct((species, dept...  5.87 us
    another operation x1, loops' own time, per_device(): lax.switch(plan[4], branches, field, kappa, rates, velocity, plan, own, s...  5.05 us
    unnamed x7, local copies, waits for them, and re-layouts  3.06 us
    pallas_call x1, Pallas kernels, per_device(): pl.pallas_call(partial(prepare_kernel, top), out_shape=(jax.ShapeDtypeStr...  2.48 us
  transfers between devices with their start and end apart: 24, of which 11 were waited for; matrix products, arithmetic and copies ran while one was open for 1% of the time, Pallas kernels for 16%

profile of v3, /device:TPU:0, one launch (start us, length us, event | category | flops | bytes accessed | tf_op | source)
XLA Modules:
  0.0 114.7 jit_solution(19919212204846933)
XLA Ops:
  2.1 2.5 %prepare.1 = (s32[8]{0:T(128)S(1)}, f32[3,8,16,128]{3,2,1,0:T(8,128)S(1)}, f32[26,8,128]{2,1,0:T(8,128)S(1)}) custom-call(s32[1]{0:T(128)} %bitcast.27.here_ref, s32[16,2]{1,0:T(8,128)S(1)} %copy.11.neighbours_ref, s32[3,16]{1,0:T(4,128)S(1)} %copy-done, s32[3]{0:T(128)S(1)} %copy-done.1, f32[1,2]{1,0:T(1,128)} %rates_ref.1, f32[2,8,128,128]{3,2,1,0:T(8,128)} %bitcast.31, ...), custom_call_target="tpu_custom_call" | custom-call | tf_op jit(solution)/shard_map/prepare/pallas_call | solution.py:437
  5.8 107.9 %conditional.1 = (f32[1,2,8,128,128]{4,3,2,1,0:T(8,128)S(1)}) conditional(s32[]{:T(128)} %bitcast.30, (s32[8]{0:T(128)S(1)}, f32[2,3]{1,0:T(2,128)}, f32[1,2]{1,0:T(1,128)}, f32[2,8,128,128]{3,2,1,0:T(8,128)}, f32[8,128,128]{2,1,0:T(8,128)}, /*index=5*/f32[26,8,128]{2,1,0:T(8,128)S(1)}, f32[3,8,16,128]{3,2,1,0:T(8,128)S(1)}) %tuple.57, ...), branch_computations={%region_0.1_spmd, %region_1.2_spmd, %region_2.3_spmd} | conditional | flops 82748416 | bytes 69153320 | solution.py:450
  6.1 4.1 %collective-permute-start.48 = (f32[1,26,8,128]{3,2,1,0:T(8,128)S(1)}, f32[1,26,8,128]{3,2,1,0:T(8,128)S(1)}, u32[]{:S(2)}, u32[]{:S(2)}) collective-permute-start(f32[1,26,8,128]{3,2,1,0:T(8,128)S(1)} %bitcast.46), channel_id=1, source_target_pairs={{0,8},{1,9},{2,10},{3,11},{4,12},{5,13},{6,14},{7,15},{8,0},{9,1},... | collective-permute-start | bytes 319496 | tf_op jit(solution)/shard_map/cond/branch_2_fun/ppermute | solution.py:309
  10.2 6.1 %interior.10 = f32[2,8,56,128]{3,2,1,0:T(8,128)S(1)} custom-call(f32[2,3]{1,0:T(2,128)} %get-tuple-element.139.velocity_ref, f32[1,2]{1,0:T(1,128)} %get-tuple-element.140.rates_ref, f32[2,8,128,128]{3,2,1,0:T(8,128)} %get-tuple-element.144.u_ref, f32[8,128,128]{2,1,0:T(8,128)} %get-tuple-element.142.k_ref), custom_call_target="tpu_custom_call" | custom-call | flops 40000000 | bytes 10000000 | tf_op jit(solution)/shard_map/cond/branch_2_fun/interior/pallas_call | solution.py:327
  16.3 1.6 %collective-permute-start.49 = (f32[2,26,8,128]{3,2,1,0:T(8,128)S(1)}, f32[2,26,8,128]{3,2,1,0:T(8,128)S(1)}, u32[]{:S(2)}, u32[]{:S(2)}) collective-permute-start(f32[2,26,8,128]{3,2,1,0:T(8,128)S(1)} %pad_maximum_fusion.11), channel_id=1, source_target_pairs={{0,4},{1,5},{2,6},{3,7},{4,0},{5,1},{6,2},{7,3},{8,12},{9,13},{10,... | collective-permute-start | bytes 638984 | tf_op jit(solution)/shard_map/cond/branch_2_fun/ppermute | solution.py:309
  18.0 6.5 %interior.11 = (f32[2,8,32,128]{3,2,1,0:T(8,128)S(1)}, f32[2,8,24,128]{3,2,1,0:T(8,128)S(1)}, f32[2,8,16,128]{3,2,1,0:T(8,128)S(1)}) custom-call(f32[2,3]{1,0:T(2,128)S(1)} %copy-done.11, f32[1,2]{1,0:T(1,128)S(1)} %copy-done.14, f32[2,8,128,128]{3,2,1,0:T(8,128)S(1)} %copy-done.4, f32[8,128,128]{2,1,0:T(8,128)S(1)} %copy-done.7), custom_call_target="tpu_custom_call" | custom-call | flops 40000000 | bytes 10000000 | tf_op jit(solution)/shard_map/cond/branch_2_fun/interior/pallas_call | solution.py:327
  24.5 1.6 %collective-permute-start.50 = (f32[4,26,8,128]{3,2,1,0:T(8,128)S(1)}, f32[4,26,8,128]{3,2,1,0:T(8,128)S(1)}, u32[]{:S(2)}, u32[]{:S(2)}) collective-permute-start(f32[4,26,8,128]{3,2,1,0:T(8,128)S(1)} %pad_maximum_fusion.10), channel_id=1, source_target_pairs={{0,2},{1,3},{2,0},{3,1},{4,6},{5,7},{6,4},{7,5},{8,10},{9,11},{10,... | collective-permute-start | bytes 1277960 | tf_op jit(solution)/shard_map/cond/branch_2_fun/ppermute | solution.py:309
  26.1 1.6 %collective-permute-start.51 = (f32[2,8,56,128]{3,2,1,0:T(8,128)S(1)}, f32[2,8,56,128]{3,2,1,0:T(8,128)S(1)}, u32[]{:S(2)}, u32[]{:S(2)}) collective-permute-start(f32[2,8,56,128]{3,2,1,0:T(8,128)S(1)} %interior.10), channel_id=1, source_target_pairs={{0,8},{1,9},{2,10},{3,11},{4,12},{5,13},{6,14},{7,15},{8,0},{9,1},... | collective-permute-start | bytes 1376264 | tf_op jit(solution)/shard_map/cond/branch_2_fun/ppermute | solution.py:309
  28.3 9.1 %collective-permute-done.50 = f32[4,26,8,128]{3,2,1,0:T(8,128)S(1)} collective-permute-done((f32[4,26,8,128]{3,2,1,0:T(8,128)S(1)}, f32[4,26,8,128]{3,2,1,0:T(8,128)S(1)}, u32[]{:S(2)}, u32[]{:S(2)}) %collective-permute-start.50) | collective-permute-done | bytes 426016 | tf_op jit(solution)/shard_map/cond/branch_2_fun/ppermute | solution.py:309
  37.4 10.7 %collective-permute-done.51 = f32[2,8,56,128]{3,2,1,0:T(8,128)S(1)} collective-permute-done((f32[2,8,56,128]{3,2,1,0:T(8,128)S(1)}, f32[2,8,56,128]{3,2,1,0:T(8,128)S(1)}, u32[]{:S(2)}, u32[]{:S(2)}) %collective-permute-start.51) | collective-permute-done | bytes 458784 | tf_op jit(solution)/shard_map/cond/branch_2_fun/ppermute | solution.py:309
  52.8 10.1 %collective-permute-done.53 = f32[2,8,32,128]{3,2,1,0:T(8,128)S(1)} collective-permute-done((f32[2,8,32,128]{3,2,1,0:T(8,128)S(1)}, f32[2,8,32,128]{3,2,1,0:T(8,128)S(1)}, u32[]{:S(2)}, u32[]{:S(2)}) %collective-permute-start.53) | collective-permute-done | bytes 262176 | tf_op jit(solution)/shard_map/cond/branch_2_fun/ppermute | solution.py:309
  63.0 3.7 %collective-permute-done.54 = f32[2,8,32,128]{3,2,1,0:T(8,128)S(1)} collective-permute-done((f32[2,8,32,128]{3,2,1,0:T(8,128)S(1)}, f32[2,8,32,128]{3,2,1,0:T(8,128)S(1)}, u32[]{:S(2)}, u32[]{:S(2)}) %collective-permute-start.54) | collective-permute-done | bytes 262176 | tf_op jit(solution)/shard_map/cond/branch_2_fun/ppermute | solution.py:309
  67.4 2.5 %collective-permute-start.57 = (f32[2,8,24,128]{3,2,1,0:T(8,128)S(1)}, f32[2,8,24,128]{3,2,1,0:T(8,128)S(1)}, u32[]{:S(2)}, u32[]{:S(2)}) collective-permute-start(f32[2,8,24,128]{3,2,1,0:T(8,128)S(1)} %get-tuple-element.159), channel_id=1, source_target_pairs={{0,8},{1,9},{2,10},{3,11},{4,12},{5,13},{6,14},{7,15},{8,0},{9,1},... | collective-permute-start | bytes 589832 | tf_op jit(solution)/shard_map/cond/branch_2_fun/ppermute | solution.py:309
  73.9 5.9 %edges.5 = f32[2,8,8,128]{3,2,1,0:T(8,128)S(1)} custom-call(s32[8]{0:T(128)S(1)} %get-tuple-element.138.plan_ref, f32[2,3]{1,0:T(2,128)S(1)} %copy-done.11, f32[1,2]{1,0:T(1,128)S(1)} %copy-done.14, f32[16,26,8,128]{3,2,1,0:T(8,128)S(1)} %pad_maximum_fusion.8.left_ref.right_ref, f32[16,26,8,128]{3,2,1,0:T(8,128)S(1)} %pad_maximum_fusion.8.left_ref.right_ref, ...), custom_call_target="tpu_custom_call" | custom-call | tf_op jit(solution)/shard_map/cond/branch_2_fun/edges/pallas_call | solution.py:352
  81.0 2.2 %collective-permute-done.60 = f32[2,8,56,128]{3,2,1,0:T(8,128)S(1)} collective-permute-done((f32[2,8,56,128]{3,2,1,0:T(8,128)S(1)}, f32[2,8,56,128]{3,2,1,0:T(8,128)S(1)}, u32[]{:S(2)}, u32[]{:S(2)}) %collective-permute-start.60) | collective-permute-done | bytes 458784 | tf_op jit(solution)/shard_map/cond/branch_2_fun/ppermute | solution.py:309
  85.0 1.7 %collective-permute-start.65 = (f32[2,8,8,128]{3,2,1,0:T(8,128)S(1)}, f32[2,8,8,128]{3,2,1,0:T(8,128)S(1)}, u32[]{:S(2)}, u32[]{:S(2)}) collective-permute-start(f32[2,8,8,128]{3,2,1,0:T(8,128)S(1)} %edges.5), channel_id=1, source_target_pairs={{0,8},{1,9},{2,10},{3,11},{4,12},{5,13},{6,14},{7,15},{8,0},{9,1},... | collective-permute-start | bytes 196616 | tf_op jit(solution)/shard_map/cond/branch_2_fun/ppermute | solution.py:309
  86.6 1.5 %collective-permute-start.66 = (f32[2,8,8,128]{3,2,1,0:T(8,128)S(1)}, f32[2,8,8,128]{3,2,1,0:T(8,128)S(1)}, u32[]{:S(2)}, u32[]{:S(2)}) collective-permute-start(f32[2,8,8,128]{3,2,1,0:T(8,128)S(1)} %edges.5), channel_id=1, source_target_pairs={{0,2},{1,3},{2,0},{3,1},{4,6},{5,7},{6,4},{7,5},{8,10},{9,11},{10,... | collective-permute-start | bytes 196616 | tf_op jit(solution)/shard_map/cond/branch_2_fun/ppermute | solution.py:309
  89.2 4.8 %collective-permute-done.65 = f32[2,8,8,128]{3,2,1,0:T(8,128)S(1)} collective-permute-done((f32[2,8,8,128]{3,2,1,0:T(8,128)S(1)}, f32[2,8,8,128]{3,2,1,0:T(8,128)S(1)}, u32[]{:S(2)}, u32[]{:S(2)}) %collective-permute-start.65) | collective-permute-done | bytes 65568 | tf_op jit(solution)/shard_map/cond/branch_2_fun/ppermute | solution.py:309
  94.7 5.4 %collective-permute-done.63 = f32[2,8,24,128]{3,2,1,0:T(8,128)S(1)} collective-permute-done((f32[2,8,24,128]{3,2,1,0:T(8,128)S(1)}, f32[2,8,24,128]{3,2,1,0:T(8,128)S(1)}, u32[]{:S(2)}, u32[]{:S(2)}) %collective-permute-start.63) | collective-permute-done | bytes 196640 | tf_op jit(solution)/shard_map/cond/branch_2_fun/ppermute | solution.py:309
  100.8 1.5 %collective-permute-start.69 = (f32[2,8,8,128]{3,2,1,0:T(8,128)S(1)}, f32[2,8,8,128]{3,2,1,0:T(8,128)S(1)}, u32[]{:S(2)}, u32[]{:S(2)}) collective-permute-start(f32[2,8,8,128]{3,2,1,0:T(8,128)S(1)} %collective-permute-done.65), channel_id=1, source_target_pairs={{0,2},{1,3},{2,0},{3,1},{4,6},{5,7},{6,4},{7,5},{8,10},{9,11},{10,... | collective-permute-start | bytes 196616 | tf_op jit(solution)/shard_map/cond/branch_2_fun/ppermute | solution.py:309
  102.4 3.5 %collective-permute-done.69 = f32[2,8,8,128]{3,2,1,0:T(8,128)S(1)} collective-permute-done((f32[2,8,8,128]{3,2,1,0:T(8,128)S(1)}, f32[2,8,8,128]{3,2,1,0:T(8,128)S(1)}, u32[]{:S(2)}, u32[]{:S(2)}) %collective-permute-start.69) | collective-permute-done | bytes 65568 | tf_op jit(solution)/shard_map/cond/branch_2_fun/ppermute | solution.py:309
  105.9 2.0 %collective-permute-start.71 = (f32[2,8,8,128]{3,2,1,0:T(8,128)S(1)}, f32[2,8,8,128]{3,2,1,0:T(8,128)S(1)}, u32[]{:S(2)}, u32[]{:S(2)}) collective-permute-start(f32[2,8,8,128]{3,2,1,0:T(8,128)S(1)} %select_select_fusion.29), channel_id=1, source_target_pairs={{0,4},{1,5},{2,6},{3,7},{4,0},{5,1},{6,2},{7,3},{8,12},{9,13},{10,... | collective-permute-start | bytes 196616 | tf_op jit(solution)/shard_map/cond/branch_2_fun/ppermute | solution.py:309
  108.2 2.1 %collective-permute-done.71 = f32[2,8,8,128]{3,2,1,0:T(8,128)S(1)} collective-permute-done((f32[2,8,8,128]{3,2,1,0:T(8,128)S(1)}, f32[2,8,8,128]{3,2,1,0:T(8,128)S(1)}, u32[]{:S(2)}, u32[]{:S(2)}) %collective-permute-start.71) | collective-permute-done | bytes 65568 | tf_op jit(solution)/shard_map/cond/branch_2_fun/ppermute | solution.py:309
  110.3 2.7 %collective-permute-done.70 = f32[2,8,16,128]{3,2,1,0:T(8,128)S(1)} collective-permute-done((f32[2,8,16,128]{3,2,1,0:T(8,128)S(1)}, f32[2,8,16,128]{3,2,1,0:T(8,128)S(1)}, u32[]{:S(2)}, u32[]{:S(2)}) %collective-permute-start.70) | collective-permute-done | bytes 131104 | tf_op jit(solution)/shard_map/cond/branch_2_fun/ppermute | solution.py:309
  (61 shorter events, 15.6 us)
Async XLA Ops:
  6.1 10.2 %collective-permute-start.48 = (f32[1,26,8,128]{3,2,1,0:T(8,128)S(1)}, f32[1,26,8,128]{3,2,1,0:T(8,128)S(1)}, u32[]{:S(2)}, u32[]{:S(2)}) collective-permute-start(f32[1,26,8,128]{3,2,1,0:T(8,128)S(1)} %bitcast.46), channel_id=1, source_target_pairs={{0,8},{1,9},{2,10},{3,11},{4,12},{5,13},{6,14},{7,15},{8,0},{9,1},... | collective-permute-start | bytes 319496 | tf_op jit(solution)/shard_map/cond/branch_2_fun/ppermute | solution.py:309
  16.3 8.1 %collective-permute-start.49 = (f32[2,26,8,128]{3,2,1,0:T(8,128)S(1)}, f32[2,26,8,128]{3,2,1,0:T(8,128)S(1)}, u32[]{:S(2)}, u32[]{:S(2)}) collective-permute-start(f32[2,26,8,128]{3,2,1,0:T(8,128)S(1)} %pad_maximum_fusion.11), channel_id=1, source_target_pairs={{0,4},{1,5},{2,6},{3,7},{4,0},{5,1},{6,2},{7,3},{8,12},{9,13},{10,... | collective-permute-start | bytes 638984 | tf_op jit(solution)/shard_map/cond/branch_2_fun/ppermute | solution.py:309
  24.5 12.8 %collective-permute-start.50 = (f32[4,26,8,128]{3,2,1,0:T(8,128)S(1)}, f32[4,26,8,128]{3,2,1,0:T(8,128)S(1)}, u32[]{:S(2)}, u32[]{:S(2)}) collective-permute-start(f32[4,26,8,128]{3,2,1,0:T(8,128)S(1)} %pad_maximum_fusion.10), channel_id=1, source_target_pairs={{0,2},{1,3},{2,0},{3,1},{4,6},{5,7},{6,4},{7,5},{8,10},{9,11},{10,... | collective-permute-start | bytes 1277960 | tf_op jit(solution)/shard_map/cond/branch_2_fun/ppermute | solution.py:309
  26.1 22.0 %collective-permute-start.51 = (f32[2,8,56,128]{3,2,1,0:T(8,128)S(1)}, f32[2,8,56,128]{3,2,1,0:T(8,128)S(1)}, u32[]{:S(2)}, u32[]{:S(2)}) collective-permute-start(f32[2,8,56,128]{3,2,1,0:T(8,128)S(1)} %interior.10), channel_id=1, source_target_pairs={{0,8},{1,9},{2,10},{3,11},{4,12},{5,13},{6,14},{7,15},{8,0},{9,1},... | collective-permute-start | bytes 1376264 | tf_op jit(solution)/shard_map/cond/branch_2_fun/ppermute | solution.py:309
  27.7 20.4 %collective-permute-start.52 = (f32[2,8,56,128]{3,2,1,0:T(8,128)S(1)}, f32[2,8,56,128]{3,2,1,0:T(8,128)S(1)}, u32[]{:S(2)}, u32[]{:S(2)}) collective-permute-start(f32[2,8,56,128]{3,2,1,0:T(8,128)S(1)} %interior.10), channel_id=1, source_target_pairs={{0,2},{1,3},{2,0},{3,1},{4,6},{5,7},{6,4},{7,5},{8,10},{9,11},{10,... | collective-permute-start | bytes 1376264 | tf_op jit(solution)/shard_map/cond/branch_2_fun/ppermute | solution.py:309
  48.1 4.6 %collective-permute-start.56 = (f32[8,26,8,128]{3,2,1,0:T(8,128)S(1)}, f32[8,26,8,128]{3,2,1,0:T(8,128)S(1)}, u32[]{:S(2)}, u32[]{:S(2)}) collective-permute-start(f32[8,26,8,128]{3,2,1,0:T(8,128)S(1)} %pad_maximum_fusion.9), channel_id=1, source_target_pairs={{0,1},{1,0},{2,3},{3,2},{4,5},{5,4},{6,7},{7,6},{8,9},{9,8},{10,11... | collective-permute-start | bytes 2555912 | tf_op jit(solution)/shard_map/cond/branch_2_fun/ppermute | solution.py:309
  48.1 18.5 %collective-permute-start.55 = (f32[2,8,56,128]{3,2,1,0:T(8,128)S(1)}, f32[2,8,56,128]{3,2,1,0:T(8,128)S(1)}, u32[]{:S(2)}, u32[]{:S(2)}) collective-permute-start(f32[2,8,56,128]{3,2,1,0:T(8,128)S(1)} %collective-permute-done.51), channel_id=1, source_target_pairs={{0,2},{1,3},{2,0},{3,1},{4,6},{5,7},{6,4},{7,5},{8,10},{9,11},{10,... | collective-permute-start | bytes 1376264 | tf_op jit(solution)/shard_map/cond/branch_2_fun/ppermute | solution.py:309
  48.7 14.3 %collective-permute-start.53 = (f32[2,8,32,128]{3,2,1,0:T(8,128)S(1)}, f32[2,8,32,128]{3,2,1,0:T(8,128)S(1)}, u32[]{:S(2)}, u32[]{:S(2)}) collective-permute-start(f32[2,8,32,128]{3,2,1,0:T(8,128)S(1)} %get-tuple-element.156), channel_id=1, source_target_pairs={{0,8},{1,9},{2,10},{3,11},{4,12},{5,13},{6,14},{7,15},{8,0},{9,1},... | collective-permute-start | bytes 786440 | tf_op jit(solution)/shard_map/cond/branch_2_fun/ppermute | solution.py:309
  49.0 17.7 %collective-permute-start.54 = (f32[2,8,32,128]{3,2,1,0:T(8,128)S(1)}, f32[2,8,32,128]{3,2,1,0:T(8,128)S(1)}, u32[]{:S(2)}, u32[]{:S(2)}) collective-permute-start(f32[2,8,32,128]{3,2,1,0:T(8,128)S(1)} %get-tuple-element.156), channel_id=1, source_target_pairs={{0,2},{1,3},{2,0},{3,1},{4,6},{5,7},{6,4},{7,5},{8,10},{9,11},{10,... | collective-permute-start | bytes 786440 | tf_op jit(solution)/shard_map/cond/branch_2_fun/ppermute | solution.py:309
  66.8 16.4 %collective-permute-start.60 = (f32[2,8,56,128]{3,2,1,0:T(8,128)S(1)}, f32[2,8,56,128]{3,2,1,0:T(8,128)S(1)}, u32[]{:S(2)}, u32[]{:S(2)}) collective-permute-start(f32[2,8,56,128]{3,2,1,0:T(8,128)S(1)} %select_select_fusion.21), channel_id=1, source_target_pairs={{0,4},{1,5},{2,6},{3,7},{4,0},{5,1},{6,2},{7,3},{8,12},{9,13},{10,... | collective-permute-start | bytes 1376264 | tf_op jit(solution)/shard_map/cond/branch_2_fun/ppermute | solution.py:309
  66.8 14.2 %collective-permute-start.59 = (f32[2,8,32,128]{3,2,1,0:T(8,128)S(1)}, f32[2,8,32,128]{3,2,1,0:T(8,128)S(1)}, u32[]{:S(2)}, u32[]{:S(2)}) collective-permute-start(f32[2,8,32,128]{3,2,1,0:T(8,128)S(1)} %collective-permute-done.53), channel_id=1, source_target_pairs={{0,2},{1,3},{2,0},{3,1},{4,6},{5,7},{6,4},{7,5},{8,10},{9,11},{10,... | collective-permute-start | bytes 786440 | tf_op jit(solution)/shard_map/cond/branch_2_fun/ppermute | solution.py:309
  67.4 13.5 %collective-permute-start.57 = (f32[2,8,24,128]{3,2,1,0:T(8,128)S(1)}, f32[2,8,24,128]{3,2,1,0:T(8,128)S(1)}, u32[]{:S(2)}, u32[]{:S(2)}) collective-permute-start(f32[2,8,24,128]{3,2,1,0:T(8,128)S(1)} %get-tuple-element.159), channel_id=1, source_target_pairs={{0,8},{1,9},{2,10},{3,11},{4,12},{5,13},{6,14},{7,15},{8,0},{9,1},... | collective-permute-start | bytes 589832 | tf_op jit(solution)/shard_map/cond/branch_2_fun/ppermute | solution.py:309
  69.9 11.1 %collective-permute-start.58 = (f32[2,8,24,128]{3,2,1,0:T(8,128)S(1)}, f32[2,8,24,128]{3,2,1,0:T(8,128)S(1)}, u32[]{:S(2)}, u32[]{:S(2)}) collective-permute-start(f32[2,8,24,128]{3,2,1,0:T(8,128)S(1)} %get-tuple-element.159), channel_id=1, source_target_pairs={{0,2},{1,3},{2,0},{3,1},{4,6},{5,7},{6,4},{7,5},{8,10},{9,11},{10,... | collective-permute-start | bytes 589832 | tf_op jit(solution)/shard_map/cond/branch_2_fun/ppermute | solution.py:309
  83.2 11.5 %collective-permute-start.61 = (f32[2,8,16,128]{3,2,1,0:T(8,128)S(1)}, f32[2,8,16,128]{3,2,1,0:T(8,128)S(1)}, u32[]{:S(2)}, u32[]{:S(2)}) collective-permute-start(f32[2,8,16,128]{3,2,1,0:T(8,128)S(1)} %get-tuple-element.166), channel_id=1, source_target_pairs={{0,8},{1,9},{2,10},{3,11},{4,12},{5,13},{6,14},{7,15},{8,0},{9,1},... | collective-permute-start | bytes 393224 | tf_op jit(solution)/shard_map/cond/branch_2_fun/ppermute | solution.py:309
  84.4 10.2 %collective-permute-start.62 = (f32[2,8,16,128]{3,2,1,0:T(8,128)S(1)}, f32[2,8,16,128]{3,2,1,0:T(8,128)S(1)}, u32[]{:S(2)}, u32[]{:S(2)}) collective-permute-start(f32[2,8,16,128]{3,2,1,0:T(8,128)S(1)} %get-tuple-element.166), channel_id=1, source_target_pairs={{0,2},{1,3},{2,0},{3,1},{4,6},{5,7},{6,4},{7,5},{8,10},{9,11},{10,... | collective-permute-start | bytes 393224 | tf_op jit(solution)/shard_map/cond/branch_2_fun/ppermute | solution.py:309
  85.0 9.0 %collective-permute-start.65 = (f32[2,8,8,128]{3,2,1,0:T(8,128)S(1)}, f32[2,8,8,128]{3,2,1,0:T(8,128)S(1)}, u32[]{:S(2)}, u32[]{:S(2)}) collective-permute-start(f32[2,8,8,128]{3,2,1,0:T(8,128)S(1)} %edges.5), channel_id=1, source_target_pairs={{0,8},{1,9},{2,10},{3,11},{4,12},{5,13},{6,14},{7,15},{8,0},{9,1},... | collective-permute-start | bytes 196616 | tf_op jit(solution)/shard_map/cond/branch_2_fun/ppermute | solution.py:309
  86.6 8.0 %collective-permute-start.66 = (f32[2,8,8,128]{3,2,1,0:T(8,128)S(1)}, f32[2,8,8,128]{3,2,1,0:T(8,128)S(1)}, u32[]{:S(2)}, u32[]{:S(2)}) collective-permute-start(f32[2,8,8,128]{3,2,1,0:T(8,128)S(1)} %edges.5), channel_id=1, source_target_pairs={{0,2},{1,3},{2,0},{3,1},{4,6},{5,7},{6,4},{7,5},{8,10},{9,11},{10,... | collective-permute-start | bytes 196616 | tf_op jit(solution)/shard_map/cond/branch_2_fun/ppermute | solution.py:309
  88.2 11.8 %collective-permute-start.64 = (f32[2,8,32,128]{3,2,1,0:T(8,128)S(1)}, f32[2,8,32,128]{3,2,1,0:T(8,128)S(1)}, u32[]{:S(2)}, u32[]{:S(2)}) collective-permute-start(f32[2,8,32,128]{3,2,1,0:T(8,128)S(1)} %select_select_fusion.23), channel_id=1, source_target_pairs={{0,4},{1,5},{2,6},{3,7},{4,0},{5,1},{6,2},{7,3},{8,12},{9,13},{10,... | collective-permute-start | bytes 786440 | tf_op jit(solution)/shard_map/cond/branch_2_fun/ppermute | solution.py:309
  94.0 6.1 %collective-permute-start.63 = (f32[2,8,24,128]{3,2,1,0:T(8,128)S(1)}, f32[2,8,24,128]{3,2,1,0:T(8,128)S(1)}, u32[]{:S(2)}, u32[]{:S(2)}) collective-permute-start(f32[2,8,24,128]{3,2,1,0:T(8,128)S(1)} %collective-permute-done.57), channel_id=1, source_target_pairs={{0,2},{1,3},{2,0},{3,1},{4,6},{5,7},{6,4},{7,5},{8,10},{9,11},{10,... | collective-permute-start | bytes 589832 | tf_op jit(solution)/shard_map/cond/branch_2_fun/ppermute | solution.py:309
  100.1 5.8 %collective-permute-start.68 = (f32[2,8,24,128]{3,2,1,0:T(8,128)S(1)}, f32[2,8,24,128]{3,2,1,0:T(8,128)S(1)}, u32[]{:S(2)}, u32[]{:S(2)}) collective-permute-start(f32[2,8,24,128]{3,2,1,0:T(8,128)S(1)} %select_select_fusion.25), channel_id=1, source_target_pairs={{0,4},{1,5},{2,6},{3,7},{4,0},{5,1},{6,2},{7,3},{8,12},{9,13},{10,... | collective-permute-start | bytes 589832 | tf_op jit(solution)/shard_map/cond/branch_2_fun/ppermute | solution.py:309
  100.2 5.7 %collective-permute-start.67 = (f32[2,8,16,128]{3,2,1,0:T(8,128)S(1)}, f32[2,8,16,128]{3,2,1,0:T(8,128)S(1)}, u32[]{:S(2)}, u32[]{:S(2)}) collective-permute-start(f32[2,8,16,128]{3,2,1,0:T(8,128)S(1)} %collective-permute-done.61), channel_id=1, source_target_pairs={{0,2},{1,3},{2,0},{3,1},{4,6},{5,7},{6,4},{7,5},{8,10},{9,11},{10,... | collective-permute-start | bytes 393224 | tf_op jit(solution)/shard_map/cond/branch_2_fun/ppermute | solution.py:309
  100.8 5.2 %collective-permute-start.69 = (f32[2,8,8,128]{3,2,1,0:T(8,128)S(1)}, f32[2,8,8,128]{3,2,1,0:T(8,128)S(1)}, u32[]{:S(2)}, u32[]{:S(2)}) collective-permute-start(f32[2,8,8,128]{3,2,1,0:T(8,128)S(1)} %collective-permute-done.65), channel_id=1, source_target_pairs={{0,2},{1,3},{2,0},{3,1},{4,6},{5,7},{6,4},{7,5},{8,10},{9,11},{10,... | collective-permute-start | bytes 196616 | tf_op jit(solution)/shard_map/cond/branch_2_fun/ppermute | solution.py:309
  105.9 4.3 %collective-permute-start.71 = (f32[2,8,8,128]{3,2,1,0:T(8,128)S(1)}, f32[2,8,8,128]{3,2,1,0:T(8,128)S(1)}, u32[]{:S(2)}, u32[]{:S(2)}) collective-permute-start(f32[2,8,8,128]{3,2,1,0:T(8,128)S(1)} %select_select_fusion.29), channel_id=1, source_target_pairs={{0,4},{1,5},{2,6},{3,7},{4,0},{5,1},{6,2},{7,3},{8,12},{9,13},{10,... | collective-permute-start | bytes 196616 | tf_op jit(solution)/shard_map/cond/branch_2_fun/ppermute | solution.py:309
  108.0 5.0 %collective-permute-start.70 = (f32[2,8,16,128]{3,2,1,0:T(8,128)S(1)}, f32[2,8,16,128]{3,2,1,0:T(8,128)S(1)}, u32[]{:S(2)}, u32[]{:S(2)}) collective-permute-start(f32[2,8,16,128]{3,2,1,0:T(8,128)S(1)} %select_select_fusion.27), channel_id=1, source_target_pairs={{0,4},{1,5},{2,6},{3,7},{4,0},{5,1},{6,2},{7,3},{8,12},{9,13},{10,... | collective-permute-start | bytes 393224 | tf_op jit(solution)/shard_map/cond/branch_2_fun/ppermute | solution.py:309
  (7 other events, 50.0 us)

commit v4 on v3

--- a/solution.py
+++ b/solution.py
@@ -32,20 +32,49 @@
     return jnp.maximum(v, 0.0), jnp.minimum(v, 0.0)
 
 
-def prepare_kernel(top, here_ref, neighbours_ref, migrate_ref, order_ref, rates_ref, u_ref, k_ref, plan_ref, own_ref, sent_ref):
+def prepare_kernel(
+    top,
+    here_ref,
+    neighbours_hbm,
+    migrate_hbm,
+    order_hbm,
+    rates_hbm,
+    u_hbm,
+    k_hbm,
+    branch_ref,
+    plan_ref,
+    own_ref,
+    sent_ref,
+    neighbours_ref,
+    migrate_ref,
+    order_ref,
+    rates_ref,
+    u_ref,
+    k_ref,
+    sems,
+):
+    pairs = (
+        (neighbours_hbm, neighbours_ref),
+        (migrate_hbm, migrate_ref),
+        (order_hbm, order_ref),
+        (rates_hbm, rates_ref),
+        (u_hbm, u_ref),
+        (k_hbm, k_ref),
+    )
+    copies = [pltpu.make_async_copy(src, dst, sems.at[n]) for n, (src, dst) in enumerate(pairs)]
+    for copy in copies:
+        copy.start()
+    for copy in copies:
+        copy.wait()
     here = here_ref[0]
     for side in range(2):
-        beside = neighbours_ref[here, side]
-        apart = jnp.bitwise_xor(jnp.maximum(beside, 0), here)
-        spot = jnp.int32(0)
-        for bit in range(top + 1):
-            spot = spot | (((apart >> bit) & 1) << (top - bit))
-        plan_ref[side] = spot
+        beside = neighbours_ref[side, here]
+        plan_ref[side] = jnp.bitwise_xor(jnp.maximum(beside, 0), here)
         plan_ref[2 + side] = (beside >= 0).astype(jnp.int32)
     order = [order_ref[r] for r in range(ROUNDS)]
     low = jnp.minimum(jnp.minimum(order[0], order[1]), order[2])
     high = order[0] + order[1] + order[2] - top - low
-    plan_ref[4] = ((low * (2 * top - 1 - low)) >> 1) + high - low - 1
+    branch_ref[0] = ((low * (2 * top - 1 - low)) >> 1) + high - low - 1
 
     def source(slot):
         for r in reversed(range(ROUNDS)):
@@ -304,9 +333,16 @@
         begin += rows
 
 
+def swap_mask(block, mask):
+    return lax.ppermute(block, AXES, [(slot, slot ^ mask) for slot in range(lax.axis_size(AXES))])
+
+
 def swap(block, bit):
-    count = lax.axis_size(AXES)
-    return lax.ppermute(block, AXES, [(low, low ^ 1 << bit) for low in range(count)])
+    return swap_mask(block, 1 << bit)
+
+
+def swap_both(block, first, second):
+    return swap_mask(block, 1 << first | 1 << second)
 
 
 def pick(index, options):
@@ -344,11 +380,18 @@
     )(velocity, rates, field, kappa)
 
 
-def edge_call(plan, velocity, rates, gathered, own):
+def edge_call(plan, velocity, rates, gathered, own, bits):
     f32 = jnp.float32
     species = 2
     depth = own.shape[1]
     tiles = gathered.shape[1]
+
+    def spot(apart):
+        place = 0
+        for n, bit in enumerate(bits):
+            place = place | (((apart >> bit) & 1) << n)
+        return place
+
     return pl.pallas_call(
         edge_kernel,
         out_shape=jax.ShapeDtypeStruct((species, depth, ROWS, LANES), f32),
@@ -358,8 +401,8 @@
             in_specs=[
                 SMEM,
                 SMEM,
-                pl.BlockSpec((1, tiles, ROWS, LANES), lambda i, plan: (plan[0], 0, 0, 0)),
-                pl.BlockSpec((1, tiles, ROWS, LANES), lambda i, plan: (plan[1], 0, 0, 0)),
+                pl.BlockSpec((1, tiles, ROWS, LANES), lambda i, plan: (spot(plan[0]), 0, 0, 0)),
+                pl.BlockSpec((1, tiles, ROWS, LANES), lambda i, plan: (spot(plan[1]), 0, 0, 0)),
                 VMEM,
             ],
             out_specs=pl.BlockSpec((species, depth, ROWS, LANES), lambda i, plan: (0, 0, 0, 0)),
@@ -384,7 +427,10 @@
 
 def run(low, high, top, field, kappa, rates, velocity, plan, own, sent):
     blocks = field.shape[2] // ROWS
-    cuts = (blocks * 7 // 16, blocks // 4, blocks * 3 // 16, blocks // 8)
+    cuts = (blocks // 4,) * 4
+    middle = [bit for bit in reversed(range(1, top)) if bit != low]
+    if low:
+        middle.insert(0, low)
     give = partial(pick, plan[5])
     keep = partial(pick, plan[6])
 
@@ -395,27 +441,26 @@
     (p0,) = interior_call(0, cuts[:1], velocity, rates, field, kappa)
     p0, strips, field = order(p0, strips, field)
     n0, a0 = swap(p0, top), swap(p0, low)
+    strips = double(strips, middle[0])
     p1, p2, p3 = interior_call(cuts[0], cuts[1:], velocity, rates, field, kappa)
-    for bit in reversed(range(1, top)):
-        strips = double(strips, bit)
-        p1, strips = order(p1, strips)
     p1, p2, p3, n0, a0, strips = order(p1, p2, p3, n0, a0, strips)
     n1, a1, f0 = swap(p1, top), swap(p1, low), swap(n0, low)
-    strips = double(strips, 0)
+    for bit in middle[1:]:
+        strips = double(strips, bit)
     p2, n1, a1, f0, strips = order(p2, n1, a1, f0, strips)
     o0 = (p0, n0, a0, f0)
     n2, a2, f1, h0 = swap(p2, top), swap(p2, low), swap(n1, low), swap(give(o0), high)
-    edges = edge_call(plan, velocity, rates, strips, own)
-    p3, n2, a2, f1, h0, edges = order(p3, n2, a2, f1, h0, edges)
+    strips = double(strips, 0)
+    p3, n2, a2, f1, h0, strips = order(p3, n2, a2, f1, h0, strips)
     o1 = (p1, n1, a1, f1)
     n3, a3, f2, h1 = swap(p3, top), swap(p3, low), swap(n2, low), swap(give(o1), high)
-    en, ea = swap(edges, top), swap(edges, low)
-    n3, a3, f2, h1, en, ea = order(n3, a3, f2, h1, en, ea)
+    edges = edge_call(plan, velocity, rates, strips, own, [top, *middle, 0])
+    n3, a3, f2, h1, edges = order(n3, a3, f2, h1, edges)
     o2 = (p2, n2, a2, f2)
-    f3, h2, ef = swap(n3, low), swap(give(o2), high), swap(en, low)
-    f3, h2, ef = order(f3, h2, ef)
+    f3, h2 = swap(n3, low), swap(give(o2), high)
+    oe = (edges, swap(edges, top), swap(edges, low), swap_both(edges, top, low))
+    f3, h2, *oe = order(f3, h2, *oe)
     o3 = (p3, n3, a3, f3)
-    oe = (edges, en, ea, ef)
     h3, eh = swap(give(o3), high), swap(give(oe), high)
     parts = [result(*pair) for pair in ((o0, h0), (o1, h1), (o2, h2), (o3, h3), (oe, eh))]
     return pl.pallas_call(
@@ -434,20 +479,30 @@
     kappa = diffusivity[0]
     depth = kappa.shape[0]
     here = lax.axis_index(AXES).astype(jnp.int32).reshape(1)
-    plan, own, sent = pl.pallas_call(
+    branch, plan, own, sent = pl.pallas_call(
         partial(prepare_kernel, top),
         out_shape=(
+            jax.ShapeDtypeStruct((1,), jnp.int32),
             jax.ShapeDtypeStruct((8,), jnp.int32),
             jax.ShapeDtypeStruct((3, depth, 16, LANES), jnp.float32),
             jax.ShapeDtypeStruct((3 * depth + 2, ROWS, LANES), jnp.float32),
         ),
-        in_specs=[SMEM] * 5 + [VMEM] * 2,
-        out_specs=(SMEM, VMEM, VMEM),
-        compiler_params=PARAMS,
+        in_specs=[SMEM] + [pl.BlockSpec(memory_space=pl.ANY)] * 6,
+        out_specs=(SMEM, SMEM, VMEM, VMEM),
+        scratch_shapes=[
+            pltpu.SMEM(neighbours.shape[::-1], jnp.int32),
+            pltpu.SMEM(migrate.shape, jnp.int32),
+            pltpu.SMEM(bit_order.shape, jnp.int32),
+            pltpu.SMEM(rates.shape, jnp.float32),
+            pltpu.VMEM(field.shape, jnp.float32),
+            pltpu.VMEM(kappa.shape, jnp.float32),
+            pltpu.SemaphoreType.DMA((6,)),
+        ],
+        compiler_params=pltpu.CompilerParams(vmem_limit_bytes=60 * 2**20),
         name="prepare",
-    )(here, neighbours, migrate, bit_order, rates, field, kappa)
+    )(here, neighbours.T, migrate, bit_order, rates, field, kappa)
     branches = [partial(run, low, high, top) for low, high in combinations(range(top), 2)]
-    final = lax.switch(plan[4], branches, field, kappa, rates, velocity, plan, own, sent)
+    final = lax.switch(branch[0], branches, field, kappa, rates, velocity, plan, own, sent)
     return final.reshape(concentration.shape)
 
 

time: 114 us -> 102 us (0.89)
  waiting for transfers between devices: 55.6 us -> 44 us
  local copies, waits for them, and re-layouts: 4.31 us -> 1.66 us
  starting transfers between devices: 26.9 us -> 28.2 us
    ppermute x24, waiting for transfers between devices: 55.6 us -> 44 us  [swap_mask(): lax.ppermute(block, AXES, [(slot, slot ^ mask) for slot in range(lax.axis...]
    unnamed x7 -> x2, local copies, waits for them, and re-layouts: 3.06 us -> 0.96 us
    ppermute x24, starting transfers between devices: 26.9 us -> 28.2 us  [swap_mask(): lax.ppermute(block, AXES, [(slot, slot ^ mask) for slot in range(lax.axis...]
  transfers between devices with their start and end apart: 24 -> 24, of which waited for: 11 -> 12; matrix products, arithmetic and copies ran while one was open for 1% -> 2% of each run, Pallas kernels for 16% -> 18%
where the time goes in v4:
time: 102 us
  waiting for transfers between devices  44 us (43%)
  starting transfers between devices  28.2 us (28%)
  Pallas kernels  21.4 us (21%)
  loops' own time  4.96 us (5%)
  local copies, waits for them, and re-layouts  1.66 us (2%)
  other arithmetic  1.06 us (1%)
    ppermute x24, waiting for transfers between devices, swap_mask(): lax.ppermute(block, AXES, [(slot, slot ^ mask) for slot in range(lax.axis...  44 us
    ppermute x24, starting transfers between devices, swap_mask(): lax.ppermute(block, AXES, [(slot, slot ^ mask) for slot in range(lax.axis...  28.2 us
    pallas_call x2, Pallas kernels, interior_call(): pl.pallas_call(partial(interior_kernel, first, cuts), out_shape=[jax.Shap...  12.6 us
    pallas_call x1, Pallas kernels, edge_call(): pl.pallas_call(edge_kernel, out_shape=jax.ShapeDtypeStruct((species, dept...  5.87 us
    another operation x1, loops' own time, per_device(): lax.switch(branch[0], branches, field, kappa, rates, velocity, plan, own,...  4.96 us
    pallas_call x1, Pallas kernels, per_device(): pl.pallas_call(partial(prepare_kernel, top), out_shape=(jax.ShapeDtypeStr...  2.52 us
  transfers between devices with their start and end apart: 24, of which 12 were waited for; matrix products, arithmetic and copies ran while one was open for 2% of the time, Pallas kernels for 18%

profile of v4, /device:TPU:0, one launch (start us, length us, event | category | flops | bytes accessed | tf_op | source)
XLA Modules:
  0.0 101.9 jit_solution(11135898808040111785)
XLA Ops:
  0.0 2.5 %prepare.1 = (s32[1]{0:T(128)}, s32[8]{0:T(128)S(1)}, f32[3,8,16,128]{3,2,1,0:T(8,128)S(1)}, f32[26,8,128]{2,1,0:T(8,128)S(1)}) custom-call(s32[1]{0:T(128)} %bitcast.27.here_ref, s32[2,16]{1,0:T(2,128)} %bitcast.49, s32[3,16]{1,0:T(4,128)} %migrate_hbm.1, s32[3]{0:T(128)} %order_hbm.1, f32[1,2]{1,0:T(1,128)} %rates_hbm.1, f32[2,8,128,128]{3,2,1,0:T(8,128)} %bitcast.32, ...), custom_call_target="tpu_custom_call" | custom-call | tf_op jit(solution)/shard_map/prepare/pallas_call | solution.py:482
  3.1 97.8 %conditional.1 = (f32[1,2,8,128,128]{4,3,2,1,0:T(8,128)S(1)}) conditional(s32[]{:T(128)} %bitcast.31, (s32[8]{0:T(128)S(1)}, f32[2,3]{1,0:T(2,128)}, f32[1,2]{1,0:T(1,128)}, f32[2,8,128,128]{3,2,1,0:T(8,128)}, f32[8,128,128]{2,1,0:T(8,128)}, /*index=5*/f32[26,8,128]{2,1,0:T(8,128)S(1)}, f32[3,8,16,128]{3,2,1,0:T(8,128)S(1)}) %tuple.51, ...), branch_computations={%region_0.1_spmd, %region_1.2_spmd, %region_2.3_spmd} | conditional | flops 82748416 | bytes 69153336 | solution.py:505
  3.4 4.1 %collective-permute-start.48 = (f32[1,26,8,128]{3,2,1,0:T(8,128)S(1)}, f32[1,26,8,128]{3,2,1,0:T(8,128)S(1)}, u32[]{:S(2)}, u32[]{:S(2)}) collective-permute-start(f32[1,26,8,128]{3,2,1,0:T(8,128)S(1)} %bitcast.47), channel_id=1, source_target_pairs={{0,8},{1,9},{2,10},{3,11},{4,12},{5,13},{6,14},{7,15},{8,0},{9,1},... | collective-permute-start | bytes 319496 | tf_op jit(solution)/shard_map/cond/branch_2_fun/ppermute | solution.py:337
  7.5 4.3 %interior.10 = f32[2,8,32,128]{3,2,1,0:T(8,128)S(1)} custom-call(f32[2,3]{1,0:T(2,128)} %get-tuple-element.135.velocity_ref, f32[1,2]{1,0:T(1,128)} %get-tuple-element.136.rates_ref, f32[2,8,128,128]{3,2,1,0:T(8,128)} %get-tuple-element.140.u_ref, f32[8,128,128]{2,1,0:T(8,128)} %get-tuple-element.138.k_ref), custom_call_target="tpu_custom_call" | custom-call | flops 40000000 | bytes 10000000 | tf_op jit(solution)/shard_map/cond/branch_2_fun/interior/pallas_call | solution.py:363
  12.8 1.6 %collective-permute-start.51 = (f32[2,26,8,128]{3,2,1,0:T(8,128)S(1)}, f32[2,26,8,128]{3,2,1,0:T(8,128)S(1)}, u32[]{:S(2)}, u32[]{:S(2)}) collective-permute-start(f32[2,26,8,128]{3,2,1,0:T(8,128)S(1)} %pad_maximum_fusion.11), channel_id=1, source_target_pairs={{0,2},{1,3},{2,0},{3,1},{4,6},{5,7},{6,4},{7,5},{8,10},{9,11},{10,... | collective-permute-start | bytes 638984 | tf_op jit(solution)/shard_map/cond/branch_2_fun/ppermute | solution.py:337
  15.3 8.3 %interior.11 = (f32[2,8,32,128]{3,2,1,0:T(8,128)S(1)}, f32[2,8,32,128]{3,2,1,0:T(8,128)S(1)}, f32[2,8,32,128]{3,2,1,0:T(8,128)S(1)}) custom-call(f32[2,3]{1,0:T(2,128)S(1)} %copy-done.9, f32[1,2]{1,0:T(1,128)S(1)} %copy-done.12, f32[2,8,128,128]{3,2,1,0:T(8,128)S(1)} %copy-done.2, f32[8,128,128]{2,1,0:T(8,128)S(1)} %copy-done.5), custom_call_target="tpu_custom_call" | custom-call | flops 40000000 | bytes 10000000 | tf_op jit(solution)/shard_map/cond/branch_2_fun/interior/pallas_call | solution.py:363
  23.7 4.2 %collective-permute-done.49 = f32[2,8,32,128]{3,2,1,0:T(8,128)S(1)} collective-permute-done((f32[2,8,32,128]{3,2,1,0:T(8,128)S(1)}, f32[2,8,32,128]{3,2,1,0:T(8,128)S(1)}, u32[]{:S(2)}, u32[]{:S(2)}) %collective-permute-start.49) | collective-permute-done | bytes 262176 | tf_op jit(solution)/shard_map/cond/branch_2_fun/ppermute | solution.py:337
  27.8 1.9 %collective-permute-start.52 = (f32[2,8,32,128]{3,2,1,0:T(8,128)S(1)}, f32[2,8,32,128]{3,2,1,0:T(8,128)S(1)}, u32[]{:S(2)}, u32[]{:S(2)}) collective-permute-start(f32[2,8,32,128]{3,2,1,0:T(8,128)S(1)} %get-tuple-element.148), channel_id=1, source_target_pairs={{0,8},{1,9},{2,10},{3,11},{4,12},{5,13},{6,14},{7,15},{8,0},{9,1},... | collective-permute-start | bytes 786440 | tf_op jit(solution)/shard_map/cond/branch_2_fun/ppermute | solution.py:337
  29.7 1.5 %collective-permute-start.53 = (f32[2,8,32,128]{3,2,1,0:T(8,128)S(1)}, f32[2,8,32,128]{3,2,1,0:T(8,128)S(1)}, u32[]{:S(2)}, u32[]{:S(2)}) collective-permute-start(f32[2,8,32,128]{3,2,1,0:T(8,128)S(1)} %get-tuple-element.148), channel_id=1, source_target_pairs={{0,2},{1,3},{2,0},{3,1},{4,6},{5,7},{6,4},{7,5},{8,10},{9,11},{10,... | collective-permute-start | bytes 786440 | tf_op jit(solution)/shard_map/cond/branch_2_fun/ppermute | solution.py:337
  31.8 11.5 %collective-permute-done.55 = f32[4,26,8,128]{3,2,1,0:T(8,128)S(1)} collective-permute-done((f32[4,26,8,128]{3,2,1,0:T(8,128)S(1)}, f32[4,26,8,128]{3,2,1,0:T(8,128)S(1)}, u32[]{:S(2)}, u32[]{:S(2)}) %collective-permute-start.55) | collective-permute-done | bytes 426016 | tf_op jit(solution)/shard_map/cond/branch_2_fun/ppermute | solution.py:337
  46.2 1.9 %collective-permute-start.59 = (f32[2,8,32,128]{3,2,1,0:T(8,128)S(1)}, f32[2,8,32,128]{3,2,1,0:T(8,128)S(1)}, u32[]{:S(2)}, u32[]{:S(2)}) collective-permute-start(f32[2,8,32,128]{3,2,1,0:T(8,128)S(1)} %select_select_fusion.27), channel_id=1, source_target_pairs={{0,4},{1,5},{2,6},{3,7},{4,0},{5,1},{6,2},{7,3},{8,12},{9,13},{10,... | collective-permute-start | bytes 786440 | tf_op jit(solution)/shard_map/cond/branch_2_fun/ppermute | solution.py:337
  48.1 1.9 %collective-permute-start.56 = (f32[2,8,32,128]{3,2,1,0:T(8,128)S(1)}, f32[2,8,32,128]{3,2,1,0:T(8,128)S(1)}, u32[]{:S(2)}, u32[]{:S(2)}) collective-permute-start(f32[2,8,32,128]{3,2,1,0:T(8,128)S(1)} %get-tuple-element.151), channel_id=1, source_target_pairs={{0,8},{1,9},{2,10},{3,11},{4,12},{5,13},{6,14},{7,15},{8,0},{9,1},... | collective-permute-start | bytes 786440 | tf_op jit(solution)/shard_map/cond/branch_2_fun/ppermute | solution.py:337
  50.8 1.2 %collective-permute-start.58 = (f32[2,8,32,128]{3,2,1,0:T(8,128)S(1)}, f32[2,8,32,128]{3,2,1,0:T(8,128)S(1)}, u32[]{:S(2)}, u32[]{:S(2)}) collective-permute-start(f32[2,8,32,128]{3,2,1,0:T(8,128)S(1)} %collective-permute-done.52), channel_id=1, source_target_pairs={{0,2},{1,3},{2,0},{3,1},{4,6},{5,7},{6,4},{7,5},{8,10},{9,11},{10,... | collective-permute-start | bytes 786440 | tf_op jit(solution)/shard_map/cond/branch_2_fun/ppermute | solution.py:337
  54.4 5.3 %collective-permute-done.59 = f32[2,8,32,128]{3,2,1,0:T(8,128)S(1)} collective-permute-done((f32[2,8,32,128]{3,2,1,0:T(8,128)S(1)}, f32[2,8,32,128]{3,2,1,0:T(8,128)S(1)}, u32[]{:S(2)}, u32[]{:S(2)}) %collective-permute-start.59) | collective-permute-done | bytes 262176 | tf_op jit(solution)/shard_map/cond/branch_2_fun/ppermute | solution.py:337
  59.7 3.4 %collective-permute-done.56 = f32[2,8,32,128]{3,2,1,0:T(8,128)S(1)} collective-permute-done((f32[2,8,32,128]{3,2,1,0:T(8,128)S(1)}, f32[2,8,32,128]{3,2,1,0:T(8,128)S(1)}, u32[]{:S(2)}, u32[]{:S(2)}) %collective-permute-start.56) | collective-permute-done | bytes 262176 | tf_op jit(solution)/shard_map/cond/branch_2_fun/ppermute | solution.py:337
  67.5 5.9 %edges.5 = f32[2,8,8,128]{3,2,1,0:T(8,128)S(1)} custom-call(s32[8]{0:T(128)S(1)} %get-tuple-element.134.plan_ref, f32[2,3]{1,0:T(2,128)S(1)} %copy-done.9, f32[1,2]{1,0:T(1,128)S(1)} %copy-done.12, f32[16,26,8,128]{3,2,1,0:T(8,128)S(1)} %pad_maximum_fusion.8.left_ref.right_ref, f32[16,26,8,128]{3,2,1,0:T(8,128)S(1)} %pad_maximum_fusion.8.left_ref.right_ref, ...), custom_call_target="tpu_custom_call" | custom-call | tf_op jit(solution)/shard_map/cond/branch_2_fun/edges/pallas_call | solution.py:395
  73.5 4.4 %collective-permute-done.64 = f32[2,8,32,128]{3,2,1,0:T(8,128)S(1)} collective-permute-done((f32[2,8,32,128]{3,2,1,0:T(8,128)S(1)}, f32[2,8,32,128]{3,2,1,0:T(8,128)S(1)}, u32[]{:S(2)}, u32[]{:S(2)}) %collective-permute-start.64) | collective-permute-done | bytes 262176 | tf_op jit(solution)/shard_map/cond/branch_2_fun/ppermute | solution.py:337
  77.9 1.4 %collective-permute-start.67 = (f32[2,8,8,128]{3,2,1,0:T(8,128)S(1)}, f32[2,8,8,128]{3,2,1,0:T(8,128)S(1)}, u32[]{:S(2)}, u32[]{:S(2)}) collective-permute-start(f32[2,8,8,128]{3,2,1,0:T(8,128)S(1)} %edges.5), channel_id=1, source_target_pairs={{0,8},{1,9},{2,10},{3,11},{4,12},{5,13},{6,14},{7,15},{8,0},{9,1},... | collective-permute-start | bytes 196616 | tf_op jit(solution)/shard_map/cond/branch_2_fun/ppermute | solution.py:337
  80.1 2.2 %collective-permute-start.69 = (f32[2,8,8,128]{3,2,1,0:T(8,128)S(1)}, f32[2,8,8,128]{3,2,1,0:T(8,128)S(1)}, u32[]{:S(2)}, u32[]{:S(2)}) collective-permute-start(f32[2,8,8,128]{3,2,1,0:T(8,128)S(1)} %edges.5), channel_id=1, source_target_pairs={{0,10},{1,11},{2,8},{3,9},{4,14},{5,15},{6,12},{7,13},{8,2},{9,3},... | collective-permute-start | bytes 196616 | tf_op jit(solution)/shard_map/cond/branch_2_fun/ppermute | solution.py:337
  85.2 1.5 %collective-permute-done.69 = f32[2,8,8,128]{3,2,1,0:T(8,128)S(1)} collective-permute-done((f32[2,8,8,128]{3,2,1,0:T(8,128)S(1)}, f32[2,8,8,128]{3,2,1,0:T(8,128)S(1)}, u32[]{:S(2)}, u32[]{:S(2)}) %collective-permute-start.69) | collective-permute-done | bytes 65568 | tf_op jit(solution)/shard_map/cond/branch_2_fun/ppermute | solution.py:337
  86.7 4.4 %collective-permute-done.66 = f32[2,8,32,128]{3,2,1,0:T(8,128)S(1)} collective-permute-done((f32[2,8,32,128]{3,2,1,0:T(8,128)S(1)}, f32[2,8,32,128]{3,2,1,0:T(8,128)S(1)}, u32[]{:S(2)}, u32[]{:S(2)}) %collective-permute-start.66) | collective-permute-done | bytes 262176 | tf_op jit(solution)/shard_map/cond/branch_2_fun/ppermute | solution.py:337
  92.0 1.3 %collective-permute-start.70 = (f32[2,8,32,128]{3,2,1,0:T(8,128)S(1)}, f32[2,8,32,128]{3,2,1,0:T(8,128)S(1)}, u32[]{:S(2)}, u32[]{:S(2)}) collective-permute-start(f32[2,8,32,128]{3,2,1,0:T(8,128)S(1)} %select_select_fusion.21), channel_id=1, source_target_pairs={{0,4},{1,5},{2,6},{3,7},{4,0},{5,1},{6,2},{7,3},{8,12},{9,13},{10,... | collective-permute-start | bytes 786440 | tf_op jit(solution)/shard_map/cond/branch_2_fun/ppermute | solution.py:337
  93.5 2.7 %collective-permute-done.71 = f32[2,8,8,128]{3,2,1,0:T(8,128)S(1)} collective-permute-done((f32[2,8,8,128]{3,2,1,0:T(8,128)S(1)}, f32[2,8,8,128]{3,2,1,0:T(8,128)S(1)}, u32[]{:S(2)}, u32[]{:S(2)}) %collective-permute-start.71) | collective-permute-done | bytes 65568 | tf_op jit(solution)/shard_map/cond/branch_2_fun/ppermute | solution.py:337
  96.2 3.9 %collective-permute-done.70 = f32[2,8,32,128]{3,2,1,0:T(8,128)S(1)} collective-permute-done((f32[2,8,32,128]{3,2,1,0:T(8,128)S(1)}, f32[2,8,32,128]{3,2,1,0:T(8,128)S(1)}, u32[]{:S(2)}, u32[]{:S(2)}) %collective-permute-start.70) | collective-permute-done | bytes 262176 | tf_op jit(solution)/shard_map/cond/branch_2_fun/ppermute | solution.py:337
  (55 shorter events, 15.1 us)
Async XLA Ops:
  3.4 9.4 %collective-permute-start.48 = (f32[1,26,8,128]{3,2,1,0:T(8,128)S(1)}, f32[1,26,8,128]{3,2,1,0:T(8,128)S(1)}, u32[]{:S(2)}, u32[]{:S(2)}) collective-permute-start(f32[1,26,8,128]{3,2,1,0:T(8,128)S(1)} %bitcast.47), channel_id=1, source_target_pairs={{0,8},{1,9},{2,10},{3,11},{4,12},{5,13},{6,14},{7,15},{8,0},{9,1},... | collective-permute-start | bytes 319496 | tf_op jit(solution)/shard_map/cond/branch_2_fun/ppermute | solution.py:337
  12.8 10.8 %collective-permute-start.51 = (f32[2,26,8,128]{3,2,1,0:T(8,128)S(1)}, f32[2,26,8,128]{3,2,1,0:T(8,128)S(1)}, u32[]{:S(2)}, u32[]{:S(2)}) collective-permute-start(f32[2,26,8,128]{3,2,1,0:T(8,128)S(1)} %pad_maximum_fusion.11), channel_id=1, source_target_pairs={{0,2},{1,3},{2,0},{3,1},{4,6},{5,7},{6,4},{7,5},{8,10},{9,11},{10,... | collective-permute-start | bytes 638984 | tf_op jit(solution)/shard_map/cond/branch_2_fun/ppermute | solution.py:337
  14.4 13.4 %collective-permute-start.49 = (f32[2,8,32,128]{3,2,1,0:T(8,128)S(1)}, f32[2,8,32,128]{3,2,1,0:T(8,128)S(1)}, u32[]{:S(2)}, u32[]{:S(2)}) collective-permute-start(f32[2,8,32,128]{3,2,1,0:T(8,128)S(1)} %interior.10), channel_id=1, source_target_pairs={{0,8},{1,9},{2,10},{3,11},{4,12},{5,13},{6,14},{7,15},{8,0},{9,1},... | collective-permute-start | bytes 786440 | tf_op jit(solution)/shard_map/cond/branch_2_fun/ppermute | solution.py:337
  14.8 13.0 %collective-permute-start.50 = (f32[2,8,32,128]{3,2,1,0:T(8,128)S(1)}, f32[2,8,32,128]{3,2,1,0:T(8,128)S(1)}, u32[]{:S(2)}, u32[]{:S(2)}) collective-permute-start(f32[2,8,32,128]{3,2,1,0:T(8,128)S(1)} %interior.10), channel_id=1, source_target_pairs={{0,2},{1,3},{2,0},{3,1},{4,6},{5,7},{6,4},{7,5},{8,10},{9,11},{10,... | collective-permute-start | bytes 786440 | tf_op jit(solution)/shard_map/cond/branch_2_fun/ppermute | solution.py:337
  27.8 15.4 %collective-permute-start.55 = (f32[4,26,8,128]{3,2,1,0:T(8,128)S(1)}, f32[4,26,8,128]{3,2,1,0:T(8,128)S(1)}, u32[]{:S(2)}, u32[]{:S(2)}) collective-permute-start(f32[4,26,8,128]{3,2,1,0:T(8,128)S(1)} %pad_maximum_fusion.10), channel_id=1, source_target_pairs={{0,4},{1,5},{2,6},{3,7},{4,0},{5,1},{6,2},{7,3},{8,12},{9,13},{10,... | collective-permute-start | bytes 1277960 | tf_op jit(solution)/shard_map/cond/branch_2_fun/ppermute | solution.py:337
  27.8 15.5 %collective-permute-start.52 = (f32[2,8,32,128]{3,2,1,0:T(8,128)S(1)}, f32[2,8,32,128]{3,2,1,0:T(8,128)S(1)}, u32[]{:S(2)}, u32[]{:S(2)}) collective-permute-start(f32[2,8,32,128]{3,2,1,0:T(8,128)S(1)} %get-tuple-element.148), channel_id=1, source_target_pairs={{0,8},{1,9},{2,10},{3,11},{4,12},{5,13},{6,14},{7,15},{8,0},{9,1},... | collective-permute-start | bytes 786440 | tf_op jit(solution)/shard_map/cond/branch_2_fun/ppermute | solution.py:337
  29.7 13.6 %collective-permute-start.53 = (f32[2,8,32,128]{3,2,1,0:T(8,128)S(1)}, f32[2,8,32,128]{3,2,1,0:T(8,128)S(1)}, u32[]{:S(2)}, u32[]{:S(2)}) collective-permute-start(f32[2,8,32,128]{3,2,1,0:T(8,128)S(1)} %get-tuple-element.148), channel_id=1, source_target_pairs={{0,2},{1,3},{2,0},{3,1},{4,6},{5,7},{6,4},{7,5},{8,10},{9,11},{10,... | collective-permute-start | bytes 786440 | tf_op jit(solution)/shard_map/cond/branch_2_fun/ppermute | solution.py:337
  31.2 12.1 %collective-permute-start.54 = (f32[2,8,32,128]{3,2,1,0:T(8,128)S(1)}, f32[2,8,32,128]{3,2,1,0:T(8,128)S(1)}, u32[]{:S(2)}, u32[]{:S(2)}) collective-permute-start(f32[2,8,32,128]{3,2,1,0:T(8,128)S(1)} %collective-permute-done.49), channel_id=1, source_target_pairs={{0,2},{1,3},{2,0},{3,1},{4,6},{5,7},{6,4},{7,5},{8,10},{9,11},{10,... | collective-permute-start | bytes 786440 | tf_op jit(solution)/shard_map/cond/branch_2_fun/ppermute | solution.py:337
  43.3 11.0 %collective-permute-start.60 = (f32[8,26,8,128]{3,2,1,0:T(8,128)S(1)}, f32[8,26,8,128]{3,2,1,0:T(8,128)S(1)}, u32[]{:S(2)}, u32[]{:S(2)}) collective-permute-start(f32[8,26,8,128]{3,2,1,0:T(8,128)S(1)} %pad_maximum_fusion.9), channel_id=1, source_target_pairs={{0,1},{1,0},{2,3},{3,2},{4,5},{5,4},{6,7},{7,6},{8,9},{9,8},{10,11... | collective-permute-start | bytes 2555912 | tf_op jit(solution)/shard_map/cond/branch_2_fun/ppermute | solution.py:337
  46.2 13.5 %collective-permute-start.59 = (f32[2,8,32,128]{3,2,1,0:T(8,128)S(1)}, f32[2,8,32,128]{3,2,1,0:T(8,128)S(1)}, u32[]{:S(2)}, u32[]{:S(2)}) collective-permute-start(f32[2,8,32,128]{3,2,1,0:T(8,128)S(1)} %select_select_fusion.27), channel_id=1, source_target_pairs={{0,4},{1,5},{2,6},{3,7},{4,0},{5,1},{6,2},{7,3},{8,12},{9,13},{10,... | collective-permute-start | bytes 786440 | tf_op jit(solution)/shard_map/cond/branch_2_fun/ppermute | solution.py:337
  48.1 15.0 %collective-permute-start.56 = (f32[2,8,32,128]{3,2,1,0:T(8,128)S(1)}, f32[2,8,32,128]{3,2,1,0:T(8,128)S(1)}, u32[]{:S(2)}, u32[]{:S(2)}) collective-permute-start(f32[2,8,32,128]{3,2,1,0:T(8,128)S(1)} %get-tuple-element.151), channel_id=1, source_target_pairs={{0,8},{1,9},{2,10},{3,11},{4,12},{5,13},{6,14},{7,15},{8,0},{9,1},... | collective-permute-start | bytes 786440 | tf_op jit(solution)/shard_map/cond/branch_2_fun/ppermute | solution.py:337
  50.0 13.1 %collective-permute-start.57 = (f32[2,8,32,128]{3,2,1,0:T(8,128)S(1)}, f32[2,8,32,128]{3,2,1,0:T(8,128)S(1)}, u32[]{:S(2)}, u32[]{:S(2)}) collective-permute-start(f32[2,8,32,128]{3,2,1,0:T(8,128)S(1)} %get-tuple-element.151), channel_id=1, source_target_pairs={{0,2},{1,3},{2,0},{3,1},{4,6},{5,7},{6,4},{7,5},{8,10},{9,11},{10,... | collective-permute-start | bytes 786440 | tf_op jit(solution)/shard_map/cond/branch_2_fun/ppermute | solution.py:337
  50.8 12.9 %collective-permute-start.58 = (f32[2,8,32,128]{3,2,1,0:T(8,128)S(1)}, f32[2,8,32,128]{3,2,1,0:T(8,128)S(1)}, u32[]{:S(2)}, u32[]{:S(2)}) collective-permute-start(f32[2,8,32,128]{3,2,1,0:T(8,128)S(1)} %collective-permute-done.52), channel_id=1, source_target_pairs={{0,2},{1,3},{2,0},{3,1},{4,6},{5,7},{6,4},{7,5},{8,10},{9,11},{10,... | collective-permute-start | bytes 786440 | tf_op jit(solution)/shard_map/cond/branch_2_fun/ppermute | solution.py:337
  63.8 14.1 %collective-permute-start.61 = (f32[2,8,32,128]{3,2,1,0:T(8,128)S(1)}, f32[2,8,32,128]{3,2,1,0:T(8,128)S(1)}, u32[]{:S(2)}, u32[]{:S(2)}) collective-permute-start(f32[2,8,32,128]{3,2,1,0:T(8,128)S(1)} %get-tuple-element.157), channel_id=1, source_target_pairs={{0,8},{1,9},{2,10},{3,11},{4,12},{5,13},{6,14},{7,15},{8,0},{9,1},... | collective-permute-start | bytes 786440 | tf_op jit(solution)/shard_map/cond/branch_2_fun/ppermute | solution.py:337
  64.8 13.1 %collective-permute-start.62 = (f32[2,8,32,128]{3,2,1,0:T(8,128)S(1)}, f32[2,8,32,128]{3,2,1,0:T(8,128)S(1)}, u32[]{:S(2)}, u32[]{:S(2)}) collective-permute-start(f32[2,8,32,128]{3,2,1,0:T(8,128)S(1)} %get-tuple-element.157), channel_id=1, source_target_pairs={{0,2},{1,3},{2,0},{3,1},{4,6},{5,7},{6,4},{7,5},{8,10},{9,11},{10,... | collective-permute-start | bytes 786440 | tf_op jit(solution)/shard_map/cond/branch_2_fun/ppermute | solution.py:337
  65.7 12.2 %collective-permute-start.64 = (f32[2,8,32,128]{3,2,1,0:T(8,128)S(1)}, f32[2,8,32,128]{3,2,1,0:T(8,128)S(1)}, u32[]{:S(2)}, u32[]{:S(2)}) collective-permute-start(f32[2,8,32,128]{3,2,1,0:T(8,128)S(1)} %select_select_fusion.25), channel_id=1, source_target_pairs={{0,4},{1,5},{2,6},{3,7},{4,0},{5,1},{6,2},{7,3},{8,12},{9,13},{10,... | collective-permute-start | bytes 786440 | tf_op jit(solution)/shard_map/cond/branch_2_fun/ppermute | solution.py:337
  66.4 11.5 %collective-permute-start.63 = (f32[2,8,32,128]{3,2,1,0:T(8,128)S(1)}, f32[2,8,32,128]{3,2,1,0:T(8,128)S(1)}, u32[]{:S(2)}, u32[]{:S(2)}) collective-permute-start(f32[2,8,32,128]{3,2,1,0:T(8,128)S(1)} %collective-permute-done.56), channel_id=1, source_target_pairs={{0,2},{1,3},{2,0},{3,1},{4,6},{5,7},{6,4},{7,5},{8,10},{9,11},{10,... | collective-permute-start | bytes 786440 | tf_op jit(solution)/shard_map/cond/branch_2_fun/ppermute | solution.py:337
  77.9 7.3 %collective-permute-start.67 = (f32[2,8,8,128]{3,2,1,0:T(8,128)S(1)}, f32[2,8,8,128]{3,2,1,0:T(8,128)S(1)}, u32[]{:S(2)}, u32[]{:S(2)}) collective-permute-start(f32[2,8,8,128]{3,2,1,0:T(8,128)S(1)} %edges.5), channel_id=1, source_target_pairs={{0,8},{1,9},{2,10},{3,11},{4,12},{5,13},{6,14},{7,15},{8,0},{9,1},... | collective-permute-start | bytes 196616 | tf_op jit(solution)/shard_map/cond/branch_2_fun/ppermute | solution.py:337
  79.3 5.9 %collective-permute-start.68 = (f32[2,8,8,128]{3,2,1,0:T(8,128)S(1)}, f32[2,8,8,128]{3,2,1,0:T(8,128)S(1)}, u32[]{:S(2)}, u32[]{:S(2)}) collective-permute-start(f32[2,8,8,128]{3,2,1,0:T(8,128)S(1)} %edges.5), channel_id=1, source_target_pairs={{0,2},{1,3},{2,0},{3,1},{4,6},{5,7},{6,4},{7,5},{8,10},{9,11},{10,... | collective-permute-start | bytes 196616 | tf_op jit(solution)/shard_map/cond/branch_2_fun/ppermute | solution.py:337
  80.1 6.6 %collective-permute-start.69 = (f32[2,8,8,128]{3,2,1,0:T(8,128)S(1)}, f32[2,8,8,128]{3,2,1,0:T(8,128)S(1)}, u32[]{:S(2)}, u32[]{:S(2)}) collective-permute-start(f32[2,8,8,128]{3,2,1,0:T(8,128)S(1)} %edges.5), channel_id=1, source_target_pairs={{0,10},{1,11},{2,8},{3,9},{4,14},{5,15},{6,12},{7,13},{8,2},{9,3},... | collective-permute-start | bytes 196616 | tf_op jit(solution)/shard_map/cond/branch_2_fun/ppermute | solution.py:337
  82.4 8.7 %collective-permute-start.66 = (f32[2,8,32,128]{3,2,1,0:T(8,128)S(1)}, f32[2,8,32,128]{3,2,1,0:T(8,128)S(1)}, u32[]{:S(2)}, u32[]{:S(2)}) collective-permute-start(f32[2,8,32,128]{3,2,1,0:T(8,128)S(1)} %select_select_fusion.23), channel_id=1, source_target_pairs={{0,4},{1,5},{2,6},{3,7},{4,0},{5,1},{6,2},{7,3},{8,12},{9,13},{10,... | collective-permute-start | bytes 786440 | tf_op jit(solution)/shard_map/cond/branch_2_fun/ppermute | solution.py:337
  83.2 8.0 %collective-permute-start.65 = (f32[2,8,32,128]{3,2,1,0:T(8,128)S(1)}, f32[2,8,32,128]{3,2,1,0:T(8,128)S(1)}, u32[]{:S(2)}, u32[]{:S(2)}) collective-permute-start(f32[2,8,32,128]{3,2,1,0:T(8,128)S(1)} %collective-permute-done.61), channel_id=1, source_target_pairs={{0,2},{1,3},{2,0},{3,1},{4,6},{5,7},{6,4},{7,5},{8,10},{9,11},{10,... | collective-permute-start | bytes 786440 | tf_op jit(solution)/shard_map/cond/branch_2_fun/ppermute | solution.py:337
  91.1 5.1 %collective-permute-start.71 = (f32[2,8,8,128]{3,2,1,0:T(8,128)S(1)}, f32[2,8,8,128]{3,2,1,0:T(8,128)S(1)}, u32[]{:S(2)}, u32[]{:S(2)}) collective-permute-start(f32[2,8,8,128]{3,2,1,0:T(8,128)S(1)} %select_select_fusion.29), channel_id=1, source_target_pairs={{0,4},{1,5},{2,6},{3,7},{4,0},{5,1},{6,2},{7,3},{8,12},{9,13},{10,... | collective-permute-start | bytes 196616 | tf_op jit(solution)/shard_map/cond/branch_2_fun/ppermute | solution.py:337
  92.0 8.1 %collective-permute-start.70 = (f32[2,8,32,128]{3,2,1,0:T(8,128)S(1)}, f32[2,8,32,128]{3,2,1,0:T(8,128)S(1)}, u32[]{:S(2)}, u32[]{:S(2)}) collective-permute-start(f32[2,8,32,128]{3,2,1,0:T(8,128)S(1)} %select_select_fusion.21), channel_id=1, source_target_pairs={{0,4},{1,5},{2,6},{3,7},{4,0},{5,1},{6,2},{7,3},{8,12},{9,13},{10,... | collective-permute-start | bytes 786440 | tf_op jit(solution)/shard_map/cond/branch_2_fun/ppermute | solution.py:337
  (5 other events, 48.8 us)

commit v5 on v4

--- a/solution.py
+++ b/solution.py
@@ -417,6 +417,7 @@
             ],
         ),
         compiler_params=PARAMS,
+        cost_estimate=pl.CostEstimate(flops=40_000_000, bytes_accessed=20_000_000, transcendentals=0),
         name="edges",
     )(plan, velocity, rates, gathered, gathered, own)
 
@@ -455,13 +456,15 @@
     o1 = (p1, n1, a1, f1)
     n3, a3, f2, h1 = swap(p3, top), swap(p3, low), swap(n2, low), swap(give(o1), high)
     edges = edge_call(plan, velocity, rates, strips, own, [top, *middle, 0])
-    n3, a3, f2, h1, edges = order(n3, a3, f2, h1, edges)
+    edges, h1, f2 = order(edges, h1, f2)
+    oe = (edges, swap(edges, top), swap(edges, low), swap_both(edges, top, low))
+    n3, a3, f2, h1, *oe = order(n3, a3, f2, h1, *oe)
     o2 = (p2, n2, a2, f2)
     f3, h2 = swap(n3, low), swap(give(o2), high)
-    oe = (edges, swap(edges, top), swap(edges, low), swap_both(edges, top, low))
-    f3, h2, *oe = order(f3, h2, *oe)
+    eh = swap(give(oe), high)
+    f3, h2, eh = order(f3, h2, eh)
     o3 = (p3, n3, a3, f3)
-    h3, eh = swap(give(o3), high), swap(give(oe), high)
+    h3 = swap(give(o3), high)
     parts = [result(*pair) for pair in ((o0, h0), (o1, h1), (o2, h2), (o3, h3), (oe, eh))]
     return pl.pallas_call(
         merge_kernel,

time: 102 us -> 105 us (1.029)
  waiting for transfers between devices: 44 us -> 55.7 us
  starting transfers between devices: 28.2 us -> 19.6 us
    ppermute x24, waiting for transfers between devices: 44 us -> 55.7 us  [swap_mask(): lax.ppermute(block, AXES, [(slot, slot ^ mask) for slot in range(lax.axis...]
    ppermute x24, starting transfers between devices: 28.2 us -> 19.6 us  [swap_mask(): lax.ppermute(block, AXES, [(slot, slot ^ mask) for slot in range(lax.axis...]
  transfers between devices with their start and end apart: 24 -> 24, of which waited for: 12 -> 12; matrix products, arithmetic and copies ran while one was open for 2% -> 1% of each run, Pallas kernels for 18% -> 18%
where the time goes in v5:
time: 105 us
  waiting for transfers between devices  55.7 us (53%)
  Pallas kernels  21.4 us (20%)
  starting transfers between devices  19.6 us (19%)
  loops' own time  4.76 us (5%)
  local copies, waits for them, and re-layouts  1.66 us (2%)
  other arithmetic  1.06 us (1%)
    ppermute x24, waiting for transfers between devices, swap_mask(): lax.ppermute(block, AXES, [(slot, slot ^ mask) for slot in range(lax.axis...  55.7 us
    ppermute x24, starting transfers between devices, swap_mask(): lax.ppermute(block, AXES, [(slot, slot ^ mask) for slot in range(lax.axis...  19.6 us
    pallas_call x2, Pallas kernels, interior_call(): pl.pallas_call(partial(interior_kernel, first, cuts), out_shape=[jax.Shap...  12.6 us
    pallas_call x1, Pallas kernels, edge_call(): pl.pallas_call(edge_kernel, out_shape=jax.ShapeDtypeStruct((species, dept...  5.87 us
    another operation x1, loops' own time, per_device(): lax.switch(branch[0], branches, field, kappa, rates, velocity, plan, own,...  4.76 us
    pallas_call x1, Pallas kernels, per_device(): pl.pallas_call(partial(prepare_kernel, top), out_shape=(jax.ShapeDtypeStr...  2.52 us
  transfers between devices with their start and end apart: 24, of which 12 were waited for; matrix products, arithmetic and copies ran while one was open for 1% of the time, Pallas kernels for 18%

profile of v5, /device:TPU:0, one launch (start us, length us, event | category | flops | bytes accessed | tf_op | source)
XLA Modules:
  0.0 104.8 jit_solution(15551097658109435317)
XLA Ops:
  0.0 2.5 %prepare.1 = (s32[1]{0:T(128)}, s32[8]{0:T(128)S(1)}, f32[3,8,16,128]{3,2,1,0:T(8,128)S(1)}, f32[26,8,128]{2,1,0:T(8,128)S(1)}) custom-call(s32[1]{0:T(128)} %bitcast.27.here_ref, s32[2,16]{1,0:T(2,128)} %bitcast.49, s32[3,16]{1,0:T(4,128)} %migrate_hbm.1, s32[3]{0:T(128)} %order_hbm.1, f32[1,2]{1,0:T(1,128)} %rates_hbm.1, f32[2,8,128,128]{3,2,1,0:T(8,128)} %bitcast.32, ...), custom_call_target="tpu_custom_call" | custom-call | tf_op jit(solution)/shard_map/prepare/pallas_call | solution.py:485
  3.1 100.7 %conditional.1 = (f32[1,2,8,128,128]{4,3,2,1,0:T(8,128)S(1)}) conditional(s32[]{:T(128)} %bitcast.31, (s32[8]{0:T(128)S(1)}, f32[2,3]{1,0:T(2,128)}, f32[1,2]{1,0:T(1,128)}, f32[2,8,128,128]{3,2,1,0:T(8,128)}, f32[8,128,128]{2,1,0:T(8,128)}, /*index=5*/f32[26,8,128]{2,1,0:T(8,128)S(1)}, f32[3,8,16,128]{3,2,1,0:T(8,128)S(1)}) %tuple.54, ...), branch_computations={%region_0.1_spmd, %region_1.2_spmd, %region_2.3_spmd} | conditional | flops 122748416 | bytes 89153336 | solution.py:508
  3.2 4.1 %collective-permute-start = (f32[1,26,8,128]{3,2,1,0:T(8,128)S(1)}, f32[1,26,8,128]{3,2,1,0:T(8,128)S(1)}, u32[]{:S(2)}, u32[]{:S(2)}) collective-permute-start(f32[1,26,8,128]{3,2,1,0:T(8,128)S(1)} %bitcast.43), channel_id=1, source_target_pairs={{0,8},{1,9},{2,10},{3,11},{4,12},{5,13},{6,14},{7,15},{8,0},{9,1},... | collective-permute-start | bytes 319496 | tf_op jit(solution)/shard_map/cond/branch_0_fun/ppermute | solution.py:337
  7.3 4.3 %interior.6 = f32[2,8,32,128]{3,2,1,0:T(8,128)S(1)} custom-call(f32[2,3]{1,0:T(2,128)} %get-tuple-element.53.velocity_ref, f32[1,2]{1,0:T(1,128)} %get-tuple-element.54.rates_ref, f32[2,8,128,128]{3,2,1,0:T(8,128)} %get-tuple-element.58.u_ref, f32[8,128,128]{2,1,0:T(8,128)} %get-tuple-element.56.k_ref), custom_call_target="tpu_custom_call" | custom-call | flops 40000000 | bytes 10000000 | tf_op jit(solution)/shard_map/cond/branch_0_fun/interior/pallas_call | solution.py:363
  11.6 1.0 collective-permute-done
  13.4 3.4 %collective-permute-start.1 = (f32[2,8,32,128]{3,2,1,0:T(8,128)S(1)}, f32[2,8,32,128]{3,2,1,0:T(8,128)S(1)}, u32[]{:S(2)}, u32[]{:S(2)}) collective-permute-start(f32[2,8,32,128]{3,2,1,0:T(8,128)S(1)} %interior.6), channel_id=1, source_target_pairs={{0,8},{1,9},{2,10},{3,11},{4,12},{5,13},{6,14},{7,15},{8,0},{9,1},... | collective-permute-start | bytes 786440 | tf_op jit(solution)/shard_map/cond/branch_0_fun/ppermute | solution.py:337
  16.8 8.3 %interior.7 = (f32[2,8,32,128]{3,2,1,0:T(8,128)S(1)}, f32[2,8,32,128]{3,2,1,0:T(8,128)S(1)}, f32[2,8,32,128]{3,2,1,0:T(8,128)S(1)}) custom-call(f32[2,3]{1,0:T(2,128)S(1)} %copy-done.7, f32[1,2]{1,0:T(1,128)S(1)} %copy-done.10, f32[2,8,128,128]{3,2,1,0:T(8,128)S(1)} %copy-done, f32[8,128,128]{2,1,0:T(8,128)S(1)} %copy-done.3), custom_call_target="tpu_custom_call" | custom-call | flops 40000000 | bytes 10000000 | tf_op jit(solution)/shard_map/cond/branch_0_fun/interior/pallas_call | solution.py:363
  25.1 3.5 %collective-permute-done.1 = f32[2,8,32,128]{3,2,1,0:T(8,128)S(1)} collective-permute-done((f32[2,8,32,128]{3,2,1,0:T(8,128)S(1)}, f32[2,8,32,128]{3,2,1,0:T(8,128)S(1)}, u32[]{:S(2)}, u32[]{:S(2)}) %collective-permute-start.1) | collective-permute-done | bytes 262176 | tf_op jit(solution)/shard_map/cond/branch_0_fun/ppermute | solution.py:337
  28.6 1.5 %collective-permute-start.7 = (f32[4,26,8,128]{3,2,1,0:T(8,128)S(1)}, f32[4,26,8,128]{3,2,1,0:T(8,128)S(1)}, u32[]{:S(2)}, u32[]{:S(2)}) collective-permute-start(f32[4,26,8,128]{3,2,1,0:T(8,128)S(1)} %pad_maximum_fusion.2), channel_id=1, source_target_pairs={{0,2},{1,3},{2,0},{3,1},{4,6},{5,7},{6,4},{7,5},{8,10},{9,11},{10,... | collective-permute-start | bytes 1277960 | tf_op jit(solution)/shard_map/cond/branch_0_fun/ppermute | solution.py:337
  30.6 8.9 %collective-permute-done.7 = f32[4,26,8,128]{3,2,1,0:T(8,128)S(1)} collective-permute-done((f32[4,26,8,128]{3,2,1,0:T(8,128)S(1)}, f32[4,26,8,128]{3,2,1,0:T(8,128)S(1)}, u32[]{:S(2)}, u32[]{:S(2)}) %collective-permute-start.7) | collective-permute-done | bytes 426016 | tf_op jit(solution)/shard_map/cond/branch_0_fun/ppermute | solution.py:337
  39.6 4.0 %collective-permute-done.4 = f32[2,8,32,128]{3,2,1,0:T(8,128)S(1)} collective-permute-done((f32[2,8,32,128]{3,2,1,0:T(8,128)S(1)}, f32[2,8,32,128]{3,2,1,0:T(8,128)S(1)}, u32[]{:S(2)}, u32[]{:S(2)}) %collective-permute-start.4) | collective-permute-done | bytes 262176 | tf_op jit(solution)/shard_map/cond/branch_0_fun/ppermute | solution.py:337
  47.6 7.5 %collective-permute-done.11 = f32[2,8,32,128]{3,2,1,0:T(8,128)S(1)} collective-permute-done((f32[2,8,32,128]{3,2,1,0:T(8,128)S(1)}, f32[2,8,32,128]{3,2,1,0:T(8,128)S(1)}, u32[]{:S(2)}, u32[]{:S(2)}) %collective-permute-start.11) | collective-permute-done | bytes 262176 | tf_op jit(solution)/shard_map/cond/branch_0_fun/ppermute | solution.py:337
  55.2 5.8 %collective-permute-done.8 = f32[2,8,32,128]{3,2,1,0:T(8,128)S(1)} collective-permute-done((f32[2,8,32,128]{3,2,1,0:T(8,128)S(1)}, f32[2,8,32,128]{3,2,1,0:T(8,128)S(1)}, u32[]{:S(2)}, u32[]{:S(2)}) %collective-permute-start.8) | collective-permute-done | bytes 262176 | tf_op jit(solution)/shard_map/cond/branch_0_fun/ppermute | solution.py:337
  61.0 1.6 %collective-permute-start.15 = (f32[2,8,32,128]{3,2,1,0:T(8,128)S(1)}, f32[2,8,32,128]{3,2,1,0:T(8,128)S(1)}, u32[]{:S(2)}, u32[]{:S(2)}) collective-permute-start(f32[2,8,32,128]{3,2,1,0:T(8,128)S(1)} %select_select_fusion.5), channel_id=1, source_target_pairs={{0,2},{1,3},{2,0},{3,1},{4,6},{5,7},{6,4},{7,5},{8,10},{9,11},{10,... | collective-permute-start | bytes 786440 | tf_op jit(solution)/shard_map/cond/branch_0_fun/ppermute | solution.py:337
  65.5 5.9 %edges.3 = f32[2,8,8,128]{3,2,1,0:T(8,128)S(1)} custom-call(s32[8]{0:T(128)S(1)} %get-tuple-element.52.plan_ref, f32[2,3]{1,0:T(2,128)S(1)} %copy-done.7, f32[1,2]{1,0:T(1,128)S(1)} %copy-done.10, f32[16,26,8,128]{3,2,1,0:T(8,128)S(1)} %pad_maximum_fusion.left_ref.right_ref, f32[16,26,8,128]{3,2,1,0:T(8,128)S(1)} %pad_maximum_fusion.left_ref.right_ref, ...), custom_call_target="tpu_custom_call" | custom-call | flops 40000000 | bytes 20000000 | tf_op jit(solution)/shard_map/cond/branch_0_fun/edges/pallas_call | solution.py:395
  71.4 2.6 %collective-permute-start.17 = (f32[2,8,8,128]{3,2,1,0:T(8,128)S(1)}, f32[2,8,8,128]{3,2,1,0:T(8,128)S(1)}, u32[]{:S(2)}, u32[]{:S(2)}) collective-permute-start(f32[2,8,8,128]{3,2,1,0:T(8,128)S(1)} %edges.3), channel_id=1, source_target_pairs={{0,8},{1,9},{2,10},{3,11},{4,12},{5,13},{6,14},{7,15},{8,0},{9,1},... | collective-permute-start | bytes 196616 | tf_op jit(solution)/shard_map/cond/branch_0_fun/ppermute | solution.py:337
  74.6 8.2 %collective-permute-done.13 = f32[2,8,32,128]{3,2,1,0:T(8,128)S(1)} collective-permute-done((f32[2,8,32,128]{3,2,1,0:T(8,128)S(1)}, f32[2,8,32,128]{3,2,1,0:T(8,128)S(1)}, u32[]{:S(2)}, u32[]{:S(2)}) %collective-permute-start.13) | collective-permute-done | bytes 262176 | tf_op jit(solution)/shard_map/cond/branch_0_fun/ppermute | solution.py:337
  82.8 1.4 %collective-permute-done.17 = f32[2,8,8,128]{3,2,1,0:T(8,128)S(1)} collective-permute-done((f32[2,8,8,128]{3,2,1,0:T(8,128)S(1)}, f32[2,8,8,128]{3,2,1,0:T(8,128)S(1)}, u32[]{:S(2)}, u32[]{:S(2)}) %collective-permute-start.17) | collective-permute-done | bytes 65568 | tf_op jit(solution)/shard_map/cond/branch_0_fun/ppermute | solution.py:337
  84.2 1.3 %collective-permute-done.19 = f32[2,8,8,128]{3,2,1,0:T(8,128)S(1)} collective-permute-done((f32[2,8,8,128]{3,2,1,0:T(8,128)S(1)}, f32[2,8,8,128]{3,2,1,0:T(8,128)S(1)}, u32[]{:S(2)}, u32[]{:S(2)}) %collective-permute-start.19) | collective-permute-done | bytes 65568 | tf_op jit(solution)/shard_map/cond/branch_0_fun/ppermute | solution.py:337
  86.2 1.6 %collective-permute-start.21 = (f32[2,8,32,128]{3,2,1,0:T(8,128)S(1)}, f32[2,8,32,128]{3,2,1,0:T(8,128)S(1)}, u32[]{:S(2)}, u32[]{:S(2)}) collective-permute-start(f32[2,8,32,128]{3,2,1,0:T(8,128)S(1)} %select_select_fusion.3), channel_id=1, source_target_pairs={{0,2},{1,3},{2,0},{3,1},{4,6},{5,7},{6,4},{7,5},{8,10},{9,11},{10,... | collective-permute-start | bytes 786440 | tf_op jit(solution)/shard_map/cond/branch_0_fun/ppermute | solution.py:337
  87.9 2.6 %collective-permute-done.22 = f32[2,8,8,128]{3,2,1,0:T(8,128)S(1)} collective-permute-done((f32[2,8,8,128]{3,2,1,0:T(8,128)S(1)}, f32[2,8,8,128]{3,2,1,0:T(8,128)S(1)}, u32[]{:S(2)}, u32[]{:S(2)}) %collective-permute-start.22) | collective-permute-done | bytes 65568 | tf_op jit(solution)/shard_map/cond/branch_0_fun/ppermute | solution.py:337
  90.6 4.8 %collective-permute-done.21 = f32[2,8,32,128]{3,2,1,0:T(8,128)S(1)} collective-permute-done((f32[2,8,32,128]{3,2,1,0:T(8,128)S(1)}, f32[2,8,32,128]{3,2,1,0:T(8,128)S(1)}, u32[]{:S(2)}, u32[]{:S(2)}) %collective-permute-start.21) | collective-permute-done | bytes 262176 | tf_op jit(solution)/shard_map/cond/branch_0_fun/ppermute | solution.py:337
  96.3 6.7 %collective-permute-done.23 = f32[2,8,32,128]{3,2,1,0:T(8,128)S(1)} collective-permute-done((f32[2,8,32,128]{3,2,1,0:T(8,128)S(1)}, f32[2,8,32,128]{3,2,1,0:T(8,128)S(1)}, u32[]{:S(2)}, u32[]{:S(2)}) %collective-permute-start.23) | collective-permute-done | bytes 262176 | tf_op jit(solution)/shard_map/cond/branch_0_fun/ppermute | solution.py:337
  103.8 1.0 copy-done.6
  (55 shorter events, 7.1 us)
Async XLA Ops:
  3.2 9.4 %collective-permute-start = (f32[1,26,8,128]{3,2,1,0:T(8,128)S(1)}, f32[1,26,8,128]{3,2,1,0:T(8,128)S(1)}, u32[]{:S(2)}, u32[]{:S(2)}) collective-permute-start(f32[1,26,8,128]{3,2,1,0:T(8,128)S(1)} %bitcast.43), channel_id=1, source_target_pairs={{0,8},{1,9},{2,10},{3,11},{4,12},{5,13},{6,14},{7,15},{8,0},{9,1},... | collective-permute-start | bytes 319496 | tf_op jit(solution)/shard_map/cond/branch_0_fun/ppermute | solution.py:337
  12.6 12.5 %collective-permute-start.3 = (f32[2,26,8,128]{3,2,1,0:T(8,128)S(1)}, f32[2,26,8,128]{3,2,1,0:T(8,128)S(1)}, u32[]{:S(2)}, u32[]{:S(2)}) collective-permute-start(f32[2,26,8,128]{3,2,1,0:T(8,128)S(1)} %pad_maximum_fusion.3), channel_id=1, source_target_pairs={{0,4},{1,5},{2,6},{3,7},{4,0},{5,1},{6,2},{7,3},{8,12},{9,13},{10,... | collective-permute-start | bytes 638984 | tf_op jit(solution)/shard_map/cond/branch_0_fun/ppermute | solution.py:337
  13.4 15.2 %collective-permute-start.1 = (f32[2,8,32,128]{3,2,1,0:T(8,128)S(1)}, f32[2,8,32,128]{3,2,1,0:T(8,128)S(1)}, u32[]{:S(2)}, u32[]{:S(2)}) collective-permute-start(f32[2,8,32,128]{3,2,1,0:T(8,128)S(1)} %interior.6), channel_id=1, source_target_pairs={{0,8},{1,9},{2,10},{3,11},{4,12},{5,13},{6,14},{7,15},{8,0},{9,1},... | collective-permute-start | bytes 786440 | tf_op jit(solution)/shard_map/cond/branch_0_fun/ppermute | solution.py:337
  16.7 11.9 %collective-permute-start.2 = (f32[2,8,32,128]{3,2,1,0:T(8,128)S(1)}, f32[2,8,32,128]{3,2,1,0:T(8,128)S(1)}, u32[]{:S(2)}, u32[]{:S(2)}) collective-permute-start(f32[2,8,32,128]{3,2,1,0:T(8,128)S(1)} %interior.6), channel_id=1, source_target_pairs={{0,1},{1,0},{2,3},{3,2},{4,5},{5,4},{6,7},{7,6},{8,9},{9,8},{10,11... | collective-permute-start | bytes 786440 | tf_op jit(solution)/shard_map/cond/branch_0_fun/ppermute | solution.py:337
  28.6 10.9 %collective-permute-start.7 = (f32[4,26,8,128]{3,2,1,0:T(8,128)S(1)}, f32[4,26,8,128]{3,2,1,0:T(8,128)S(1)}, u32[]{:S(2)}, u32[]{:S(2)}) collective-permute-start(f32[4,26,8,128]{3,2,1,0:T(8,128)S(1)} %pad_maximum_fusion.2), channel_id=1, source_target_pairs={{0,2},{1,3},{2,0},{3,1},{4,6},{5,7},{6,4},{7,5},{8,10},{9,11},{10,... | collective-permute-start | bytes 1277960 | tf_op jit(solution)/shard_map/cond/branch_0_fun/ppermute | solution.py:337
  30.1 13.4 %collective-permute-start.4 = (f32[2,8,32,128]{3,2,1,0:T(8,128)S(1)}, f32[2,8,32,128]{3,2,1,0:T(8,128)S(1)}, u32[]{:S(2)}, u32[]{:S(2)}) collective-permute-start(f32[2,8,32,128]{3,2,1,0:T(8,128)S(1)} %get-tuple-element.66), channel_id=1, source_target_pairs={{0,8},{1,9},{2,10},{3,11},{4,12},{5,13},{6,14},{7,15},{8,0},{9,1},... | collective-permute-start | bytes 786440 | tf_op jit(solution)/shard_map/cond/branch_0_fun/ppermute | solution.py:337
  30.1 13.4 %collective-permute-start.5 = (f32[2,8,32,128]{3,2,1,0:T(8,128)S(1)}, f32[2,8,32,128]{3,2,1,0:T(8,128)S(1)}, u32[]{:S(2)}, u32[]{:S(2)}) collective-permute-start(f32[2,8,32,128]{3,2,1,0:T(8,128)S(1)} %get-tuple-element.66), channel_id=1, source_target_pairs={{0,1},{1,0},{2,3},{3,2},{4,5},{5,4},{6,7},{7,6},{8,9},{9,8},{10,11... | collective-permute-start | bytes 786440 | tf_op jit(solution)/shard_map/cond/branch_0_fun/ppermute | solution.py:337
  30.1 13.4 %collective-permute-start.6 = (f32[2,8,32,128]{3,2,1,0:T(8,128)S(1)}, f32[2,8,32,128]{3,2,1,0:T(8,128)S(1)}, u32[]{:S(2)}, u32[]{:S(2)}) collective-permute-start(f32[2,8,32,128]{3,2,1,0:T(8,128)S(1)} %collective-permute-done.1), channel_id=1, source_target_pairs={{0,1},{1,0},{2,3},{3,2},{4,5},{5,4},{6,7},{7,6},{8,9},{9,8},{10,11... | collective-permute-start | bytes 786440 | tf_op jit(solution)/shard_map/cond/branch_0_fun/ppermute | solution.py:337
  43.5 4.0 %collective-permute-start.12 = (f32[8,26,8,128]{3,2,1,0:T(8,128)S(1)}, f32[8,26,8,128]{3,2,1,0:T(8,128)S(1)}, u32[]{:S(2)}, u32[]{:S(2)}) collective-permute-start(f32[8,26,8,128]{3,2,1,0:T(8,128)S(1)} %pad_maximum_fusion.1), channel_id=1, source_target_pairs={{0,1},{1,0},{2,3},{3,2},{4,5},{5,4},{6,7},{7,6},{8,9},{9,8},{10,11... | collective-permute-start | bytes 2555912 | tf_op jit(solution)/shard_map/cond/branch_0_fun/ppermute | solution.py:337
  46.4 8.8 %collective-permute-start.11 = (f32[2,8,32,128]{3,2,1,0:T(8,128)S(1)}, f32[2,8,32,128]{3,2,1,0:T(8,128)S(1)}, u32[]{:S(2)}, u32[]{:S(2)}) collective-permute-start(f32[2,8,32,128]{3,2,1,0:T(8,128)S(1)} %select_select_fusion.7), channel_id=1, source_target_pairs={{0,2},{1,3},{2,0},{3,1},{4,6},{5,7},{6,4},{7,5},{8,10},{9,11},{10,... | collective-permute-start | bytes 786440 | tf_op jit(solution)/shard_map/cond/branch_0_fun/ppermute | solution.py:337
  47.0 8.2 %collective-permute-start.10 = (f32[2,8,32,128]{3,2,1,0:T(8,128)S(1)}, f32[2,8,32,128]{3,2,1,0:T(8,128)S(1)}, u32[]{:S(2)}, u32[]{:S(2)}) collective-permute-start(f32[2,8,32,128]{3,2,1,0:T(8,128)S(1)} %collective-permute-done.4), channel_id=1, source_target_pairs={{0,1},{1,0},{2,3},{3,2},{4,5},{5,4},{6,7},{7,6},{8,9},{9,8},{10,11... | collective-permute-start | bytes 786440 | tf_op jit(solution)/shard_map/cond/branch_0_fun/ppermute | solution.py:337
  47.2 13.8 %collective-permute-start.8 = (f32[2,8,32,128]{3,2,1,0:T(8,128)S(1)}, f32[2,8,32,128]{3,2,1,0:T(8,128)S(1)}, u32[]{:S(2)}, u32[]{:S(2)}) collective-permute-start(f32[2,8,32,128]{3,2,1,0:T(8,128)S(1)} %get-tuple-element.69), channel_id=1, source_target_pairs={{0,8},{1,9},{2,10},{3,11},{4,12},{5,13},{6,14},{7,15},{8,0},{9,1},... | collective-permute-start | bytes 786440 | tf_op jit(solution)/shard_map/cond/branch_0_fun/ppermute | solution.py:337
  47.2 13.8 %collective-permute-start.9 = (f32[2,8,32,128]{3,2,1,0:T(8,128)S(1)}, f32[2,8,32,128]{3,2,1,0:T(8,128)S(1)}, u32[]{:S(2)}, u32[]{:S(2)}) collective-permute-start(f32[2,8,32,128]{3,2,1,0:T(8,128)S(1)} %get-tuple-element.69), channel_id=1, source_target_pairs={{0,1},{1,0},{2,3},{3,2},{4,5},{5,4},{6,7},{7,6},{8,9},{9,8},{10,11... | collective-permute-start | bytes 786440 | tf_op jit(solution)/shard_map/cond/branch_0_fun/ppermute | solution.py:337
  61.0 10.3 %collective-permute-start.15 = (f32[2,8,32,128]{3,2,1,0:T(8,128)S(1)}, f32[2,8,32,128]{3,2,1,0:T(8,128)S(1)}, u32[]{:S(2)}, u32[]{:S(2)}) collective-permute-start(f32[2,8,32,128]{3,2,1,0:T(8,128)S(1)} %select_select_fusion.5), channel_id=1, source_target_pairs={{0,2},{1,3},{2,0},{3,1},{4,6},{5,7},{6,4},{7,5},{8,10},{9,11},{10,... | collective-permute-start | bytes 786440 | tf_op jit(solution)/shard_map/cond/branch_0_fun/ppermute | solution.py:337
  62.6 8.8 %collective-permute-start.16 = (f32[2,8,32,128]{3,2,1,0:T(8,128)S(1)}, f32[2,8,32,128]{3,2,1,0:T(8,128)S(1)}, u32[]{:S(2)}, u32[]{:S(2)}) collective-permute-start(f32[2,8,32,128]{3,2,1,0:T(8,128)S(1)} %collective-permute-done.8), channel_id=1, source_target_pairs={{0,1},{1,0},{2,3},{3,2},{4,5},{5,4},{6,7},{7,6},{8,9},{9,8},{10,11... | collective-permute-start | bytes 786440 | tf_op jit(solution)/shard_map/cond/branch_0_fun/ppermute | solution.py:337
  64.9 17.9 %collective-permute-start.13 = (f32[2,8,32,128]{3,2,1,0:T(8,128)S(1)}, f32[2,8,32,128]{3,2,1,0:T(8,128)S(1)}, u32[]{:S(2)}, u32[]{:S(2)}) collective-permute-start(f32[2,8,32,128]{3,2,1,0:T(8,128)S(1)} %get-tuple-element.75), channel_id=1, source_target_pairs={{0,8},{1,9},{2,10},{3,11},{4,12},{5,13},{6,14},{7,15},{8,0},{9,1},... | collective-permute-start | bytes 786440 | tf_op jit(solution)/shard_map/cond/branch_0_fun/ppermute | solution.py:337
  64.9 17.9 %collective-permute-start.14 = (f32[2,8,32,128]{3,2,1,0:T(8,128)S(1)}, f32[2,8,32,128]{3,2,1,0:T(8,128)S(1)}, u32[]{:S(2)}, u32[]{:S(2)}) collective-permute-start(f32[2,8,32,128]{3,2,1,0:T(8,128)S(1)} %get-tuple-element.75), channel_id=1, source_target_pairs={{0,1},{1,0},{2,3},{3,2},{4,5},{5,4},{6,7},{7,6},{8,9},{9,8},{10,11... | collective-permute-start | bytes 786440 | tf_op jit(solution)/shard_map/cond/branch_0_fun/ppermute | solution.py:337
  71.4 12.8 %collective-permute-start.17 = (f32[2,8,8,128]{3,2,1,0:T(8,128)S(1)}, f32[2,8,8,128]{3,2,1,0:T(8,128)S(1)}, u32[]{:S(2)}, u32[]{:S(2)}) collective-permute-start(f32[2,8,8,128]{3,2,1,0:T(8,128)S(1)} %edges.3), channel_id=1, source_target_pairs={{0,8},{1,9},{2,10},{3,11},{4,12},{5,13},{6,14},{7,15},{8,0},{9,1},... | collective-permute-start | bytes 196616 | tf_op jit(solution)/shard_map/cond/branch_0_fun/ppermute | solution.py:337
  74.0 10.2 %collective-permute-start.18 = (f32[2,8,8,128]{3,2,1,0:T(8,128)S(1)}, f32[2,8,8,128]{3,2,1,0:T(8,128)S(1)}, u32[]{:S(2)}, u32[]{:S(2)}) collective-permute-start(f32[2,8,8,128]{3,2,1,0:T(8,128)S(1)} %edges.3), channel_id=1, source_target_pairs={{0,1},{1,0},{2,3},{3,2},{4,5},{5,4},{6,7},{7,6},{8,9},{9,8},{10,11... | collective-permute-start | bytes 196616 | tf_op jit(solution)/shard_map/cond/branch_0_fun/ppermute | solution.py:337
  74.1 11.5 %collective-permute-start.19 = (f32[2,8,8,128]{3,2,1,0:T(8,128)S(1)}, f32[2,8,8,128]{3,2,1,0:T(8,128)S(1)}, u32[]{:S(2)}, u32[]{:S(2)}) collective-permute-start(f32[2,8,8,128]{3,2,1,0:T(8,128)S(1)} %edges.3), channel_id=1, source_target_pairs={{0,9},{1,8},{2,11},{3,10},{4,13},{5,12},{6,15},{7,14},{8,1},{9,0},... | collective-permute-start | bytes 196616 | tf_op jit(solution)/shard_map/cond/branch_0_fun/ppermute | solution.py:337
  85.6 5.0 %collective-permute-start.22 = (f32[2,8,8,128]{3,2,1,0:T(8,128)S(1)}, f32[2,8,8,128]{3,2,1,0:T(8,128)S(1)}, u32[]{:S(2)}, u32[]{:S(2)}) collective-permute-start(f32[2,8,8,128]{3,2,1,0:T(8,128)S(1)} %select_select_fusion.9), channel_id=1, source_target_pairs={{0,2},{1,3},{2,0},{3,1},{4,6},{5,7},{6,4},{7,5},{8,10},{9,11},{10,... | collective-permute-start | bytes 196616 | tf_op jit(solution)/shard_map/cond/branch_0_fun/ppermute | solution.py:337
  86.2 9.1 %collective-permute-start.21 = (f32[2,8,32,128]{3,2,1,0:T(8,128)S(1)}, f32[2,8,32,128]{3,2,1,0:T(8,128)S(1)}, u32[]{:S(2)}, u32[]{:S(2)}) collective-permute-start(f32[2,8,32,128]{3,2,1,0:T(8,128)S(1)} %select_select_fusion.3), channel_id=1, source_target_pairs={{0,2},{1,3},{2,0},{3,1},{4,6},{5,7},{6,4},{7,5},{8,10},{9,11},{10,... | collective-permute-start | bytes 786440 | tf_op jit(solution)/shard_map/cond/branch_0_fun/ppermute | solution.py:337
  87.8 7.6 %collective-permute-start.20 = (f32[2,8,32,128]{3,2,1,0:T(8,128)S(1)}, f32[2,8,32,128]{3,2,1,0:T(8,128)S(1)}, u32[]{:S(2)}, u32[]{:S(2)}) collective-permute-start(f32[2,8,32,128]{3,2,1,0:T(8,128)S(1)} %collective-permute-done.13), channel_id=1, source_target_pairs={{0,1},{1,0},{2,3},{3,2},{4,5},{5,4},{6,7},{7,6},{8,9},{9,8},{10,11... | collective-permute-start | bytes 786440 | tf_op jit(solution)/shard_map/cond/branch_0_fun/ppermute | solution.py:337
  95.5 7.6 %collective-permute-start.23 = (f32[2,8,32,128]{3,2,1,0:T(8,128)S(1)}, f32[2,8,32,128]{3,2,1,0:T(8,128)S(1)}, u32[]{:S(2)}, u32[]{:S(2)}) collective-permute-start(f32[2,8,32,128]{3,2,1,0:T(8,128)S(1)} %select_select_fusion.1), channel_id=1, source_target_pairs={{0,2},{1,3},{2,0},{3,1},{4,6},{5,7},{6,4},{7,5},{8,10},{9,11},{10,... | collective-permute-start | bytes 786440 | tf_op jit(solution)/shard_map/cond/branch_0_fun/ppermute | solution.py:337
  (5 other events, 55.3 us)
